TPU v7x, 32 devices: a whole 2x2x4 slice. The times are simulated.
32 devices in a mesh: dom: 8 (over z, x), rep: 4 (over y, core).
Axes of the slice: x: 2, y: 2, z: 4, core: 2. Of those that a mesh axis runs over, the one named last changes fastest.
Arguments:
- features: bfloat16 [32768, 100], P('dom'), may hold values from -6 to 6
- labels: int32 [32768], P('dom'), may hold values from 0 to 46
- train_mask: int32 [32768], P('dom'), may hold values from 0 to 1
- edge_src: int32 [32768, 16], P('dom'), may hold values from 0 to 4351
- edge_norm: float32 [32768, 16], P('dom'), may hold values from 0.15 to 0.35
- send_rows: int32 [8, 8, 32], P('dom'), may hold values from 0 to 4095
- changed: int32 [3, 8], P(None, 'dom'), may hold values 0 or 1
- cache_hidden: bfloat16 [2, 2048, 256], P(None, 'dom', 'rep'), may hold values from -6 to 6
- cache_out: bfloat16 [2048, 47], P('dom'), may hold values from -5 to 5
- first_weight: float32 [100, 256], P(None, 'rep'), may hold values from -0.625 to 0.625
- second_weight: float32 [256, 256], P(None, 'rep'), may hold values from -0.375 to 0.375
- last_weight: float32 [256, 47], replicated, may hold values from -0.375 to 0.375
- hidden_bias: float32 [2, 256], P(None, 'rep'), may hold values from -2 to 2
- out_bias: float32 [47], replicated, may hold values from -2 to 2
- moment_first: float32 [100, 256], P(None, 'rep'), may hold values from -0.0078125 to 0.0078125
- moment_second: float32 [256, 256], P(None, 'rep'), may hold values from -0.0078125 to 0.0078125
- moment_last: float32 [256, 47], replicated, may hold values from -0.0078125 to 0.0078125
- moment_hidden: float32 [2, 256], P(None, 'rep'), may hold values from -0.015625 to 0.015625
- moment_out: float32 [47], replicated, may hold values from -0.015625 to 0.015625
- square_first: float32 [100, 256], P(None, 'rep'), may hold values from 1.5258789e-07 to 1.2207031e-06
- square_second: float32 [256, 256], P(None, 'rep'), may hold values from 1.5258789e-07 to 1.2207031e-06
- square_last: float32 [256, 47], replicated, may hold values from 1.5258789e-07 to 1.2207031e-06
- square_hidden: float32 [2, 256], P(None, 'rep'), may hold values from 1e-05 to 0.1, as said below
- square_out: float32 [47], replicated, may hold values from 6.1035155e-07 to 4.8828124e-06
Outputs:
- loss_sum: float32 [], replicated
- train_count: float32 [], replicated
- next_first: float32 [100, 256], P(None, 'rep')
- next_moment_first: float32 [100, 256], P(None, 'rep')
- next_square_first: float32 [100, 256], P(None, 'rep')
- next_second: float32 [256, 256], P(None, 'rep')
- next_moment_second: float32 [256, 256], P(None, 'rep')
- next_square_second: float32 [256, 256], P(None, 'rep')
- next_last: float32 [256, 47], replicated
- next_moment_last: float32 [256, 47], replicated
- next_square_last: float32 [256, 47], replicated
- next_hidden: float32 [2, 256], P(None, 'rep')
- next_moment_hidden: float32 [2, 256], P(None, 'rep')
- next_square_hidden: float32 [2, 256], P(None, 'rep')
- next_out: float32 [47], replicated
- next_moment_out: float32 [47], replicated
- next_square_out: float32 [47], replicated
Inputs may be any that keep to these rules, and one draw needn't show every extreme that they name: `square_hidden`: positive.
All inputs are finite; a program needn't handle non-finite values. No bound on the sum of `changed` on one device may be relied on, other than what follows from the above.
Results may differ from a plain program's by a relative error of at most 0.00145.
The roundings to bfloat16 on the way count: a program that leaves them out, or rounds other values in their place, can miss the bound.
Values may be sent and summed in bfloat16 or wider, within the bound.
No kernel may reach another device: no remote copies, remote signals or barrier semaphores. Data moves between devices by JAX's collectives and lax.ppermute only.
A program may use at most 128 MiB of HBM per device.

v0:
```python
import jax
import jax.numpy as jnp
from jax import lax
from jax.sharding import PartitionSpec as P

STEP = 5


beta_one = 0.5
beta_two = 0.5
rate_step = 0.03
decay_rate = 0.01
epsilon = 1e-08


def aggregate(values, stored, fresh, send_list, edge_src, edge_norm):
    breadth = values.shape[1]
    outgoing = values[send_list.reshape(-1)].reshape(send_list.shape + (breadth,))
    arrived = lax.all_to_all(outgoing, "dom", split_axis=0, concat_axis=0, tiled=True)
    border = jnp.where((fresh == 1)[:, None, None], arrived, stored.reshape(outgoing.shape))
    lookup = jnp.concatenate([values, border.reshape(-1, breadth)], axis=0)
    picked = lookup[edge_src].astype(jnp.float32)
    return jnp.sum(picked * edge_norm[:, :, None], axis=1)


def spread_back(upstream, fresh, send_list, edge_src, edge_norm):
    breadth = upstream.shape[1]
    own_count = upstream.shape[0]
    table_rows = own_count + send_list.size
    terms = (edge_norm[:, :, None] * upstream[:, None, :]).reshape(-1, breadth)
    totals = jnp.zeros((table_rows, breadth), jnp.float32).at[edge_src.reshape(-1)].add(terms)
    keep = (fresh == 1).astype(jnp.float32)[:, None, None]
    border = totals[own_count:].reshape(send_list.shape + (breadth,)) * keep
    returned = lax.all_to_all(border, "dom", split_axis=0, concat_axis=0, tiled=True)
    return totals[:own_count].at[send_list.reshape(-1)].add(returned.reshape(-1, breadth))


def widen(hidden_part):
    return lax.all_gather(hidden_part, "rep", axis=1, tiled=True)


def gelu_slope(before, upstream):
    return jax.vjp(jax.nn.gelu, before)[1](upstream)[0]


def contract_rows(left, right):
    return lax.dot_general(
        left, right, (((0,), (0,)), ((), ())), preferred_element_type=jnp.float32
    )


def contract_cols(left, right):
    return lax.dot_general(
        left, right, (((1,), (1,)), ((), ())), preferred_element_type=jnp.float32
    )


def adamw(weight, moment, square, gradient):
    moment = beta_one * moment + (1.0 - beta_one) * gradient
    square = beta_two * square + (1.0 - beta_two) * gradient * gradient
    moment_hat = moment / (1.0 - beta_one**STEP)
    square_hat = square / (1.0 - beta_two**STEP)
    weight = weight - rate_step * (
        moment_hat / (jnp.sqrt(square_hat) + epsilon) + decay_rate * weight
    )
    return (weight, moment, square)


def body(
    features,
    labels,
    train_mask,
    edge_src,
    edge_norm,
    send_rows,
    changed,
    cache_hidden,
    cache_out,
    first_weight,
    second_weight,
    last_weight,
    hidden_bias,
    out_bias,
    moment_first,
    moment_second,
    moment_last,
    moment_hidden,
    moment_out,
    square_first,
    square_second,
    square_last,
    square_hidden,
    square_out,
):
    flags = lax.all_gather(changed, "dom", axis=1, tiled=True)
    send_list = send_rows[0]
    classes = last_weight.shape[1]

    def spread(values, stored, fresh):
        return aggregate(values, stored, fresh, send_list, edge_src, edge_norm)

    def spread_grad(upstream, fresh):
        return spread_back(upstream, fresh, send_list, edge_src, edge_norm).astype(jnp.bfloat16)

    first_low = first_weight.astype(jnp.bfloat16)
    second_low = second_weight.astype(jnp.bfloat16)
    last_low = last_weight.astype(jnp.bfloat16)
    z_one = jnp.dot(features, first_low, preferred_element_type=jnp.float32).astype(jnp.bfloat16)
    pre_one = spread(z_one, cache_hidden[0], flags[0]) + hidden_bias[0]
    h_one = widen(jax.nn.gelu(pre_one).astype(jnp.bfloat16))
    z_two = jnp.dot(h_one, second_low, preferred_element_type=jnp.float32).astype(jnp.bfloat16)
    pre_two = spread(z_two, cache_hidden[1], flags[1]) + hidden_bias[1]
    h_two = widen(jax.nn.gelu(pre_two).astype(jnp.bfloat16))
    z_three = jnp.dot(h_two, last_low, preferred_element_type=jnp.float32).astype(jnp.bfloat16)
    logits = spread(z_three, cache_out, flags[2]) + out_bias
    logp = jax.nn.log_softmax(logits, axis=-1)
    target = 0.9 * jax.nn.one_hot(labels, classes, dtype=jnp.float32) + 0.1 / classes
    masked = train_mask.astype(jnp.float32)
    row_loss = -jnp.sum(target * logp, axis=-1)
    loss_sum, train_count = lax.psum((jnp.sum(row_loss * masked), jnp.sum(masked)), "dom")
    d_logits = (jnp.exp(logp) - target) * (masked / train_count)[:, None]
    grad_out = jnp.sum(d_logits, axis=0)
    d_three = spread_grad(d_logits, flags[2])
    grad_last = contract_rows(h_two, d_three)
    columns = hidden_bias.shape[1]
    begin = lax.axis_index("rep") * columns
    last_mine = lax.dynamic_slice_in_dim(last_low, begin, columns, 0)
    d_pre_two = gelu_slope(pre_two, contract_cols(d_three, last_mine))
    d_two = spread_grad(d_pre_two, flags[1])
    grad_second = contract_rows(h_one, d_two)
    rows_whole, weight_whole = (
        lax.all_gather(d_two, "rep", axis=1, tiled=True),
        lax.all_gather(second_low, "rep", axis=1, tiled=True),
    )
    weight_mine = lax.dynamic_slice_in_dim(weight_whole, begin, columns, 0)
    d_h_one = contract_cols(rows_whole, weight_mine)
    d_pre_one = gelu_slope(pre_one, d_h_one)
    d_one = spread_grad(d_pre_one, flags[0])
    grad_first = contract_rows(features, d_one)
    grad_hidden = jnp.stack([jnp.sum(d_pre_one, axis=0), jnp.sum(d_pre_two, axis=0)])
    params = (first_weight, second_weight, last_weight, hidden_bias, out_bias)
    moments = (moment_first, moment_second, moment_last, moment_hidden, moment_out)
    squares = (square_first, square_second, square_last, square_hidden, square_out)
    local_grads = (grad_first, grad_second, grad_last, grad_hidden, grad_out)
    summed = lax.psum(
        (local_grads[0], local_grads[1], local_grads[2], local_grads[3], local_grads[4]), "dom"
    )
    results = [
        adamw(w_item, m_item, v_item, g_item)
        for w_item, m_item, v_item, g_item in zip(params, moments, squares, summed)
    ]
    return (
        loss_sum,
        train_count,
        results[0][0],
        results[0][1],
        results[0][2],
        results[1][0],
        results[1][1],
        results[1][2],
        results[2][0],
        results[2][1],
        results[2][2],
        results[3][0],
        results[3][1],
        results[3][2],
        results[4][0],
        results[4][1],
        results[4][2],
    )


def solution(mesh):
    placed = (
        P("dom", None),
        P("dom"),
        P("dom"),
        P("dom", None),
        P("dom", None),
        P("dom", None, None),
        P(None, "dom"),
        P(None, "dom", "rep"),
        P("dom", None),
        P(None, "rep"),
        P(None, "rep"),
        P(),
        P(None, "rep"),
        P(),
        P(None, "rep"),
        P(None, "rep"),
        P(),
        P(None, "rep"),
        P(),
        P(None, "rep"),
        P(None, "rep"),
        P(),
        P(None, "rep"),
        P(),
    )
    return jax.shard_map(
        body,
        mesh=mesh,
        in_specs=placed,
        out_specs=(
            P(),
            P(),
            P(None, "rep"),
            P(None, "rep"),
            P(None, "rep"),
            P(None, "rep"),
            P(None, "rep"),
            P(None, "rep"),
            P(),
            P(),
            P(),
            P(None, "rep"),
            P(None, "rep"),
            P(None, "rep"),
            P(),
            P(),
            P(),
        ),
        check_vma=False,
    )
```

profile of v0, /device:TPU:0, one launch (start us, length us, event | category | flops | bytes accessed | tf_op | source)
XLA Modules:
  0.0 2204.8 jit_solution(2352994811419298481)
XLA Ops:
  11.5 7.3 all-to-all-start
  18.8 20.8 all-gather
  50.8 227.3 %gather_fusion.1 = bf16[65536,64]{1,0:T(8,128)(2,1)} fusion(bf16[4352,64]{1,0:T(8,128)(2,1)S(1)} %copy.309, s32[65536]{0:T(1024)S(1)} %broadcast_clamp_fusion), kind=kCustom, calls=%fused_computation.1 | custom fusion | bytes 17039360 | tf_op jit(solution)/shard_map/gather | solution.py:22
  278.1 46.5 %fusion.2 = f32[4096,64]{1,0:T(8,128)S(1)} fusion(f32[4096,16]{1,0:T(8,128)} %copy.310, bf16[65536,64]{1,0:T(8,128)(2,1)} %gather_fusion.1), kind=kLoop, calls=%fused_computation.17 | loop fusion | flops 12320768 | bytes 9699328 | tf_op jit(solution)/shard_map/reduce_sum | solution.py:23
  328.7 20.0 all-gather.5.cloned.1.call-done
  352.9 5.5 all-to-all-start.1
  358.7 6.4 all-to-all-done.1
  366.1 227.3 %gather_fusion.3 = bf16[65536,64]{1,0:T(8,128)(2,1)} fusion(bf16[4352,64]{1,0:T(8,128)(2,1)S(1)} %copy.315, s32[65536]{0:T(1024)S(1)} %broadcast_clamp_fusion), kind=kCustom, calls=%fused_computation.3 | custom fusion | bytes 17039360 | tf_op jit(solution)/shard_map/gather | solution.py:22
  593.4 46.5 %fusion.1 = f32[4096,64]{1,0:T(8,128)S(1)} fusion(f32[4096,16]{1,0:T(8,128)} %copy.310, bf16[65536,64]{1,0:T(8,128)(2,1)} %gather_fusion.3), kind=kLoop, calls=%fused_computation.15 | loop fusion | flops 12320768 | bytes 9699328 | tf_op jit(solution)/shard_map/reduce_sum | solution.py:23
  646.1 17.2 all-gather.7.cloned.1.call-done
  672.9 5.5 all-to-all-start.2
  687.8 227.3 %gather_fusion.5 = bf16[65536,47]{1,0:T(8,128)(2,1)} fusion(bf16[4352,47]{1,0:T(8,128)(2,1)S(1)} %copy.319, s32[65536]{0:T(1024)S(1)} %broadcast_clamp_fusion), kind=kCustom, calls=%fused_computation.5 | custom fusion | bytes 12582912 | tf_op jit(solution)/shard_map/gather | solution.py:22
  915.1 47.9 %fusion = f32[4096,47]{1,0:T(8,128)} fusion(f32[4096,16]{1,0:T(8,128)} %copy.310, bf16[65536,47]{1,0:T(8,128)(2,1)} %gather_fusion.5), kind=kLoop, calls=%fused_computation.13 | loop fusion | flops 9048064 | bytes 7192576 | tf_op jit(solution)/shard_map/reduce_sum | solution.py:23
  966.6 18.6 psum.50
  989.0 11.5 bitcast_multiply_fusion.2
  1000.5 347.9 %scatter_custom_fusion = f32[4352,47]{1,0:T(8,128)S(1)} fusion(s32[65536]{0:T(1024)} %bitcast.81, f32[65536,47]{1,0:T(8,128)} %bitcast_multiply_fusion.2, f32[]{:T(128)} %constant.22.clone.1), kind=kCustom, calls=%fused_computation.29 | custom fusion | flops 3080192 | bytes 818688 | tf_op jit(solution)/shard_map/scatter-add | solution.py:31
  1373.9 12.6 bitcast_multiply_fusion.1
  1386.5 348.8 %scatter_custom_fusion.2 = f32[4352,64]{1,0:T(8,128)} fusion(s32[65536]{0:T(1024)} %bitcast.82, f32[65536,64]{1,0:T(8,128)} %bitcast_multiply_fusion.1, f32[]{:T(128)} %constant.22.clone.1), kind=kCustom, calls=%fused_computation.33 | custom fusion | flops 4194304 | bytes 1114624 | tf_op jit(solution)/shard_map/scatter-add | solution.py:31
  1758.0 5.7 all_gather.19
  1767.7 9.7 all-gather.9.cloned.1.call-done
  1783.1 11.5 bitcast_multiply_fusion
  1794.6 348.0 %scatter_custom_fusion.4 = f32[4352,64]{1,0:T(8,128)S(1)} fusion(s32[65536]{0:T(1024)} %bitcast.83, f32[65536,64]{1,0:T(8,128)} %bitcast_multiply_fusion, f32[]{:T(128)} %constant.22.clone.1), kind=kCustom, calls=%fused_computation.31 | custom fusion | flops 4194304 | bytes 1114624 | tf_op jit(solution)/shard_map/scatter-add | solution.py:31
  2143.7 5.6 all-to-all-start.5
  2160.3 35.0 %all-reduce.5 = (f32[]{:T(128)}, f32[100,64]{0,1:T(8,128)S(1)}, f32[256,47]{0,1:T(8,128)S(1)}, f32[2,64]{1,0:T(2,128)S(1)}, f32[47]{0:T(128)S(1)}) all-reduce(f32[]{:T(128)} %get-tuple-element.18, f32[100,64]{0,1:T(8,128)S(1)} %convolution_bitcast_fusion, f32[256,47]{0,1:T(8,128)S(1)} %fusion.22, ...), channel_id=1, replica_groups=mesh['dom'=8,'rep'=4] {'dom'}, use_global_device_ids=true, to_apply=%region_7.8 | all-reduce | flops 18608 | bytes 148864 | tf_op jit(solution)/shard_map/psum | solution.py:120
  (199 shorter events, 129.4 us)
Async XLA Ops:
  8.4 342.9 %copy-start.27 = (s32[1024]{0:T(1024)}, s32[1024]{0:T(1024)S(1)}, u32[]{:S(2)}) copy-start(s32[1024]{0:T(1024)S(1)} %pad_clamp_fusion) | copy-start | bytes 12292
  11.5 38.3 %all-to-all-start = ((bf16[8,2,1024]{2,1,0:T(2,128)(2,1)}), bf16[8,2,1024]{2,1,0:T(2,128)(2,1)S(1)}, u32[]{:S(2)}, u32[]{:S(2)}) async-start(bf16[8,2,1024]{2,1,0:T(2,128)(2,1)} %reshape.380), calls=%async_computation | async-start | bytes 65536 | tf_op jit(solution)/shard_map/all_to_all | solution.py:19
  18.8 329.9 %all-gather.5.cloned.1.call-start = ((), (), s32[]{:S(2)}) async-start(), calls=%async_computation.6 | async-start | bytes 2621440 | tf_op jit(solution)/shard_map/all_gather | solution.py:39
  352.9 12.2 all-to-all-start.1
  358.4 304.9 %all-gather.7.cloned.1.call-start = ((), (), s32[]{:S(2)}) async-start(), calls=%async_computation.7 | async-start | bytes 2621440 | tf_op jit(solution)/shard_map/all_gather | solution.py:39
  672.9 12.1 all-to-all-start.2
  1000.5 349.0 %copy-start.32 = (f32[8]{0:T(128)S(1)}, f32[8]{0:T(128)}, u32[]{:S(2)}) copy-start(f32[8]{0:T(128)} %get-tuple-element.44) | copy-start | bytes 100
  1353.1 10.1 all-to-all-start.3
  1386.5 349.8 %copy-start.31 = (f32[8]{0:T(128)S(1)}, f32[8]{0:T(128)}, u32[]{:S(2)}) copy-start(f32[8]{0:T(128)} %get-tuple-element.45) | copy-start | bytes 100
  1737.1 10.2 all-to-all-start.4
  1740.5 36.9 %all-gather.9.cloned.1.call-start = ((), (), s32[]{:S(2)}) async-start(), calls=%async_computation.8 | async-start | bytes 2621440 | tf_op jit(solution)/shard_map/all_gather | solution.py:132
  1758.0 391.3 %all-reduce.4.cloned.1.call-start = ((), (), s32[]{:S(2)}) async-start(), calls=%async_computation.9 | async-start | bytes 131072 | tf_op jit(solution)/shard_map/psum | solution.py:145
  1794.6 348.0 %copy-start.30 = (f32[8]{0:T(128)S(1)}, f32[8]{0:T(128)}, u32[]{:S(2)}) copy-start(f32[8]{0:T(128)} %get-tuple-element.43) | copy-start | bytes 100
  1794.6 354.7 %copy-start.10 = (f32[256,64]{0,1:T(8,128)S(1)}, f32[256,64]{0,1:T(8,128)}, u32[]{:S(2)}) copy-start(f32[256,64]{0,1:T(8,128)} %param.34) | copy-start | bytes 196612
  1794.6 354.7 %copy-start.16 = (f32[256,64]{0,1:T(8,128)S(1)}, f32[256,64]{0,1:T(8,128)}, u32[]{:S(2)}) copy-start(f32[256,64]{0,1:T(8,128)} %param.39) | copy-start | bytes 196612
  1794.6 354.7 %copy-start.17 = (f32[256,64]{0,1:T(8,128)S(1)}, f32[256,64]{0,1:T(8,128)}, u32[]{:S(2)}) copy-start(f32[256,64]{0,1:T(8,128)} %param.44) | copy-start | bytes 196612
  2143.7 12.5 all-to-all-start.5
  2157.0 38.3 %copy-start.39 = (f32[47]{0:T(128)S(1)}, f32[47]{0:T(128)}, u32[]{:S(2)}) copy-start(f32[47]{0:T(128)} %param.42) | copy-start | bytes 568
  2157.0 38.3 %copy-start.40 = (f32[47]{0:T(128)S(1)}, f32[47]{0:T(128)}, u32[]{:S(2)}) copy-start(f32[47]{0:T(128)} %param.47) | copy-start | bytes 568
  2157.0 38.8 %copy-start.29 = (f32[2,64]{1,0:T(2,128)S(1)}, f32[2,64]{1,0:T(2,128)}, u32[]{:S(2)}) copy-start(f32[2,64]{1,0:T(2,128)} %param.36) | copy-start | bytes 1540
  2157.0 38.8 %copy-start.36 = (f32[2,64]{1,0:T(2,128)S(1)}, f32[2,64]{1,0:T(2,128)}, u32[]{:S(2)}) copy-start(f32[2,64]{1,0:T(2,128)} %param.41) | copy-start | bytes 1540
  2157.1 38.8 %copy-start.37 = (f32[2,64]{1,0:T(2,128)S(1)}, f32[2,64]{1,0:T(2,128)}, u32[]{:S(2)}) copy-start(f32[2,64]{1,0:T(2,128)} %param.46) | copy-start | bytes 1540
  2159.8 37.3 %copy-start.12 = (f32[256,47]{0,1:T(8,128)S(1)}, f32[256,47]{0,1:T(8,128)}, u32[]{:S(2)}) copy-start(f32[256,47]{0,1:T(8,128)} %param.35) | copy-start | bytes 144388
  2159.8 37.3 %copy-start.20 = (f32[256,47]{0,1:T(8,128)S(1)}, f32[256,47]{0,1:T(8,128)}, u32[]{:S(2)}) copy-start(f32[256,47]{0,1:T(8,128)} %param.40) | copy-start | bytes 144388
  (27 other events, 363.4 us)
Sparse Core Ops, SparseCore 0:
  328.8 19.8 all-gather.4
  644.2 19.0 all-gather.6
  1758.1 19.2 all-gather.8
  1781.2 68.5 all-reduce.3
where the time goes:
time: 2210 us; the launch traced here: 2200 us
  other arithmetic  1260 us (57%)
  local copies, waits for them, and re-layouts  735 us (33%)
  blocking collectives  80.1 us (4%)
  waiting for transfers between devices  69.8 us (3%)
  starting transfers between devices  30.9 us (1%)
    scatter-add x3, other arithmetic, spread_back(): jnp.zeros((table_rows, breadth), jnp.float32).at[edge_src.reshape(-1)]  1040 us
    gather x3, local copies, waits for them, and re-layouts, aggregate(): picked = lookup[edge_src].astype(jnp.float32)  682 us
    reduce_sum x3, other arithmetic, aggregate(): return jnp.sum(picked * edge_norm[:, :, None], axis=1)  141 us
    psum x2, blocking collectives, body(): lax.psum((jnp.sum(row_loss * masked), jnp.sum(masked)), 'dom')  53.6 us
  transfers between devices with their start and end apart: 10, of which 8 were waited for; matrix products, arithmetic and copies ran while one was open for 18% of the time, Pallas kernels for 0%

commit v1 on v0

v1 whole, which is shorter than its diff:
```python
import functools

import jax
import jax.numpy as jnp
from jax import lax
from jax.experimental import pallas as pl
from jax.experimental.pallas import tpu as pltpu
from jax.sharding import PartitionSpec as P

STEP = 5
beta_one = 0.5
beta_two = 0.5
rate_step = 0.03
decay_rate = 0.01
epsilon = 1e-08

BF16, F32, F8, I32 = jnp.bfloat16, jnp.float32, jnp.float8_e4m3fn, jnp.int32
REST_GAIN = 4096.0
TAIL_GAIN = 256.0
FLAG_LANE = 100
ROWS = 512
LIMIT = 36 << 20

SMEM = pl.BlockSpec(memory_space=pltpu.SMEM)
HBM = pl.BlockSpec(memory_space=pltpu.HBM)


def whole(array):
    rank = len(array.shape)
    return array, pl.BlockSpec(array.shape, lambda *_: (0,) * rank)


def wholes(*arrays):
    return [whole(a) for a in arrays]


def columns_of(array, size=ROWS):
    return array, pl.BlockSpec((array.shape[0], size), lambda i: (0, i))


def run(kernel, name, grid, args, outs, scratch=(), flops=0):
    shapes = [jax.ShapeDtypeStruct(shape, kind) for shape, kind, _ in outs]
    return pl.pallas_call(
        kernel,
        grid=(grid,),
        in_specs=[spec for _, spec in args],
        out_specs=[spec if spec is not None else whole(s)[1] for s, (_, _, spec) in zip(shapes, outs)],
        out_shape=shapes,
        scratch_shapes=list(scratch),
        name=name,
        cost_estimate=pl.CostEstimate(flops=flops, bytes_accessed=1 << 20, transcendentals=0),
        compiler_params=pltpu.CompilerParams(vmem_limit_bytes=LIMIT),
    )(*[a for a, _ in args])


def dot_nn(left, right):
    return lax.dot_general(left, right, (((1,), (0,)), ((), ())), preferred_element_type=F32)


def dot_nt(left, right):
    return lax.dot_general(left, right, (((1,), (1,)), ((), ())), preferred_element_type=F32)


def dot_tn(left, right):
    return lax.dot_general(left, right, (((0,), (0,)), ((), ())), preferred_element_type=F32)


def scale_of(value):
    most = jnp.maximum(jnp.max(jnp.abs(value)), 1e-30)
    return 256.0 / most, most * (1.0 / 256.0)


def span(start, size):
    return pl.ds(pl.multiple_of(start, size), size)


def pick_rows(send, first, count):
    nodes = lax.broadcasted_iota(I32, (send.shape[0], count), 1) + first
    return jnp.where(send == nodes, 1.0, 0.0).astype(BF16)


class Ring:
    def __init__(self, refs, bufs, sems, cut):
        self.refs, self.bufs, self.sems, self.cut = refs, bufs, sems, cut
        self.step, self.steps = pl.program_id(0), pl.num_programs(0)
        self.slot = lax.rem(self.step, 2)

    def copies(self, step, slot):
        return [
            pltpu.make_async_copy(ref.at[self.cut(step)], buf.at[slot], self.sems.at[k, slot])
            for k, (ref, buf) in enumerate(zip(self.refs, self.bufs))
        ]

    def begin(self):
        @pl.when(self.step == 0)
        def _():
            for copy in self.copies(0, 0):
                copy.start()

        @pl.when((self.step == 0) & (self.steps > 1))
        def _():
            for copy in self.copies(1, 1):
                copy.start()

    def wait(self):
        for copy in self.copies(self.step, self.slot):
            copy.wait()
        return [buf.at[self.slot] for buf in self.bufs]

    def end(self):
        @pl.when(self.step + 2 < self.steps)
        def _():
            for copy in self.copies(self.step + 2, self.slot):
                copy.start()


def ring_scratch(shape, kinds):
    return [pltpu.VMEM((2, *shape), kind) for kind in kinds] + [pltpu.SemaphoreType.DMA((len(kinds), 2))]


def pack_kernel(feat_t, send, changed, mask, first_t, second_t, cache_t, bias, rows_out, pack_out):
    nodes, halo = feat_t.shape[1], send.shape[0]
    width, cols = feat_t.shape[0], first_t.shape[0]

    def pick(i, total):
        return total + dot_nt(pick_rows(send[...], i * ROWS, ROWS), feat_t[:, span(i * ROWS, ROWS)])

    total = lax.fori_loop(0, nodes // ROWS, pick, jnp.zeros((halo, width), F32))
    count = jnp.sum(mask[...].astype(F32))
    many = jnp.floor(count * (1.0 / 64.0))
    lane = lax.broadcasted_iota(I32, (halo, 128), 1)
    row = jnp.concatenate([total, jnp.zeros((halo, 128 - width), F32)], axis=1)
    for layer in range(3):
        row = jnp.where(lane == FLAG_LANE + layer, changed[layer, 0].astype(F32), row)
    row = jnp.where(lane == FLAG_LANE + 3, many, row)
    row = jnp.where(lane == FLAG_LANE + 4, count - 64.0 * many, row)
    rows_out[...] = row.astype(BF16).reshape(rows_out.shape)

    units = second_t.shape[1]
    pack_out[:, 0:128] = jnp.concatenate(
        [first_t[...], jnp.zeros((cols, 128 - width), F32)], axis=1
    ).astype(BF16)
    pack_out[:, 128 : 128 + units] = second_t[...].astype(BF16)
    left = jnp.concatenate([bias[...], jnp.zeros((2, 128 - cols), F32)], axis=1)
    terms = []
    for _ in range(3):
        term = left.astype(BF16).astype(F32)
        terms.append(term)
        left = left - term
    terms = jnp.concatenate(terms + [jnp.zeros((122, 128), F32)], axis=0).T
    pack_out[:, 128 + units : 256 + units] = terms[0:cols, :].astype(BF16)
    base = 256 + units
    for layer in range(2):
        pack_out[:, base + layer * halo : base + (layer + 1) * halo] = cache_t[layer]


def bias_column(packs, layer):
    units = packs.shape[0]
    terms = packs[:, 128 + units : 256 + units].astype(F32)
    return terms[:, layer : layer + 1] + terms[:, layer + 2 : layer + 3] + terms[:, layer + 4 : layer + 5]


def stale_columns(packs, layer, halo):
    base = 256 + packs.shape[0] + layer * halo
    return packs[:, base : base + halo].astype(F32)


def build_kernel(place, src_t, norm_t, high, rest):
    slots = src_t.shape[0]
    half = src_t.shape[1] // 2
    blocks = high.shape[1] // 256
    per_group = 256 // slots
    here = span(place[0] * half + pl.program_id(0) * 128, 128)
    lean = lambda tile: [
        pltpu.roll(tile[first : first + 8, :], 0, 1, stride=per_group, stride_axis=0)
        for first in range(0, slots, 8)
    ]
    source, weights = lean(src_t[:, here]), lean(norm_t[:, here])
    in_slot = lax.broadcasted_iota(I32, (8, 128), 1) // per_group == lax.broadcasted_iota(I32, (8, 128), 0)
    node_row = lax.broadcasted_iota(I32, (per_group, 256), 0)
    mine = lax.rem(lax.broadcasted_iota(I32, (per_group, 256), 1), per_group) == node_row
    inner = lax.broadcasted_iota(I32, (256, 256), 0)

    def flat(tiles, group):
        moved = [pltpu.roll(tile, (128 - per_group * group) % 128, 1) for tile in tiles]
        return jnp.concatenate(
            [jnp.sum(jnp.where(in_slot, tile, 0), axis=0, keepdims=True) for tile in moved], axis=1
        )

    def one(group):
        at = flat(source, group)
        weight = flat(weights, group)
        weight_high = weight.astype(BF16).astype(F32)
        hit = inner == jnp.bitwise_and(at, 255)
        right = jnp.concatenate(
            [
                jnp.where(hit, weight_high, 0.0).astype(BF16),
                jnp.where(hit, weight - weight_high, 0.0).astype(BF16),
            ],
            axis=1,
        )
        block = jnp.where(mine, jnp.right_shift(at, 8), -1)
        left = jnp.concatenate(
            [jnp.where(block == j, 1.0, 0.0).astype(BF16) for j in range(blocks)], axis=0
        )
        return dot_nt(jnp.concatenate([left, left], axis=1), right)

    parts = [one(group) for group in range(128 // per_group)]
    for j in range(blocks):
        full = jnp.concatenate([p[per_group * j : per_group * (j + 1), :] for p in parts], axis=0)
        top = full.astype(BF16)
        cols = slice(256 * j, 256 * (j + 1))
        high[:, cols] = top
        rest[:, cols] = ((full - top.astype(F32)) * REST_GAIN).astype(F8)


def gelu_both(u):
    square = u * u
    t = jnp.tanh(0.79788456 * (u + 0.044715 * u * square))
    half = 0.5 * (1.0 + t)
    slope = half + 0.5 * u * (1.0 - t * t) * (0.79788456 * (1.0 + 3.0 * 0.044715 * square))
    return u * half, slope


def layer_one_kernel(place, rows, feat_t, packs, send, high, rest, hidden_t, slope_t, z_own, z_send, flags_t, table, table8, back, hbuf, rbuf, sems):
    width, nodes = feat_t.shape
    halo = send.shape[0]
    step = pl.program_id(0)
    ring = Ring((high, rest), (hbuf, rbuf), sems, lambda i: (span(i * ROWS, ROWS), slice(None)))
    ring.begin()

    @pl.when(step == 0)
    def _():
        weight = packs[:, 0:width]
        flat = rows[...].reshape(halo, 128)
        flags = flat.astype(F32).T[FLAG_LANE : FLAG_LANE + 8, :]
        counts = jnp.sum(rows[...].astype(F32)[:, 0, :], axis=0, keepdims=True)
        count = 64.0 * counts[:, FLAG_LANE + 3 : FLAG_LANE + 4] + counts[:, FLAG_LANE + 4 : FLAG_LANE + 5]
        row = lax.broadcasted_iota(I32, flags.shape, 0)
        flags_t[...] = jnp.where(row == 3, count, flags)

        def first(i, most):
            here = span(i * ROWS, ROWS)
            z = dot_nn(weight, feat_t[:, here])
            table[:, here] = z.astype(BF16)
            return jnp.maximum(most, jnp.abs(z))

        most = lax.fori_loop(0, nodes // ROWS, first, jnp.zeros((table.shape[0], ROWS), F32))
        border = dot_nt(weight, flat[:, 0:width]).astype(BF16).astype(F32)
        border = jnp.where(flags[0:1, :] == 1.0, border, stale_columns(packs, 0, halo))
        table[:, nodes : nodes + halo] = border.astype(BF16)
        scale, inverse = scale_of(jnp.maximum(jnp.max(most), jnp.max(jnp.abs(border))))
        back[0] = inverse * (1.0 / REST_GAIN)

        def small(i, carry):
            here = span(i * 256, 256)
            table8[:, here] = (table[:, here].astype(F32) * scale).astype(F8)
            return carry

        lax.fori_loop(0, (nodes + halo) // 256, small, 0)
        z_send[...] = jnp.zeros(z_send.shape, BF16)

    units = packs.shape[0]
    top, low = ring.wait()
    total = dot_nt(table[...], top[...]) + dot_nt(table8[...], low[...]) * back[0]
    ring.end()
    value, slope = gelu_both(total + bias_column(packs, 0))
    value = value.astype(BF16)
    hidden_t[...] = value
    slope_t[...] = slope
    z = dot_nn(packs[:, 128 : 128 + units], value).astype(BF16)
    z_own[...] = z
    half = nodes // 2
    chosen = dot_nt(pick_rows(send[...], place[0] * half + step * ROWS, ROWS), z)
    z_send[...] = (z_send[...].astype(F32) + chosen.reshape(z_send.shape)).astype(BF16)


def own_part_kernel(place, high, rest, z_own, z_oth, total, high8, table, table8, back, hbuf, rbuf, sems):
    half = z_own.shape[1]
    nodes = 2 * half
    ring = Ring((high, rest), (hbuf, rbuf), sems, lambda i: (span(i * ROWS, ROWS), slice(None)))
    ring.begin()

    @pl.when(pl.program_id(0) == 0)
    def _():
        def larger(i, most):
            here = span(i * ROWS, ROWS)
            both = jnp.maximum(jnp.abs(z_own[:, here].astype(F32)), jnp.abs(z_oth[:, here].astype(F32)))
            return jnp.maximum(most, both)

        most = lax.fori_loop(0, half // ROWS, larger, jnp.zeros((z_own.shape[0], ROWS), F32))
        scale, inverse = scale_of(most)
        back[0] = inverse * (1.0 / REST_GAIN)
        for ref, first in ((z_own, place[0] * half), (z_oth, (1 - place[0]) * half)):

            def put(i, carry):
                value = ref[:, span(i * ROWS, ROWS)]
                cols = span(first + i * ROWS, ROWS)
                table[:, cols] = value
                table8[:, cols] = (value.astype(F32) * scale).astype(F8)
                return carry

            lax.fori_loop(0, half // ROWS, put, 0)

    top, low = ring.wait()
    total[...] = dot_nt(table[...], top[:, 0:nodes]) + dot_nt(table8[...], low[:, 0:nodes]) * back[0]
    if high8 is not None:
        high8[...] = top[...].astype(F8)
    ring.end()


def own_part_plain_kernel(place, high, rest, z_own, z_oth, total, *scratch):
    own_part_kernel(place, high, rest, z_own, z_oth, total, None, *scratch)


def layer_two_end_kernel(place, flags_t, packs, send, high, rest, total, came, came_oth, last_t, hidden_t, slope_t, z_own, z_send, border, border8, back):
    halo = send.shape[0]
    width = hidden_t.shape[0]
    kinds = last_t.shape[0]
    step = pl.program_id(0)
    half = ROWS * pl.num_programs(0)

    @pl.when(step == 0)
    def _():
        both = came[...].reshape(halo, width).astype(F32) + came_oth[...].reshape(halo, width).astype(F32)
        value = jnp.where(flags_t[1:2, :] == 1.0, both.T, stale_columns(packs, 1, halo))
        scale, inverse = scale_of(value)
        border[...] = value.astype(BF16)
        border8[...] = (value * scale).astype(F8)
        back[0] = inverse * (1.0 / REST_GAIN)
        z_send[...] = jnp.zeros(z_send.shape, BF16)

    sums = total[...] + dot_nt(border[...], high[...]) + dot_nt(border8[...], rest[...]) * back[0]
    value, slope = gelu_both(sums + bias_column(packs, 1))
    value = value.astype(BF16)
    hidden_t[...] = value
    slope_t[...] = slope
    z = dot_nn(last_t[...].astype(BF16), value).astype(BF16)
    z_own[...] = z
    chosen = dot_nt(pick_rows(send[...], place[0] * half + step * ROWS, ROWS), z)
    chosen = jnp.concatenate([chosen, jnp.zeros((halo, 128 - kinds), F32)], axis=1)
    z_send[...] = (z_send[...].astype(F32) + chosen.reshape(z_send.shape)).astype(BF16)


def put_scales(back_out, step, rest_value, tail_value):
    lane = lax.broadcasted_iota(I32, (1, 128), 1)
    back_out[pl.ds(step, 1), :] = jnp.where(lane == 0, rest_value, tail_value)


def put_border(border_grad, total, keep):
    value = (total * keep).T
    bound = value.shape[0] // border_grad.shape[0]
    border_grad[:, 0:bound, :] = value.reshape(border_grad.shape[0], bound, value.shape[1])


def loss_kernel(classes, place, flags_t, high, rest, total, came, came_oth, stale_t, bias, labels, mask, sums, grads, grads8, back_out, border_grad, border, border8, back, border_sum):
    kinds = total.shape[0]
    halo = stale_t.shape[1]
    step = pl.program_id(0)

    @pl.when(step == 0)
    def _():
        both = came[...].reshape(halo, 128).astype(F32) + came_oth[...].reshape(halo, 128).astype(F32)
        old = jnp.concatenate([stale_t[...].astype(F32), jnp.zeros((kinds - classes, halo), F32)], axis=0)
        value = jnp.where(flags_t[2:3, :] == 1.0, both.T[0:kinds, :], old)
        scale, inverse = scale_of(value)
        border[...] = value.astype(BF16)
        border8[...] = (value * scale).astype(F8)
        back[0] = inverse * (1.0 / REST_GAIN)
        sums[...] = jnp.zeros(sums.shape, F32)
        border_sum[...] = jnp.zeros(border_sum.shape, F32)

    count = flags_t[3:4, 0:1]
    logits = total[...] + dot_nt(border[...], high[...]) + dot_nt(border8[...], rest[...]) * back[0]
    logits = logits + bias[...]
    kind = lax.broadcasted_iota(I32, logits.shape, 0)
    real = kind < classes
    logits = jnp.where(real, logits, -jnp.inf)
    shifted = logits - jnp.max(logits, axis=0, keepdims=True)
    powers = jnp.exp(shifted)
    norm = jnp.sum(powers, axis=0, keepdims=True)
    logp = jnp.where(real, shifted - jnp.log(norm), 0.0)
    here = span(step * ROWS, ROWS)
    target = jnp.where(kind == labels[pl.ds(place[0], 1), here], 0.9, 0.0) + 0.1 / classes
    used = mask[pl.ds(place[0], 1), here].astype(F32)
    loss = -jnp.sum(jnp.sum(target * logp, axis=0, keepdims=True) * used)
    grad = jnp.where(real, (powers / norm - target) * (used / count), 0.0)
    sums[0:kinds, :] += jnp.broadcast_to(jnp.sum(grad, axis=1, keepdims=True), (kinds, 128))
    sums[kinds : kinds + 8, :] += jnp.full((8, 128), loss, F32)
    top = grad.astype(BF16)
    tail = (grad - top.astype(F32)).astype(BF16)
    stacked = jnp.concatenate([top, tail], axis=0)
    small = (top.astype(F32) * (256.0 * count)).astype(F8)
    grads[...] = stacked
    grads8[...] = small
    inverse = (1.0 / (256.0 * REST_GAIN)) / count
    back_out[...] = jnp.broadcast_to(inverse, back_out.shape)
    both = dot_nn(stacked, high[...])
    border_sum[0:kinds, :] += both[0:kinds] + both[kinds : 2 * kinds] + dot_nn(small, rest[...]) * inverse

    @pl.when(step == pl.num_programs(0) - 1)
    def _():
        put_border(border_grad, border_sum[...], flags_t[2:3, :])


def back_three_kernel(other, place, high, rest, grads, grads8, back, out, hbuf, rbuf, sems):
    kinds, size = out.shape
    half = size * pl.num_programs(0)
    owner = 1 - place[0] if other else place[0]
    ring = Ring((high, rest), (hbuf, rbuf), sems, lambda i: (slice(None), span(owner * half + i * size, size)))
    ring.begin()
    top, low = ring.wait()
    both = dot_nn(grads[...], top[...])
    out[...] = both[0:kinds] + both[kinds : 2 * kinds] + dot_nn(grads8[...], low[...]) * back[0:1, 0:1]
    ring.end()


def back_kernel(other, halves, place, high, rest, high8, grads, grads8, tails8, back, out, hbuf, rbuf, tbuf, sems):
    size = out.shape[1]
    count = size * pl.num_programs(0)
    owner = 1 - place[0] if other else place[0]
    base = owner * count * halves + (place[1] * count if halves == 2 else 0)
    ring = Ring((high, rest, high8), (hbuf, rbuf, tbuf), sems, lambda i: (slice(None), span(base + i * size, size)))
    ring.begin()
    top, low, eight = ring.wait()
    total = dot_nn(grads[...], top[...])
    for b in range(grads.shape[1] // ROWS):
        cut = slice(b * ROWS, (b + 1) * ROWS)
        total = total + dot_nn(grads8[:, cut], low[cut, :]) * back[b : b + 1, 0:1]
        total = total + dot_nn(tails8[:, cut], eight[cut, :]) * back[b : b + 1, 1:2]
    out[...] = total
    ring.end()


def returned_terms(ret, ret_oth, bound, kinds):
    value = ret[:, 0:bound, :] + ret_oth[:, 0:bound, :]
    value = value.reshape(value.shape[0] * bound, value.shape[2]).T[0:kinds, :]
    top = value.astype(BF16)
    return top, (value - top.astype(F32)).astype(BF16)


def round_gradient(own, came_part, terms, send, first_node):
    chosen = pick_rows(send, first_node, own.shape[1])
    total = own[...] + came_part[...]
    for term in terms:
        total = total + dot_nn(term[...], chosen)
    return total.astype(BF16)


def upstream(grad, high, rest, high8, sums, grads, grads8, tails8, back_out, border_sum):
    sums[...] += jnp.broadcast_to(jnp.sum(grad, axis=1, keepdims=True), sums.shape)
    scale, inverse = scale_of(grad)
    top = grad.astype(BF16)
    wide = top.astype(F32)
    small = (wide * scale).astype(F8)
    tail = ((grad - wide) * (scale * TAIL_GAIN)).astype(F8)
    grads[...] = top
    grads8[...] = small
    tails8[...] = tail
    back_rest = inverse * (1.0 / REST_GAIN)
    back_tail = inverse * (1.0 / TAIL_GAIN)
    put_scales(back_out, pl.program_id(0), back_rest, back_tail)
    got = dot_nn(top, high[...])
    got = got + dot_nn(small, rest[...]) * back_rest
    border_sum[...] += got + dot_nn(tail, high8[...]) * back_tail


def end_three_kernel(place, flags_t, high, rest, high8, own, came_part, ret, ret_oth, send, hidden_t, slope_t, last, sums, grads, grads8, tails8, back_out, border_grad, border_sum, term_one, term_two, grad_last):
    kinds = own.shape[0]
    step = pl.program_id(0)
    half = ROWS * pl.num_programs(0)
    bound = send.shape[0] // ret.shape[0]

    @pl.when(step == 0)
    def _():
        term_one[...], term_two[...] = returned_terms(ret, ret_oth, bound, kinds)
        sums[...] = jnp.zeros(sums.shape, F32)
        border_sum[...] = jnp.zeros(border_sum.shape, F32)
        grad_last[...] = jnp.zeros(grad_last.shape, F32)

    d_z = round_gradient(own, came_part, (term_one, term_two), send[...], place[0] * half + step * ROWS)
    grad_last[0:kinds, :] += dot_nt(d_z, hidden_t[...])
    grad = dot_nn(last[...].astype(BF16), d_z) * slope_t[...]
    upstream(grad, high, rest, high8, sums, grads, grads8, tails8, back_out, border_sum)

    @pl.when(step == pl.num_programs(0) - 1)
    def _():
        put_border(border_grad, border_sum[...], flags_t[1:2, :])
        parts, _, width = border_grad.shape
        border_grad[:, bound:, :] = grad_last[...].reshape(parts, 64 // parts, width)


def end_two_kernel(place, flags_t, packs, high, rest, high8, own, came_part, ret, ret_oth, send, hidden_t, slope_t, sums, grads, grads8, tails8, back_out, border_grad, last_chunk, border_sum, term_one, term_two, grad_second):
    units = own.shape[0]
    step = pl.program_id(0)
    half = ROWS * pl.num_programs(0)
    bound = send.shape[0] // ret.shape[0]

    @pl.when(step == 0)
    def _():
        term_one[...], term_two[...] = returned_terms(ret, ret_oth, bound, units)
        last_chunk[...] = jnp.sum(ret[:, bound:, :] + ret_oth[:, bound:, :], axis=0)
        sums[...] = jnp.zeros(sums.shape, F32)
        border_sum[...] = jnp.zeros(border_sum.shape, F32)
        grad_second[...] = jnp.zeros(grad_second.shape, F32)

    d_z = round_gradient(own, came_part, (term_one, term_two), send[...], place[0] * half + step * ROWS)
    grad_second[...] += dot_nt(d_z, hidden_t[...])
    grad = dot_tn(packs[:, 128 : 128 + units], d_z) * slope_t[...]
    upstream(grad, high, rest, high8, sums, grads, grads8, tails8, back_out, border_sum)

    @pl.when(step == pl.num_programs(0) - 1)
    def _():
        put_border(border_grad, border_sum[...], flags_t[0:1, :])
        parts, _, width = border_grad.shape
        size = 64 // parts
        for core in range(2):
            block = grad_second[span(place[1] * 128 + core * 64, 64), :]
            first = bound + core * size
            border_grad[:, first : first + size, :] = block.reshape(parts, size, width)


def end_one_kernel(place, own, came_part, ret, ret_oth, send, feat_t, sums_one, sums_two, sums_out, *rest_refs):
    outs, second_chunk, term_one, term_two, grad_first = (
        rest_refs[0:4],
        rest_refs[4],
        rest_refs[5],
        rest_refs[6],
        rest_refs[7],
    )
    units = own.shape[0]
    step = pl.program_id(0)
    size = ROWS * pl.num_programs(0)
    parts = ret.shape[0]
    bound = send.shape[0] // parts
    width = feat_t.shape[0]
    chunk = 64 // parts

    @pl.when(step == 0)
    def _():
        term_one[...], term_two[...] = returned_terms(ret, ret_oth, bound, units)
        mine = pl.ds(bound + place[0] * chunk, chunk)
        second_chunk[...] = jnp.sum(ret[:, mine, :] + ret_oth[:, mine, :], axis=0)
        grad_first[...] = jnp.zeros(grad_first.shape, F32)

    base = place[0] * 2 * size + place[1] * size + step * ROWS
    d_z = round_gradient(own, came_part, (term_one, term_two), send[...], base)
    grad_first[:, 0:width] += dot_nt(d_z, feat_t[:, span(base, ROWS)])

    @pl.when(step == pl.num_programs(0) - 1)
    def _():
        lead = jnp.where(place[1] == 0, 1.0, 0.0)
        lane = lax.broadcasted_iota(I32, (64, 128), 1)
        for k, out in enumerate(outs):
            rows = span(jnp.bitwise_xor(place[0] + 2 * place[1], k) * 64, 64)
            value = grad_first[rows, :]
            value = jnp.where(lane == FLAG_LANE, sums_one[rows, :] * lead, value)
            value = jnp.where(lane == FLAG_LANE + 1, sums_two[rows, :] * lead, value)
            out[...] = jnp.where(lane == FLAG_LANE + 2, sums_out[...] * lead, value)


def gather_kernel(mine, one, two, three, second_chunk, last_chunk, out):
    total = mine[...] + one[...] + two[...] + three[...]
    size = second_chunk.shape[0]
    parts = [total]
    for chunk in (second_chunk, last_chunk):
        parts += [chunk[:, 0:128], chunk[:, 128:256]]
    value = jnp.concatenate(parts, axis=0)
    for p in range(out.shape[0]):
        out[p] = value


def adamw(weight, moment, square, gradient):
    moment = beta_one * moment + (1.0 - beta_one) * gradient
    square = beta_two * square + (1.0 - beta_two) * gradient * gradient
    moment_hat = moment / (1.0 - beta_one**STEP)
    square_hat = square / (1.0 - beta_two**STEP)
    weight = weight - rate_step * (
        moment_hat / (jnp.sqrt(square_hat) + epsilon) + decay_rate * weight
    )
    return (weight, moment, square)


def update_kernel(came, flags_t, *refs):
    params, outs = refs[0:15], refs[15:]
    parts = came.shape[0]
    size = 64 // parts
    width, kinds = params[0].shape[1], params[6].shape[0]
    total = jnp.sum(came[:, 0:64, :], axis=0)

    def chunks(first):
        halves = [
            came[:, first + k * size : first + (k + 1) * size, :].reshape(64, 128) for k in range(2)
        ]
        return jnp.concatenate(halves, axis=1)

    turned = jnp.concatenate([total, jnp.zeros((64, 128), F32)], axis=0).T
    gradients = (
        total[:, 0:width],
        chunks(64),
        chunks(64 + 2 * size)[0:kinds, :],
        turned[FLAG_LANE : FLAG_LANE + 2, 0:64],
        turned[FLAG_LANE + 2 : FLAG_LANE + 3, 0:kinds],
    )
    for k, gradient in enumerate(gradients):
        values = adamw(*[ref[...] for ref in params[3 * k : 3 * k + 3]], gradient)
        for ref, value in zip(outs[3 * k : 3 * k + 3], values):
            ref[...] = value
    padded = turned[FLAG_LANE + 2 : FLAG_LANE + 3, 48:49]
    outs[15][...] = jnp.broadcast_to(padded, (1, 128))
    outs[16][...] = jnp.broadcast_to(flags_t[3:4, 0:1], (1, 128))


def body(
    parts,
    reps,
    features,
    labels,
    train_mask,
    edge_src,
    edge_norm,
    send_rows,
    changed,
    cache_hidden,
    cache_out,
    first_weight,
    second_weight,
    last_weight,
    hidden_bias,
    out_bias,
    moment_first,
    moment_second,
    moment_last,
    moment_hidden,
    moment_out,
    square_first,
    square_second,
    square_last,
    square_hidden,
    square_out,
):
    nodes, in_width = features.shape
    half = nodes // 2
    bound = send_rows.shape[2]
    halo = parts * bound
    table = nodes + halo
    units, classes = last_weight.shape
    kinds = -(-classes // 16) * 16
    steps = half // ROWS

    rep = lax.axis_index("rep")
    place = jnp.stack([lax.rem(rep, 2), lax.div(rep, 2)]).astype(I32)
    where = (place, SMEM)
    feat_t = features.T
    send = send_rows.reshape(halo, 1)
    last_t = jnp.pad(last_weight.T, ((0, kinds - classes), (0, 0)))
    last_pad = last_t.T
    bias_out = jnp.pad(out_bias, (0, kinds - classes)).reshape(kinds, 1)
    label_rows = labels.reshape(2, half)
    mask_rows = train_mask.reshape(2, half)

    def swap(x, k=1):
        return lax.ppermute(x, "rep", [(i, i ^ k) for i in range(reps)])

    def exchange(x):
        return lax.all_to_all(x, "dom", split_axis=0, concat_axis=0, tiled=True)

    def late(x, after):
        return lax.optimization_barrier((x, after))

    node_block = lambda size, rows: pl.BlockSpec((rows, size), lambda i: (0, i))
    border_rows = lambda a: (a, pl.BlockSpec((ROWS, halo), lambda i: (i, nodes // halo)))
    work = 2 * half * table * units

    rows_out, pack = run(
        pack_kernel,
        "pack",
        1,
        [*wholes(feat_t, send), (changed, SMEM)]
        + wholes(
            train_mask.reshape(nodes // 128, 128),
            first_weight.T,
            second_weight.T,
            jnp.transpose(cache_hidden, (0, 2, 1)),
            hidden_bias,
        ),
        [((parts, bound, 128), BF16, None), ((units // reps, 256 + units + 2 * halo), BF16, None)],
        flops=2 * halo * nodes * 128,
    )
    rows = exchange(rows_out)
    packs = lax.all_gather(pack, "rep", axis=0, tiled=True)
    row_block = pl.BlockSpec((128, table), lambda i: (i, 0))
    high, rest = run(
        build_kernel,
        "build",
        half // 128,
        [where, *wholes(edge_src.T, edge_norm.T)],
        [((half, table), BF16, row_block), ((half, table), F8, row_block)],
        flops=4 * 256 * table * half,
    )
    in_hbm = [(high, HBM), (rest, HBM)]
    row_ring = ring_scratch((ROWS, table), (BF16, F8))
    scalar = pltpu.SMEM((1,), F32)
    block = node_block(ROWS, units)

    hidden_one, slope_one, z_own, z_send, flags_t = run(
        layer_one_kernel,
        "layer_one",
        steps,
        [where, *wholes(rows, feat_t, packs, send), *in_hbm],
        [
            ((units, half), BF16, block),
            ((units, half), F32, block),
            ((units, half), BF16, block),
            ((parts, bound, units), BF16, None),
            ((8, halo), F32, None),
        ],
        [pltpu.VMEM((units, table), BF16), pltpu.VMEM((units, table), F8), scalar, *row_ring],
        flops=work,
    )
    z_oth = swap(z_own)
    came = exchange(z_send)
    total, high8 = run(
        own_part_kernel,
        "layer_two_own",
        steps,
        [where, *in_hbm, *wholes(z_own, z_oth)],
        [((units, half), F32, block), ((half, table), F8, pl.BlockSpec((ROWS, table), lambda i: (i, 0)))],
        [pltpu.VMEM((units, nodes), BF16), pltpu.VMEM((units, nodes), F8), scalar, *row_ring],
        flops=work,
    )
    came, total = late(came, total)
    came_oth = swap(came)
    small = node_block(ROWS, kinds)
    border_scratch = lambda n: [pltpu.VMEM((n, halo), BF16), pltpu.VMEM((n, halo), F8), scalar]
    hidden_two, slope_two, z_own, z_send = run(
        layer_two_end_kernel,
        "layer_two_end",
        steps,
        [where, *wholes(flags_t, packs, send), border_rows(high), border_rows(rest), columns_of(total)]
        + wholes(came, came_oth, last_t),
        [
            ((units, half), BF16, block),
            ((units, half), F32, block),
            ((kinds, half), BF16, small),
            ((parts, bound, 128), BF16, None),
        ],
        border_scratch(units),
        flops=work // 4,
    )
    z_oth = swap(z_own)
    came = exchange(z_send)
    total = run(
        own_part_plain_kernel,
        "layer_three_own",
        steps,
        [where, *in_hbm, *wholes(z_own, z_oth)],
        [((kinds, half), F32, small)],
        [pltpu.VMEM((kinds, nodes), BF16), pltpu.VMEM((kinds, nodes), F8), scalar, *row_ring],
        flops=work,
    )[0]
    came, total = late(came, total)
    came_oth = swap(came)
    sums_out, grads, grads8, back, border_grad = run(
        functools.partial(loss_kernel, classes),
        "loss",
        steps,
        [where, whole(flags_t), border_rows(high), border_rows(rest), columns_of(total)]
        + wholes(came, came_oth, cache_out.T, bias_out, label_rows, mask_rows),
        [
            ((64, 128), F32, None),
            ((2 * kinds, half), BF16, node_block(ROWS, 2 * kinds)),
            ((kinds, half), F8, small),
            ((8, 128), F32, None),
            ((parts, bound, 128), F32, None),
        ],
        border_scratch(kinds) + [pltpu.VMEM((128, halo), F32)],
        flops=work // 4,
    )
    ret = exchange(border_grad)
    far, near = [
        run(
            functools.partial(back_three_kernel, other),
            "back_three",
            steps,
            [where, *in_hbm, *wholes(grads, grads8, back)],
            [((kinds, half), F32, small)],
            ring_scratch((half, ROWS), (BF16, F8)),
            flops=work // 2,
        )[0]
        for other in (True, False)
    ]
    far = swap(far)
    ret, near = late(ret, near)
    ret_oth = swap(ret)
    all_borders = [border_rows(high), border_rows(rest), border_rows(high8)]
    in_hbm3 = [*in_hbm, (high8, HBM)]
    chunk = 64 // parts

    def upstream_outs(extra):
        return [
            ((units, 128), F32, None),
            ((units, half), BF16, block),
            ((units, half), F8, block),
            ((units, half), F8, block),
            ((8, 128), F32, None),
            ((parts, bound + extra, units), F32, None),
        ]

    def end_scratch(n):
        return [pltpu.VMEM((units, halo), F32), pltpu.VMEM((n, halo), BF16), pltpu.VMEM((n, halo), BF16)]

    sums_two, grads, grads8, tails8, back, border_grad = run(
        end_three_kernel,
        "end_three",
        steps,
        [where, whole(flags_t), *all_borders, columns_of(near), columns_of(far)]
        + [*wholes(ret, ret_oth, send), columns_of(hidden_two), columns_of(slope_two), whole(last_pad)],
        upstream_outs(chunk),
        end_scratch(kinds) + [pltpu.VMEM((64, units), F32)],
        flops=work // 4,
    )
    ret = exchange(border_grad)

    def back_pair(halves):
        return [
            run(
                functools.partial(back_kernel, other, halves),
                "back",
                steps // halves,
                [where, *in_hbm3, *wholes(grads, grads8, tails8, back)],
                [((units, half // halves), F32, block)],
                ring_scratch((half, ROWS), (BF16, F8, F8)),
                flops=work // 2,
            )[0]
            for other in (True, False)
        ]

    far, near = back_pair(1)
    far = swap(far)
    ret, near = late(ret, near)
    ret_oth = swap(ret)
    sums_one, grads, grads8, tails8, back, border_grad, last_chunk = run(
        end_two_kernel,
        "end_two",
        steps,
        [where, *wholes(flags_t, packs), *all_borders, columns_of(near), columns_of(far)]
        + [*wholes(ret, ret_oth, send), columns_of(hidden_one), columns_of(slope_one)],
        [*upstream_outs(2 * chunk), ((chunk, units), F32, None)],
        end_scratch(units) + [pltpu.VMEM((units, units), F32)],
        flops=work // 4,
    )
    ret = exchange(border_grad)
    far, near = back_pair(2)
    far = swap(far)
    ret, near = late(ret, near)
    ret_oth = swap(ret)
    *pieces, second_chunk = run(
        end_one_kernel,
        "end_one",
        steps // 2,
        [where, columns_of(near), columns_of(far), *wholes(ret, ret_oth, send, feat_t, sums_one, sums_two, sums_out)],
        [((64, 128), F32, None)] * 4 + [((chunk, units), F32, None)],
        end_scratch(units)[1:] + [pltpu.VMEM((units, 128), F32)],
        flops=work // 8,
    )
    pieces = [piece if k == 0 else swap(piece, k) for k, piece in enumerate(pieces)]
    gathered = run(
        gather_kernel,
        "gather",
        1,
        wholes(*pieces, second_chunk, last_chunk),
        [((parts, 64 + 4 * chunk, 128), F32, None)],
    )[0]
    came = exchange(gathered)

    turn = lambda x: x.T
    same = lambda x: x
    row = lambda x: x.reshape(1, -1)
    forms = (turn, turn, turn, same, row)
    weights = (first_weight, second_weight, last_weight, hidden_bias, out_bias)
    moments = (moment_first, moment_second, moment_last, moment_hidden, moment_out)
    squares = (square_first, square_second, square_last, square_hidden, square_out)
    params = [form(x) for form, triple in zip(forms, zip(weights, moments, squares)) for x in triple]
    outs = run(
        update_kernel,
        "update",
        1,
        wholes(came, flags_t, *params),
        [(p.shape, F32, None) for p in params] + [((1, 128), F32, None)] * 2,
    )
    undo = (turn, turn, turn, same, lambda x: x.reshape(-1))
    results = [undo[k // 3](x) for k, x in enumerate(outs[0:15])]
    return (outs[15][0, 0], outs[16][0, 0], *results)


def solution(mesh):
    placed = (
        P("dom", None),
        P("dom"),
        P("dom"),
        P("dom", None),
        P("dom", None),
        P("dom", None, None),
        P(None, "dom"),
        P(None, "dom", "rep"),
        P("dom", None),
        P(None, "rep"),
        P(None, "rep"),
        P(),
        P(None, "rep"),
        P(),
        P(None, "rep"),
        P(None, "rep"),
        P(),
        P(None, "rep"),
        P(),
        P(None, "rep"),
        P(None, "rep"),
        P(),
        P(None, "rep"),
        P(),
    )
    return jax.shard_map(
        functools.partial(body, mesh.shape["dom"], mesh.shape["rep"]),
        mesh=mesh,
        in_specs=placed,
        out_specs=(P(), P()) + (P(None, "rep"),) * 6 + (P(),) * 3 + (P(None, "rep"),) * 3 + (P(),) * 3,
        check_vma=False,
    )
```

time: 2210 us -> 288 us (0.13)
  other arithmetic: 1260 us -> 0.07 us
  local copies, waits for them, and re-layouts: 735 us -> 75.8 us
  Pallas kernels: 0 us -> 133 us
  waiting for transfers between devices: 69.8 us -> 9.15 us
  blocking collectives: 80.1 us -> 25.3 us
    scatter-add x6 -> x0, other arithmetic: 1050 us -> none  [the longest x3 1040 us: spread_back(): jnp.zeros((table_rows, breadth), jnp.float32).at[edge_src.reshape(-1)]]
    gather x6 -> x0, local copies, waits for them, and re-layouts: 686 us -> none  [the longest x3 682 us: aggregate(): picked = lookup[edge_src].astype(jnp.float32)]
    reduce_sum x7 -> x0, other arithmetic: 143 us -> none  [the longest x3 141 us: aggregate(): return jnp.sum(picked * edge_norm[:, :, None], axis=1)]
    pallas_call x0 -> x18, Pallas kernels: none -> 133 us  [run(): pl.pallas_call(kernel, grid=(grid,), in_specs=[spec for _, spec in args],...]
    unnamed x98 -> x155, local copies, waits for them, and re-layouts: 11.4 us -> 72.9 us
    psum x2 -> x0, blocking collectives: 53.6 us -> none  [body(): lax.psum((jnp.sum(row_loss * masked), jnp.sum(masked)), 'dom')]
    all_gather x3 -> x0, waiting for transfers between devices: 46.9 us -> none  [the longest x2 37.2 us: widen(): return lax.all_gather(hidden_part, 'rep', axis=1, tiled=True)]
    mul x6 -> x0, other arithmetic: 37.4 us -> none  [the longest x3 35.6 us: spread_back(): terms = (edge_norm[:, :, None] * upstream[:, None, :]).reshape(-1, breadth)]
  transfers between devices with their start and end apart: 10 -> 19, of which waited for: 8 -> 7; matrix products, arithmetic and copies ran while one was open for 18% -> 1% of each run, Pallas kernels for 0% -> 24%
where the time goes in v1:
time: 288 us; the launch traced here: 286 us
  Pallas kernels  133 us (46%)
  local copies, waits for them, and re-layouts  75.8 us (26%)
  starting transfers between devices  41.1 us (14%)
  blocking collectives  25.3 us (9%)
  waiting for transfers between devices  9.15 us (3%)
    pallas_call x18, Pallas kernels, run(): pl.pallas_call(kernel, grid=(grid,), in_specs=[spec for _, spec in args],...  133 us
    unnamed x155, local copies, waits for them, and re-layouts  72.9 us
    all_to_all x6, starting transfers between devices, exchange(): return lax.all_to_all(x, 'dom', split_axis=0, concat_axis=0, tiled=True)  37.2 us
    all_to_all x1, blocking collectives, exchange(): return lax.all_to_all(x, 'dom', split_axis=0, concat_axis=0, tiled=True)  18.1 us
    ppermute x13, waiting for transfers between devices, swap(): return lax.ppermute(x, 'rep', [(i, i ^ k) for i in range(reps)])  9.13 us
    all_gather x1, blocking collectives, body(): packs = lax.all_gather(pack, 'rep', axis=0, tiled=True)  7.18 us
  transfers between devices with their start and end apart: 19, of which 7 were waited for; matrix products, arithmetic and copies ran while one was open for 1% of the time, Pallas kernels for 24%

profile of v1, /device:TPU:0, one launch (start us, length us, event | category | flops | bytes accessed | tf_op | source)
XLA Modules:
  0.0 285.8 jit_solution(5461277929722341339)
XLA Ops:
  10.8 7.3 %all-to-all-start = ((bf16[8,32,128]{2,1,0:T(8,128)(2,1)}), bf16[8,32,128]{2,1,0:T(8,128)(2,1)S(1)}, u32[]{:S(2)}, u32[]{:S(2)}) async-start(bf16[8,32,128]{2,1,0:T(8,128)(2,1)} %get-tuple-element.82), calls=%async_computation | async-start | bytes 131072 | tf_op jit(solution)/shard_map/all_to_all | solution.py:666
  20.0 20.0 %build.1 = (bf16[2048,4352]{1,0:T(8,128)(2,1)}, f8e4m3fn[2048,4352]{1,0:T(32,128)(4,1)S(1)}) custom-call(s32[2]{0:T(128)S(1)} %pad_add_fusion.place, s32[16,4096]{1,0:T(8,128)S(1)} %bitcast.61, f32[16,4096]{1,0:T(8,128)S(1)} %bitcast.62), custom_call_target="tpu_custom_call" | custom-call | flops 9126805504 | bytes 1048576 | tf_op jit(solution)/shard_map/build/pallas_call | solution.py:43
  43.6 7.2 %all_gather.3.packs = bf16[256,1024]{1,0:T(8,128)(2,1)S(1)} all-gather(bf16[64,1024]{1,0:T(8,128)(2,1)S(1)} %get-tuple-element.83), channel_id=1, replica_groups=mesh['dom'=8,'rep'=4] {'rep'}, dimensions={0}, use_global_device_ids=true | all-gather | bytes 655360 | tf_op jit(solution)/shard_map/all_gather | solution.py:691
  50.8 3.6 %copy-done.1 = f8e4m3fn[2048,4352]{1,0:T(32,128)(4,1)S(1)} copy-done((f8e4m3fn[2048,4352]{1,0:T(32,128)(4,1)S(1)}, f8e4m3fn[2048,4352]{1,0:T(32,128)(4,1)}, u32[]{:S(2)}) %copy-start.1) | copy-done | bytes 8912920
  54.4 17.7 %layer_one.1 = (bf16[256,2048]{1,0:T(8,128)(2,1)S(1)}, f32[256,2048]{1,0:T(8,128)S(1)}, bf16[256,2048]{1,0:T(8,128)(2,1)S(1)}, bf16[8,32,256]{2,1,0:T(8,128)(2,1)}, f32[8,256]{1,0:T(8,128)S(1)}) custom-call(s32[2]{0:T(128)S(1)} %pad_add_fusion.place, bf16[8,32,128]{2,1,0:T(8,128)(2,1)S(1)} %all-to-all-done.rows, bf16[100,4096]{1,0:T(8,128)(2,1)S(1)} %bitcast.41, ...), custom_call_target="tpu_custom_call" | custom-call | flops 4563402752 | bytes 1048576 | tf_op jit(solution)/shard_map/layer_one/pallas_call | solution.py:43
  74.7 6.0 %all-to-all-start.1 = ((bf16[8,32,256]{2,1,0:T(8,128)(2,1)}), bf16[8,32,256]{2,1,0:T(8,128)(2,1)S(1)}, u32[]{:S(2)}, u32[]{:S(2)}) async-start(bf16[8,32,256]{2,1,0:T(8,128)(2,1)} %get-tuple-element.89), calls=%async_computation.1 | async-start | bytes 262144 | tf_op jit(solution)/shard_map/all_to_all | solution.py:666
  80.7 13.6 %layer_two_own.1 = (f32[256,2048]{1,0:T(8,128)S(1)}, f8e4m3fn[2048,4352]{1,0:T(32,128)(4,1)S(1)}) custom-call(s32[2]{0:T(128)S(1)} %pad_add_fusion.place, bf16[2048,4352]{1,0:T(8,128)(2,1)} %get-tuple-element.84.high, f8e4m3fn[2048,4352]{1,0:T(32,128)(4,1)} %copy-done, bf16[256,2048]{1,0:T(8,128)(2,1)S(1)} %get-tuple-element.87.z_own, ...), custom_call_target="tpu_custom_call" | custom-call | flops 4563402752 | bytes 1048576 | tf_op jit(solution)/shard_map/layer_two_own/pallas_call | solution.py:43
  100.4 3.6 %copy-done.2 = f8e4m3fn[2048,4352]{1,0:T(32,128)(4,1)S(1)} copy-done((f8e4m3fn[2048,4352]{1,0:T(32,128)(4,1)S(1)}, f8e4m3fn[2048,4352]{1,0:T(32,128)(4,1)}, u32[]{:S(2)}) %copy-start.2) | copy-done | bytes 8912920
  105.6 5.9 %layer_two_end.1 = (bf16[256,2048]{1,0:T(8,128)(2,1)S(1)}, f32[256,2048]{1,0:T(8,128)S(1)}, bf16[48,2048]{1,0:T(8,128)(2,1)S(1)}, bf16[8,32,128]{2,1,0:T(8,128)(2,1)}) custom-call(s32[2]{0:T(128)S(1)} %pad_add_fusion.place, f32[8,256]{1,0:T(8,128)S(1)} %get-tuple-element.86.flags_t, bf16[256,1024]{1,0:T(8,128)(2,1)S(1)} %all_gather.3.packs, ...), custom_call_target="tpu_custom_call" | custom-call | flops 1140850688 | bytes 1048576 | tf_op jit(solution)/shard_map/layer_two_end/pallas_call | solution.py:43
  114.2 6.0 %all-to-all-start.2 = ((bf16[8,32,128]{2,1,0:T(8,128)(2,1)}), bf16[8,32,128]{2,1,0:T(8,128)(2,1)S(1)}, u32[]{:S(2)}, u32[]{:S(2)}) async-start(bf16[8,32,128]{2,1,0:T(8,128)(2,1)} %get-tuple-element.93), calls=%async_computation.2 | async-start | bytes 131072 | tf_op jit(solution)/shard_map/all_to_all | solution.py:666
  123.8 11.1 %layer_three_own.1.total = f32[48,2048]{1,0:T(8,128)S(1)} custom-call(s32[2]{0:T(128)S(1)} %pad_add_fusion.place, bf16[2048,4352]{1,0:T(8,128)(2,1)} %get-tuple-element.84.high, f8e4m3fn[2048,4352]{1,0:T(32,128)(4,1)S(1)} %copy-done.3, bf16[48,2048]{1,0:T(8,128)(2,1)S(1)} %get-tuple-element.94.z_own, bf16[48,2048]{1,0:T(8,128)(2,1)S(1)} %collective-permute-done.2.z_oth), custom_call_target="tpu_custom_call" | custom-call | flops 4563402752 | bytes 1048576 | tf_op jit(solution)/shard_map/layer_three_own/pallas_call | solution.py:43
  143.5 3.9 %loss.1 = (f32[64,128]{1,0:T(8,128)S(1)}, bf16[96,2048]{1,0:T(8,128)(2,1)S(1)}, f8e4m3fn[48,2048]{1,0:T(8,128)(4,1)S(1)}, f32[8,128]{1,0:T(8,128)S(1)}, f32[8,32,128]{2,1,0:T(8,128)S(1)}) custom-call(s32[2]{0:T(128)S(1)} %pad_add_fusion.place, f32[8,256]{1,0:T(8,128)S(1)} %get-tuple-element.86.flags_t, bf16[2048,4352]{1,0:T(8,128)(2,1)} %get-tuple-element.84.high, ...), custom_call_target="tpu_custom_call" | custom-call | flops 1140850688 | bytes 1048576 | tf_op jit(solution)/shard_map/loss/pallas_call | solution.py:43
  147.4 6.3 %back_three.3 = f32[48,2048]{1,0:T(8,128)} custom-call(s32[2]{0:T(128)S(1)} %pad_add_fusion.place, bf16[2048,4352]{1,0:T(8,128)(2,1)} %get-tuple-element.84.high, f8e4m3fn[2048,4352]{1,0:T(32,128)(4,1)S(1)} %copy-done.4, bf16[96,2048]{1,0:T(8,128)(2,1)S(1)} %get-tuple-element.98.grads, f8e4m3fn[48,2048]{1,0:T(8,128)(4,1)S(1)} %get-tuple-element.99.grads8, ...), custom_call_target="tpu_custom_call" | custom-call | flops 2281701376 | bytes 1048576 | tf_op jit(solution)/shard_map/back_three/pallas_call | solution.py:43
  153.9 6.0 %all-to-all-start.3 = ((f32[8,32,128]{2,1,0:T(8,128)}), f32[8,32,128]{2,1,0:T(8,128)S(1)}, u32[]{:S(2)}, u32[]{:S(2)}) async-start(f32[8,32,128]{2,1,0:T(8,128)} %copy-done.46), calls=%async_computation.3 | async-start | bytes 262144 | tf_op jit(solution)/shard_map/all_to_all | solution.py:666
  164.4 5.6 %back_three.2.own = f32[48,2048]{1,0:T(8,128)S(1)} custom-call(s32[2]{0:T(128)S(1)} %pad_add_fusion.place, bf16[2048,4352]{1,0:T(8,128)(2,1)} %get-tuple-element.84.high, f8e4m3fn[2048,4352]{1,0:T(32,128)(4,1)S(1)} %copy-done.5, bf16[96,2048]{1,0:T(8,128)(2,1)S(1)} %get-tuple-element.98.grads, f8e4m3fn[48,2048]{1,0:T(8,128)(4,1)S(1)} %copy-done.36, ...), custom_call_target="tpu_custom_call" | custom-call | flops 2281701376 | bytes 1048576 | tf_op jit(solution)/shard_map/back_three/pallas_call | solution.py:43
  176.7 6.3 %end_three.1 = (f32[256,128]{1,0:T(8,128)S(1)}, bf16[256,2048]{1,0:T(8,128)(2,1)S(1)}, f8e4m3fn[256,2048]{1,0:T(32,128)(4,1)S(1)}, f8e4m3fn[256,2048]{1,0:T(32,1...) custom-call(s32[2]{0:T(128)S(1)} %pad_add_fusion.place, f32[8,256]{1,0:T(8,128)S(1)} %get-tuple-element.86.flags_t, ...), custom_call_target="tpu_custom_call" | custom-call | flops 1140850688 | bytes 1048576 | tf_op jit(solution)/shard_map/end_three/pallas_call | solution.py:43
  183.0 9.8 %back.5 = f32[256,2048]{1,0:T(8,128)} custom-call(s32[2]{0:T(128)S(1)} %pad_add_fusion.place, bf16[2048,4352]{1,0:T(8,128)(2,1)} %get-tuple-element.84.high, f8e4m3fn[2048,4352]{1,0:T(32,128)(4,1)S(1)} %copy-done.6, f8e4m3fn[2048,4352]{1,0:T(32,128)(4,1)} %copy-done.9, bf16[256,2048]{1,0:T(8,128)(2,1)S(1)} %get-tuple-element.106.grads, ...), custom_call_target="tpu_custom_call" | custom-call | flops 2281701376 | bytes 1048576 | tf_op jit(solution)/shard_map/back/pallas_call | solution.py:43
  193.0 6.0 %all-to-all-start.4 = ((f32[8,40,256]{2,1,0:T(8,128)}), f32[8,40,256]{2,1,0:T(8,128)}, u32[]{:S(2)}, u32[]{:S(2)}) async-start(f32[8,40,256]{2,1,0:T(8,128)} %get-tuple-element.105), calls=%async_computation.4 | async-start | bytes 655360 | tf_op jit(solution)/shard_map/all_to_all | solution.py:666
  205.9 8.6 %back.4.own = f32[256,2048]{1,0:T(8,128)S(1)} custom-call(s32[2]{0:T(128)S(1)} %pad_add_fusion.place, bf16[2048,4352]{1,0:T(8,128)(2,1)} %get-tuple-element.84.high, f8e4m3fn[2048,4352]{1,0:T(32,128)(4,1)S(1)} %copy-done.7, f8e4m3fn[2048,4352]{1,0:T(32,128)(4,1)} %copy-done.9, bf16[256,2048]{1,0:T(8,128)(2,1)S(1)} %copy-done.18, ...), custom_call_target="tpu_custom_call" | custom-call | flops 2281701376 | bytes 1048576 | tf_op jit(solution)/shard_map/back/pallas_call | solution.py:43
  220.2 6.5 %end_two.1 = (f32[256,128]{1,0:T(8,128)S(1)}, bf16[256,2048]{1,0:T(8,128)(2,1)S(1)}, f8e4m3fn[256,2048]{1,0:T(32,128)(4,1)S(1)}, f8e4m3fn[256,2048]{1,0:T(32,128...) custom-call(s32[2]{0:T(128)S(1)} %pad_add_fusion.place, ...), custom_call_target="tpu_custom_call" | custom-call | flops 1140850688 | bytes 1048576 | tf_op jit(solution)/shard_map/end_two/pallas_call | solution.py:43
  230.7 6.0 %all-to-all-start.5 = ((f32[8,48,256]{2,1,0:T(8,128)}), f32[8,48,256]{2,1,0:T(8,128)S(1)}, u32[]{:S(2)}, u32[]{:S(2)}) async-start(f32[8,48,256]{2,1,0:T(8,128)} %copy-done.37), calls=%async_computation.5 | async-start | bytes 786432 | tf_op jit(solution)/shard_map/all_to_all | solution.py:666
  243.6 5.4 %back.7 = f32[256,1024]{1,0:T(8,128)S(1)} custom-call(s32[2]{0:T(128)S(1)} %pad_add_fusion.place, bf16[2048,4352]{1,0:T(8,128)(2,1)} %get-tuple-element.84.high, f8e4m3fn[2048,4352]{1,0:T(32,128)(4,1)S(1)} %copy-done.8, f8e4m3fn[2048,4352]{1,0:T(32,128)(4,1)} %copy-done.9, bf16[256,2048]{1,0:T(8,128)(2,1)S(1)} %copy-done.16, ...), custom_call_target="tpu_custom_call" | custom-call | flops 2281701376 | bytes 1048576 | tf_op jit(solution)/shard_map/back/pallas_call | solution.py:43
  249.0 5.4 %back.6.own = f32[256,1024]{1,0:T(8,128)S(1)} custom-call(s32[2]{0:T(128)S(1)} %pad_add_fusion.place, bf16[2048,4352]{1,0:T(8,128)(2,1)} %get-tuple-element.84.high, f8e4m3fn[2048,4352]{1,0:T(32,128)(4,1)S(1)} %copy-done.8, f8e4m3fn[2048,4352]{1,0:T(32,128)(4,1)} %copy-done.9, bf16[256,2048]{1,0:T(8,128)(2,1)S(1)} %copy-done.16, ...), custom_call_target="tpu_custom_call" | custom-call | flops 2281701376 | bytes 1048576 | tf_op jit(solution)/shard_map/back/pallas_call | solution.py:43
  266.5 18.1 %all_to_all.35.came = f32[8,96,128]{2,1,0:T(8,128)S(1)} all-to-all(f32[8,96,128]{2,1,0:T(8,128)S(1)} %gather.1), channel_id=1, replica_groups=mesh['dom'=8,'rep'=4] {'dom'}, dimensions={0} | all-to-all | bytes 786432 | tf_op jit(solution)/shard_map/all_to_all | solution.py:666
  (197 shorter events, 88.7 us)
Async XLA Ops:
  2.2 169.3 %copy-start.12 = (s32[256,1]{1,0:T(8,128)}, s32[256,1]{1,0:T(8,128)S(1)}, u32[]{:S(2)}) copy-start(s32[256,1]{1,0:T(8,128)S(1)} %reshape.78.send) | copy-start | bytes 3076
  10.8 40.0 %all-to-all-start = ((bf16[8,32,128]{2,1,0:T(8,128)(2,1)}), bf16[8,32,128]{2,1,0:T(8,128)(2,1)S(1)}, u32[]{:S(2)}, u32[]{:S(2)}) async-start(bf16[8,32,128]{2,1,0:T(8,128)(2,1)} %get-tuple-element.82), calls=%async_computation | async-start | bytes 131072 | tf_op jit(solution)/shard_map/all_to_all | solution.py:666
  20.0 30.7 %copy-start.11 = (bf16[4096,100]{0,1:T(8,128)(2,1)S(1)}, bf16[4096,100]{0,1:T(8,128)(2,1)}, u32[]{:S(2)}) copy-start(bf16[4096,100]{0,1:T(8,128)(2,1)} %param.24) | copy-start | bytes 2457604
  74.3 6.4 %collective-permute-start = (bf16[256,2048]{1,0:T(8,128)(2,1)S(1)}, bf16[256,2048]{1,0:T(8,128)(2,1)}, u32[]{:S(2)}, u32[]{:S(2)}) collective-permute-start(bf16[256,2048]{1,0:T(8,128)(2,1)S(1)} %get-tuple-element.87.z_own), channel_id=1, source_target_pairs={{0,1},{1,0},{2,3},{3,2},{4,5},{5,4},{6,7},{7,6},{8,9},{9,8},{10,11... | collective-permute-start | bytes 3145736 | tf_op jit(solution)/shard_map/ppermute | solution.py:663
  74.7 24.4 %all-to-all-start.1 = ((bf16[8,32,256]{2,1,0:T(8,128)(2,1)}), bf16[8,32,256]{2,1,0:T(8,128)(2,1)S(1)}, u32[]{:S(2)}, u32[]{:S(2)}) async-start(bf16[8,32,256]{2,1,0:T(8,128)(2,1)} %get-tuple-element.89), calls=%async_computation.1 | async-start | bytes 262144 | tf_op jit(solution)/shard_map/all_to_all | solution.py:666
  99.1 1.3 collective-permute-start.1
  112.8 7.4 %collective-permute-start.2 = (bf16[48,2048]{1,0:T(8,128)(2,1)S(1)}, bf16[48,2048]{1,0:T(8,128)(2,1)S(1)}, u32[]{:S(2)}, u32[]{:S(2)}) collective-permute-start(bf16[48,2048]{1,0:T(8,128)(2,1)S(1)} %get-tuple-element.94.z_own), channel_id=1, source_target_pairs={{0,1},{1,0},{2,3},{3,2},{4,5},{5,4},{6,7},{7,6},{8,9},{9,8},{10,11... | collective-permute-start | bytes 589832 | tf_op jit(solution)/shard_map/ppermute | solution.py:663
  114.2 20.7 %all-to-all-start.2 = ((bf16[8,32,128]{2,1,0:T(8,128)(2,1)}), bf16[8,32,128]{2,1,0:T(8,128)(2,1)S(1)}, u32[]{:S(2)}, u32[]{:S(2)}) async-start(bf16[8,32,128]{2,1,0:T(8,128)(2,1)} %get-tuple-element.93), calls=%async_computation.2 | async-start | bytes 131072 | tf_op jit(solution)/shard_map/all_to_all | solution.py:666
  134.9 1.3 collective-permute-start.3
  153.7 17.8 %collective-permute-start.4 = (f32[48,2048]{1,0:T(8,128)}, f32[48,2048]{1,0:T(8,128)}, u32[]{:S(2)}, u32[]{:S(2)}) collective-permute-start(f32[48,2048]{1,0:T(8,128)} %back_three.3), channel_id=1, source_target_pairs={{0,1},{1,0},{2,3},{3,2},{4,5},{5,4},{6,7},{7,6},{8,9},{9,8},{10,11... | collective-permute-start | bytes 1179656 | tf_op jit(solution)/shard_map/ppermute | solution.py:663
  153.9 16.1 %all-to-all-start.3 = ((f32[8,32,128]{2,1,0:T(8,128)}), f32[8,32,128]{2,1,0:T(8,128)S(1)}, u32[]{:S(2)}, u32[]{:S(2)}) async-start(f32[8,32,128]{2,1,0:T(8,128)} %copy-done.46), calls=%async_computation.3 | async-start | bytes 262144 | tf_op jit(solution)/shard_map/all_to_all | solution.py:666
  170.1 1.4 collective-permute-start.5
  192.8 23.6 %collective-permute-start.6 = (f32[256,2048]{1,0:T(8,128)}, f32[256,2048]{1,0:T(8,128)}, u32[]{:S(2)}, u32[]{:S(2)}) collective-permute-start(f32[256,2048]{1,0:T(8,128)} %back.5), channel_id=1, source_target_pairs={{0,1},{1,0},{2,3},{3,2},{4,5},{5,4},{6,7},{7,6},{8,9},{9,8},{10,11... | collective-permute-start | bytes 6291464 | tf_op jit(solution)/shard_map/ppermute | solution.py:663
  193.0 21.5 %all-to-all-start.4 = ((f32[8,40,256]{2,1,0:T(8,128)}), f32[8,40,256]{2,1,0:T(8,128)}, u32[]{:S(2)}, u32[]{:S(2)}) async-start(f32[8,40,256]{2,1,0:T(8,128)} %get-tuple-element.105), calls=%async_computation.4 | async-start | bytes 655360 | tf_op jit(solution)/shard_map/all_to_all | solution.py:666
  214.6 1.9 collective-permute-start.7
  230.7 23.8 %all-to-all-start.5 = ((f32[8,48,256]{2,1,0:T(8,128)}), f32[8,48,256]{2,1,0:T(8,128)S(1)}, u32[]{:S(2)}, u32[]{:S(2)}) async-start(f32[8,48,256]{2,1,0:T(8,128)} %copy-done.37), calls=%async_computation.5 | async-start | bytes 786432 | tf_op jit(solution)/shard_map/all_to_all | solution.py:666
  249.0 6.0 %collective-permute-start.8 = (f32[256,1024]{1,0:T(8,128)S(1)}, f32[256,1024]{1,0:T(8,128)}, u32[]{:S(2)}, u32[]{:S(2)}) collective-permute-start(f32[256,1024]{1,0:T(8,128)S(1)} %back.7), channel_id=1, source_target_pairs={{0,1},{1,0},{2,3},{3,2},{4,5},{5,4},{6,7},{7,6},{8,9},{9,8},{10,11... | collective-permute-start | bytes 3145736 | tf_op jit(solution)/shard_map/ppermute | solution.py:663
  254.4 1.9 collective-permute-start.9
  258.9 25.7 %copy-start.56 = (f32[256,64]{0,1:T(8,128)S(1)}, f32[256,64]{0,1:T(8,128)}, u32[]{:S(2)}) copy-start(f32[256,64]{0,1:T(8,128)} %param.44) | copy-start | bytes 196612
  258.9 25.7 %copy-start.58 = (f32[256,47]{0,1:T(8,128)S(1)}, f32[256,47]{0,1:T(8,128)}, u32[]{:S(2)}) copy-start(f32[256,47]{0,1:T(8,128)} %param.40) | copy-start | bytes 144388
  258.9 25.7 %copy-start.59 = (f32[256,47]{0,1:T(8,128)S(1)}, f32[256,47]{0,1:T(8,128)}, u32[]{:S(2)}) copy-start(f32[256,47]{0,1:T(8,128)} %param.45) | copy-start | bytes 144388
  261.5 1.9 collective-permute-start.10
  261.9 4.0 %collective-permute-start.11 = (f32[64,128]{1,0:T(8,128)S(1)}, f32[64,128]{1,0:T(8,128)S(1)}, u32[]{:S(2)}, u32[]{:S(2)}) collective-permute-start(f32[64,128]{1,0:T(8,128)S(1)} %get-tuple-element.126), channel_id=1, source_target_pairs={{0,2},{1,3},{2,0},{3,1},{4,6},{5,7},{6,4},{7,5},{8,10},{9,11},{10,... | collective-permute-start | bytes 98312 | tf_op jit(solution)/shard_map/ppermute | solution.py:663
  262.7 3.7 %collective-permute-start.12 = (f32[64,128]{1,0:T(8,128)S(1)}, f32[64,128]{1,0:T(8,128)S(1)}, u32[]{:S(2)}, u32[]{:S(2)}) collective-permute-start(f32[64,128]{1,0:T(8,128)S(1)} %get-tuple-element.127), channel_id=1, source_target_pairs={{0,3},{1,2},{2,1},{3,0},{4,7},{5,6},{6,5},{7,4},{8,11},{9,10},{10,... | collective-permute-start | bytes 98312 | tf_op jit(solution)/shard_map/ppermute | solution.py:663
  (72 other events, 497.1 us)

commit v2 on v1

v2 whole, which is shorter than its diff:
```python
import functools

import jax
import jax.numpy as jnp
from jax import lax
from jax.experimental import pallas as pl
from jax.experimental.pallas import tpu as pltpu
from jax.sharding import PartitionSpec as P

STEP = 5
beta_one = 0.5
beta_two = 0.5
rate_step = 0.03
decay_rate = 0.01
epsilon = 1e-08

BF16, F32, F8, I32 = jnp.bfloat16, jnp.float32, jnp.float8_e4m3fn, jnp.int32
REST_GAIN = 4096.0
TAIL_GAIN = 256.0
FLAG_LANE = 100
ROWS = 512
FINE = 256
AHEAD = 3
LIMIT = 52 << 20

SMEM = pl.BlockSpec(memory_space=pltpu.SMEM)
VMEM = pl.BlockSpec(memory_space=pltpu.VMEM)
OWN = pl.BlockSpec(memory_space=pltpu.VMEM)
HBM = pl.BlockSpec(memory_space=pltpu.HBM)
ANY = pl.BlockSpec(memory_space=pl.ANY)


def whole_spec(shape):
    return pl.BlockSpec(shape, lambda *_: (0,) * len(shape))


def placed(spec, *arrays):
    return [(a, spec) for a in arrays]


def run(kernel, name, args, outs, scratch=(), flops=0, grid=()):
    pinned = [
        a if any(spec is s for s in (SMEM, VMEM, ANY)) else pltpu.with_memory_space_constraint(a, pltpu.HBM)
        for a, spec in args
    ]
    return pl.pallas_call(
        kernel,
        grid=grid,
        in_specs=[spec for _, spec in args],
        out_specs=[spec for _, _, spec in outs],
        out_shape=[
            jax.ShapeDtypeStruct(shape, kind) if spec is VMEM else pltpu.HBM(shape, kind)
            for shape, kind, spec in outs
        ],
        scratch_shapes=list(scratch),
        name=name,
        cost_estimate=pl.CostEstimate(flops=flops, bytes_accessed=1 << 20, transcendentals=0),
        compiler_params=pltpu.CompilerParams(vmem_limit_bytes=LIMIT),
    )(*pinned)


def dot_nn(left, right):
    return lax.dot_general(left, right, (((1,), (0,)), ((), ())), preferred_element_type=F32)


def dot_nt(left, right):
    return lax.dot_general(left, right, (((1,), (1,)), ((), ())), preferred_element_type=F32)


def dot_tn(left, right):
    return lax.dot_general(left, right, (((0,), (0,)), ((), ())), preferred_element_type=F32)


def scale_of(value):
    most = jnp.maximum(jnp.max(jnp.abs(value)), 1e-30)
    return 256.0 / most, most * (1.0 / 256.0)


def span(start, size):
    return pl.ds(pl.multiple_of(start, size), size)


def rows_at(size, cols=slice(None)):
    return lambda i: (span(i * size, size), cols)


def cols_at(size, base=0):
    return lambda i: (slice(None), span(base + i * size, size))


def all_of(i):
    return (slice(None), slice(None))


def loop(count, step):
    def one(i, carry):
        step(i)
        return carry

    lax.fori_loop(0, count, one, 0)


class Ring:
    def __init__(self, refs, bufs, sems, cut, first=0):
        self.refs, self.bufs, self.sems, self.cut = refs, bufs, sems, cut
        self.begins = pl.program_id(0) == 0
        self.step, self.steps = pl.program_id(0) - first, pl.num_programs(0) - first
        self.depth = bufs[0].shape[0]
        self.slot = lax.rem(self.step, self.depth)

    def copies(self, step, slot):
        return [
            pltpu.make_async_copy(ref.at[self.cut(step)], buf.at[slot], self.sems.at[k, slot])
            for k, (ref, buf) in enumerate(zip(self.refs, self.bufs))
        ]

    def begin(self):
        for step in range(self.depth):

            @pl.when(self.begins & (step < self.steps))
            def _():
                for copy in self.copies(step, step):
                    copy.start()

    def wait(self):
        for copy in self.copies(self.step, self.slot):
            copy.wait()
        return [buf.at[self.slot] for buf in self.bufs]

    def end(self):
        @pl.when(self.step + self.depth < self.steps)
        def _():
            for copy in self.copies(self.step + self.depth, self.slot):
                copy.start()


def ring_scratch(shape, depth=3):
    kinds = (BF16, F8)
    return [pltpu.VMEM((depth, *shape), kind) for kind in kinds] + [pltpu.SemaphoreType.DMA((len(kinds), depth))]


class Stream:
    def __init__(self, sems, *legs):
        self.sems, self.legs = sems, legs

    def copies(self, i):
        return [
            pltpu.make_async_copy(source.at[source_at(i)], target.at[target_at(i)], self.sems.at[k, i])
            for k, (source, source_at, target, target_at) in enumerate(self.legs)
        ]

    def start(self, i):
        for copy in self.copies(i):
            copy.start()

    def wait(self, i):
        for copy in self.copies(i):
            copy.wait()

    def wait_all(self, count):
        loop(count, self.wait)

    def start_first(self, count):
        for i in range(min(AHEAD, count)):
            self.start(i)

    def next(self, i, count):
        self.wait(i)

        @pl.when(i + AHEAD < count)
        def _():
            self.start(i + AHEAD)


def sems(legs, count):
    return pltpu.SemaphoreType.DMA((legs, count))


def pick_rows(send, first, count):
    nodes = lax.broadcasted_iota(I32, (send.shape[0], count), 1) + first
    return jnp.where(send == nodes, 1.0, 0.0).astype(BF16)


def pack_kernel(feat_t, send_list, changed, mask, first_t, second_t, cache_t, bias, rows_out, pack_out, send):
    nodes, halo = feat_t.shape[1], send.shape[0]
    parts, bound = send_list.shape
    turned = send_list[...].astype(F32)
    turned = jnp.concatenate([turned, jnp.zeros((parts, 128 - bound), F32)], axis=1)
    turned = turned.T.astype(I32)
    for q in range(parts):
        send[q * bound : (q + 1) * bound, :] = turned[0:bound, q : q + 1]
    width, cols = feat_t.shape[0], first_t.shape[0]

    def pick(i, total):
        return total + dot_nt(pick_rows(send[...], i * ROWS, ROWS), feat_t[:, span(i * ROWS, ROWS)])

    total = lax.fori_loop(0, nodes // ROWS, pick, jnp.zeros((halo, width), F32))
    count = jnp.sum(mask[...].astype(F32))
    many = jnp.floor(count * (1.0 / 64.0))
    lane = lax.broadcasted_iota(I32, (halo, 128), 1)
    row = jnp.concatenate([total, jnp.zeros((halo, 128 - width), F32)], axis=1)
    for layer in range(3):
        row = jnp.where(lane == FLAG_LANE + layer, changed[0, layer].astype(F32), row)
    row = jnp.where(lane == FLAG_LANE + 3, many, row)
    row = jnp.where(lane == FLAG_LANE + 4, count - 64.0 * many, row)
    rows_out[...] = row.astype(BF16).reshape(rows_out.shape)

    units = second_t.shape[1]
    pack_out[:, 0:128] = jnp.concatenate(
        [first_t[...], jnp.zeros((cols, 128 - width), F32)], axis=1
    ).astype(BF16)
    pack_out[:, 128 : 128 + units] = second_t[...].astype(BF16)
    left = jnp.concatenate([bias[...], jnp.zeros((2, 128 - cols), F32)], axis=1)
    terms = []
    for _ in range(3):
        term = left.astype(BF16).astype(F32)
        terms.append(term)
        left = left - term
    terms = jnp.concatenate(terms + [jnp.zeros((122, 128), F32)], axis=0).T
    pack_out[:, 128 + units : 256 + units] = terms[0:cols, :].astype(BF16)
    base = 256 + units
    for layer in range(2):
        pack_out[:, base + layer * halo : base + (layer + 1) * halo] = cache_t[layer]


def bias_column(packs, layer):
    units = packs.shape[0]
    terms = packs[:, 128 + units : 256 + units].astype(F32)
    return terms[:, layer : layer + 1] + terms[:, layer + 2 : layer + 3] + terms[:, layer + 4 : layer + 5]


def stale_columns(packs, layer, halo):
    base = 256 + packs.shape[0] + layer * halo
    return packs[:, base : base + halo].astype(F32)


def build_kernel(place, src_t, norm_t, high_hbm, rest_hbm, high, rest, out_sems):
    slots = src_t.shape[0]
    half = src_t.shape[1] // 2
    blocks = high.shape[1] // 256
    per_group = 256 // slots
    in_slot = lax.broadcasted_iota(I32, (8, 128), 1) // per_group == lax.broadcasted_iota(I32, (8, 128), 0)
    node_row = lax.broadcasted_iota(I32, (per_group, 256), 0)
    mine = lax.rem(lax.broadcasted_iota(I32, (per_group, 256), 1), per_group) == node_row
    inner = lax.broadcasted_iota(I32, (256, 256), 0)
    stores = Stream(out_sems, (high, rows_at(128), high_hbm, rows_at(128)), (rest, rows_at(128), rest_hbm, rows_at(128)))

    def lean(tile):
        return [
            pltpu.roll(tile[first : first + 8, :], 0, 1, stride=per_group, stride_axis=0)
            for first in range(0, slots, 8)
        ]

    def flat(tiles, group):
        moved = [pltpu.roll(tile, (128 - per_group * group) % 128, 1) for tile in tiles]
        return jnp.concatenate(
            [jnp.sum(jnp.where(in_slot, tile, 0), axis=0, keepdims=True) for tile in moved], axis=1
        )

    def one(at, weight):
        weight_high = weight.astype(BF16).astype(F32)
        hit = inner == jnp.bitwise_and(at, 255)
        right = jnp.where(hit, weight_high, 0.0).astype(BF16)
        right_rest = jnp.where(hit, (weight - weight_high) * REST_GAIN, 0.0).astype(BF16)
        block = jnp.where(mine, jnp.right_shift(at, 8), -1)
        left = jnp.concatenate(
            [jnp.where(block == j, 1.0, 0.0).astype(BF16) for j in range(blocks)], axis=0
        )
        return dot_nt(left, right), dot_nt(left, right_rest)

    def step(i):
        here = span(place[0] * half + i * 128, 128)
        at, weight = src_t[:, here], norm_t[:, here]
        slot = lax.broadcasted_iota(I32, at.shape, 0)
        merged, repeat = weight, slot < 0
        for shift in range(1, slots):
            same = at == pltpu.roll(at, shift, 0)
            merged = merged + jnp.where(same, pltpu.roll(weight, shift, 0), 0.0)
            repeat = repeat | (same & (slot >= shift))
        source, weights = lean(at), lean(jnp.where(repeat, 0.0, merged))
        pairs = [one(flat(source, group), flat(weights, group)) for group in range(128 // per_group)]
        rows = span(i * 128, 128)
        for j in range(blocks):
            cols = slice(256 * j, 256 * (j + 1))
            for ref, parts in zip((high, rest), zip(*pairs)):
                piece = jnp.concatenate([p[per_group * j : per_group * (j + 1), :] for p in parts], axis=0)
                ref[rows, cols] = piece.astype(ref.dtype)
        stores.start(i)

    loop(half // 128, step)
    stores.wait_all(half // 128)


def gelu_both(u):
    square = u * u
    t = jnp.tanh(0.79788456 * (u + 0.044715 * u * square))
    half = 0.5 * (1.0 + t)
    slope = half + 0.5 * u * (1.0 - t * t) * (0.79788456 * (1.0 + 3.0 * 0.044715 * square))
    return u * half, slope


def layer_one_kernel(place, rows, feat_t, pack, pack_one, pack_two, pack_three, send, high, rest, packs, hidden_t, slope_t, z_own, z_send, flags_t, table, table8, back, hbuf, rbuf, sems):
    width, nodes = feat_t.shape
    halo = send.shape[0]
    step = pl.program_id(0)
    ring = Ring((high, rest), (hbuf, rbuf), sems, lambda i: (span(i * ROWS, ROWS), slice(None)))
    ring.begin()

    @pl.when(step == 0)
    def _():
        for k, ref in enumerate((pack, pack_one, pack_two, pack_three)):
            packs[span(jnp.bitwise_xor(place[0] + 2 * place[1], k) * 64, 64), :] = ref[...]
        weight = packs[:, 0:width]
        flat = rows[...].reshape(halo, 128)
        flags = flat.astype(F32).T[FLAG_LANE : FLAG_LANE + 8, :]
        counts = jnp.sum(rows[...].astype(F32)[:, 0, :], axis=0, keepdims=True)
        count = 64.0 * counts[:, FLAG_LANE + 3 : FLAG_LANE + 4] + counts[:, FLAG_LANE + 4 : FLAG_LANE + 5]
        row = lax.broadcasted_iota(I32, flags.shape, 0)
        flags_t[...] = jnp.where(row == 3, count, flags)

        def first(i, most):
            here = span(i * ROWS, ROWS)
            z = dot_nn(weight, feat_t[:, here])
            table[:, here] = z.astype(BF16)
            return jnp.maximum(most, jnp.abs(z))

        most = lax.fori_loop(0, nodes // ROWS, first, jnp.zeros((table.shape[0], ROWS), F32))
        border = dot_nt(weight, flat[:, 0:width]).astype(BF16).astype(F32)
        border = jnp.where(flags[0:1, :] == 1.0, border, stale_columns(packs, 0, halo))
        table[:, nodes : nodes + halo] = border.astype(BF16)
        scale, inverse = scale_of(jnp.maximum(jnp.max(most), jnp.max(jnp.abs(border))))
        back[0] = inverse * (1.0 / REST_GAIN)

        def small(i, carry):
            here = span(i * 256, 256)
            table8[:, here] = (table[:, here].astype(F32) * scale).astype(F8)
            return carry

        lax.fori_loop(0, (nodes + halo) // 256, small, 0)
        z_send[...] = jnp.zeros(z_send.shape, BF16)

    units = packs.shape[0]
    top, low = ring.wait()
    total = dot_nt(table[...], top[...]) + dot_nt(table8[...], low[...]) * back[0]
    ring.end()
    value, slope = gelu_both(total + bias_column(packs, 0))
    value = value.astype(BF16)
    hidden_t[...] = value
    slope_t[...] = slope
    z = dot_nn(packs[:, 128 : 128 + units], value).astype(BF16)
    z_own[...] = z
    half = nodes // 2
    chosen = dot_nt(pick_rows(send[...], place[0] * half + step * ROWS, ROWS), z)
    z_send[...] = (z_send[...].astype(F32) + chosen.reshape(z_send.shape)).astype(BF16)


def own_part_kernel(place, high, rest, z_own, z_oth, total, table, table8, back, hbuf, rbuf, sems):
    half = z_own.shape[1]
    nodes = 2 * half
    ring = Ring((high, rest), (hbuf, rbuf), sems, lambda i: (span(i * FINE, FINE), slice(0, nodes)))
    ring.begin()

    @pl.when(pl.program_id(0) == 0)
    def _():
        def larger(i, most):
            here = span(i * ROWS, ROWS)
            both = jnp.maximum(jnp.abs(z_own[:, here].astype(F32)), jnp.abs(z_oth[:, here].astype(F32)))
            return jnp.maximum(most, both)

        most = lax.fori_loop(0, half // ROWS, larger, jnp.zeros((z_own.shape[0], ROWS), F32))
        scale, inverse = scale_of(most)
        back[0] = inverse * (1.0 / REST_GAIN)
        for ref, first in ((z_own, place[0] * half), (z_oth, (1 - place[0]) * half)):

            def put(i, carry):
                value = ref[:, span(i * ROWS, ROWS)]
                cols = span(first + i * ROWS, ROWS)
                table[:, cols] = value
                table8[:, cols] = (value.astype(F32) * scale).astype(F8)
                return carry

            lax.fori_loop(0, half // ROWS, put, 0)

    top, low = ring.wait()
    total[...] = dot_nt(table[...], top[...]) + dot_nt(table8[...], low[...]) * back[0]
    ring.end()


def padded_rows(ref, count):
    value = ref[...]
    extra = jnp.zeros((count - value.shape[0], value.shape[1]), value.dtype)
    return jnp.concatenate([value, extra], axis=0).astype(BF16)


def border_cut(nodes, halo):
    return lambda i: (span(i * ROWS, ROWS), slice(nodes, nodes + halo))


def layer_two_end_kernel(place, flags_t, packs, send, high, rest, total, came, came_oth, last_t, hidden_t, slope_t, z_own, z_send, border, border8, back):
    halo = send.shape[0]
    width = hidden_t.shape[0]
    kinds = z_own.shape[0]
    step = pl.program_id(0)
    half = ROWS * pl.num_programs(0)

    @pl.when(step == 0)
    def _():
        both = came[...].reshape(halo, width).astype(F32) + came_oth[...].reshape(halo, width).astype(F32)
        value = jnp.where(flags_t[1:2, :] == 1.0, both.T, stale_columns(packs, 1, halo))
        scale, inverse = scale_of(value)
        border[...] = value.astype(BF16)
        border8[...] = (value * scale).astype(F8)
        back[0] = inverse * (1.0 / REST_GAIN)
        z_send[...] = jnp.zeros(z_send.shape, BF16)

    sums = total[...] + dot_nt(border[...], high[...]) + dot_nt(border8[...], rest[...]) * back[0]
    value, slope = gelu_both(sums + bias_column(packs, 1))
    value = value.astype(BF16)
    hidden_t[...] = value
    slope_t[...] = slope
    z = dot_nn(padded_rows(last_t, kinds), value).astype(BF16)
    z_own[...] = z
    chosen = dot_nt(pick_rows(send[...], place[0] * half + step * ROWS, ROWS), z)
    chosen = jnp.concatenate([chosen, jnp.zeros((halo, 128 - kinds), F32)], axis=1)
    z_send[...] = (z_send[...].astype(F32) + chosen.reshape(z_send.shape)).astype(BF16)


def put_border(border_grad, total, keep):
    value = (total * keep).T
    bound = value.shape[0] // border_grad.shape[0]
    border_grad[:, 0:bound, :] = value.reshape(border_grad.shape[0], bound, value.shape[1])


def loss_kernel(classes, place, flags_t, came, came_oth, stale_t, bias, labels, mask, total_hbm, high, rest, sums, back_out, border_grad, grads_hbm, grads8_hbm, far_hbm, border_sum, hrows, rrows, total, grads, grads8, far, hbuf, rbuf, in_sems, edge_sems, out_sems, far_sems):
    kinds, half = total.shape
    halo = stale_t.shape[1]
    steps = half // ROWS
    cut = border_cut(2 * half, halo)
    blocks = Stream(
        in_sems,
        (high, cut, hrows, rows_at(ROWS)),
        (rest, cut, rrows, rows_at(ROWS)),
        (total_hbm, cols_at(ROWS), total, cols_at(ROWS)),
    )
    others = cols_at(ROWS, (1 - place[0]) * half)
    edges = Stream(edge_sems, (high, others, hbuf, cols_at(ROWS)), (rest, others, rbuf, cols_at(ROWS)))
    stores = Stream(
        out_sems, *[(a, cols_at(ROWS), b, cols_at(ROWS)) for a, b in ((grads, grads_hbm), (grads8, grads8_hbm))]
    )
    far_stores = Stream(far_sems, (far, cols_at(ROWS), far_hbm, cols_at(ROWS)))
    blocks.start_first(steps)
    both = came[...].reshape(halo, 128).astype(F32) + came_oth[...].reshape(halo, 128).astype(F32)
    old = jnp.concatenate([stale_t[...].astype(F32), jnp.zeros((kinds - classes, halo), F32)], axis=0)
    value = jnp.where(flags_t[2:3, :] == 1.0, both.T[0:kinds, :], old)
    scale, back = scale_of(value)
    back = back * (1.0 / REST_GAIN)
    border = value.astype(BF16)
    border8 = (value * scale).astype(F8)
    row = jnp.concatenate([bias[...], jnp.zeros((1, 128 - classes), F32)], axis=1)
    bias_col = jnp.broadcast_to(row, (8, 128)).T[0:kinds, 0:1]
    sums[...] = jnp.zeros(sums.shape, F32)
    border_sum[...] = jnp.zeros(border_sum.shape, F32)
    count = flags_t[3:4, 0:1]
    inverse = (1.0 / (256.0 * REST_GAIN)) / count
    back_out[...] = jnp.broadcast_to(inverse, back_out.shape)

    def step(i):
        blocks.next(i, steps)
        edges.start(i)
        here = span(i * ROWS, ROWS)
        logits = total[:, here] + dot_nt(border, hrows[here, :]) + dot_nt(border8, rrows[here, :]) * back
        logits = logits + bias_col
        kind = lax.broadcasted_iota(I32, logits.shape, 0)
        real = kind < classes
        logits = jnp.where(real, logits, -jnp.inf)
        shifted = logits - jnp.max(logits, axis=0, keepdims=True)
        powers = jnp.exp(shifted)
        norm = jnp.sum(powers, axis=0, keepdims=True)
        logp = jnp.where(real, shifted - jnp.log(norm), 0.0)
        first = (place[0] * steps + i) * (ROWS // 128)
        row_of = lambda ref: jnp.concatenate([ref[pl.ds(first + k, 1), :] for k in range(ROWS // 128)], axis=1)
        target = jnp.where(kind == row_of(labels), 0.9, 0.0) + 0.1 / classes
        used = row_of(mask).astype(F32)
        loss = jnp.sum(target * logp, axis=0, keepdims=True) * used
        grad = jnp.where(real, (powers / norm - target) * (used / count), 0.0)
        sums[0:kinds, :] += lane_sums(grad)
        sums[kinds : kinds + 1, :] -= lane_sums(loss)
        top = grad.astype(BF16)
        tail = (grad - top.astype(F32)).astype(BF16)
        stacked = jnp.concatenate([top, tail], axis=0)
        small = (top.astype(F32) * (256.0 * count)).astype(F8)
        grads[:, here] = stacked
        grads8[:, here] = small
        stores.start(i)
        both = dot_nn(stacked, hrows[here, :])
        low = dot_nn(small, rrows[here, :]) * inverse
        border_sum[0:kinds, :] += both[0:kinds] + both[kinds : 2 * kinds] + low

    loop(steps, step)
    put_border(border_grad, border_sum[...], flags_t[2:3, :])

    def far_step(i):
        edges.wait(i)
        here = span(i * ROWS, ROWS)
        both = dot_nn(grads[...], hbuf[:, here])
        far[:, here] = both[0:kinds] + both[kinds : 2 * kinds] + dot_nn(grads8[...], rbuf[:, here]) * inverse
        far_stores.start(i)

    loop(steps, far_step)
    stores.wait_all(steps)
    far_stores.wait_all(steps)


def lane_sums(value):
    total = value[:, 0:128]
    for first in range(128, value.shape[1], 128):
        total = total + value[:, first : first + 128]
    return total


def back_three_kernel(place, high, rest, grads, grads8, back, out, hbuf, rbuf, sems):
    kinds, size = out.shape
    base = place[0] * size * pl.num_programs(0)
    ring = Ring((high, rest), (hbuf, rbuf), sems, lambda i: (slice(None), span(base + i * size, size)))
    ring.begin()
    top, low = ring.wait()
    both = dot_nn(grads[...], top[...])
    out[...] = both[0:kinds] + both[kinds : 2 * kinds] + dot_nn(grads8[...], low[...]) * back[0:1, 0:1]
    ring.end()


def back_block(grads, grads8, tails8, back_rest, back_tail, top, low):
    total = dot_nn(grads[...], top) + dot_nn(grads8[...], low) * back_rest
    return total + dot_nn(tails8[...], top.astype(F8)) * back_tail


def back_kernel(halves, place, high, rest, grads, grads8, tails8, back, *refs):
    *outs, hbuf, rbuf, sems = refs
    size = outs[0].shape[1]
    steps = pl.num_programs(0) // len(outs)
    base = place[1] * size * steps if halves == 2 else 0

    def cut(i):
        owner = jnp.where(i < steps * (len(outs) - 1), 1 - place[0], place[0])
        return slice(None), span(owner * size * steps * halves + base + lax.rem(i, steps) * size, size)

    ring = Ring((high, rest), (hbuf, rbuf), sems, cut)
    ring.begin()
    top, low = ring.wait()
    total = back_block(grads, grads8, tails8, back[0:1, 0:1], back[0:1, 1:2], top[...], low[...])
    for k, out in enumerate(outs):

        @pl.when((ring.step >= k * steps) & (ring.step < (k + 1) * steps))
        def _():
            out[...] = total

    ring.end()


def returned_terms(ret, ret_oth, bound, kinds):
    value = ret[:, 0:bound, :] + ret_oth[:, 0:bound, :]
    value = value.reshape(value.shape[0] * bound, value.shape[2]).T[0:kinds, :]
    top = value.astype(BF16)
    return top, (value - top.astype(F32)).astype(BF16)


def round_gradient(own, came_part, terms, send, first_node):
    chosen = pick_rows(send, first_node, own.shape[1])
    total = own + came_part
    for term in terms:
        total = total + dot_nn(term, chosen)
    return total.astype(BF16)


def end_kernel(layer, place, flags_t, ret, ret_oth, weight_ref, send, far_in_any, near_hbm, hidden_hbm, slope_hbm, high, rest, sums, back_out, border_grad, chunk_out, grads_hbm, grads8_hbm, tails8_hbm, *more):
    if layer == 1:
        far_hbm, far, hbuf, rbuf, edge_sems, far_sems = more[0], *more[-5:]
        more = more[1:-5]
    near, far_in, hidden_t, slope_t, hrows, rrows, grad_rows, grad_weight, border_sum, grads, grads8, tails8, in_sems, row_sems, out_sems = more
    kinds, half = near.shape
    units = slope_t.shape[0]
    parts = ret.shape[0]
    bound = send.shape[0] // parts
    halo = send.shape[0]
    steps = half // ROWS
    size = 64 // parts
    cut = border_cut(2 * half, halo)
    blocks = Stream(
        in_sems,
        *[
            (a, cols_at(ROWS), b, cols_at(ROWS))
            for a, b in ((near_hbm, near), (far_in_any, far_in), (hidden_hbm, hidden_t), (slope_hbm, slope_t))
        ],
    )
    borders = Stream(row_sems, (high, cut, hrows, rows_at(ROWS)), (rest, cut, rrows, rows_at(ROWS)))
    stores = Stream(
        out_sems,
        *[
            (a, cols_at(ROWS), b, cols_at(ROWS))
            for a, b in ((grads, grads_hbm), (grads8, grads8_hbm), (tails8, tails8_hbm))
        ],
    )
    if layer == 1:
        others = cols_at(ROWS, (1 - place[0]) * half)
        edges = Stream(edge_sems, (high, others, hbuf, cols_at(ROWS)), (rest, others, rbuf, cols_at(ROWS)))
        far_stores = Stream(far_sems, (far, cols_at(ROWS), far_hbm, cols_at(ROWS)))
    blocks.start_first(steps)
    terms = returned_terms(ret, ret_oth, bound, kinds)
    if layer == 0:
        chunk_out[...] = jnp.sum(ret[:, bound:, :] + ret_oth[:, bound:, :], axis=0)
        weight = weight_ref[:, 128 : 128 + units]
    else:
        chunk_out[...] = jnp.zeros(chunk_out.shape, F32)
        weight = padded_rows(weight_ref, kinds)
    sums[...] = jnp.zeros(sums.shape, F32)
    grad_weight[...] = jnp.zeros(grad_weight.shape, F32)
    border_sum[...] = jnp.zeros(border_sum.shape, F32)

    def first_step(i, most):
        blocks.next(i, steps)
        borders.start(i)
        here = span(i * ROWS, ROWS)
        d_z = round_gradient(near[:, here], far_in[:, here], terms, send[...], (place[0] * steps + i) * ROWS)
        grad_weight[0:kinds, :] += dot_nt(d_z, hidden_t[:, here])
        grad = dot_tn(weight, d_z) * slope_t[:, here]
        sums[...] += lane_sums(grad)
        grad_rows[:, here] = grad
        return jnp.maximum(most, jnp.max(jnp.abs(grad), axis=0, keepdims=True))

    most = lax.fori_loop(0, steps, first_step, jnp.zeros((1, ROWS), F32))
    if layer == 1:
        edges.start_first(steps)
    scale, back = scale_of(most)
    back_rest, back_tail = back * (1.0 / REST_GAIN), back * (1.0 / TAIL_GAIN)
    lane = lax.broadcasted_iota(I32, back_out.shape, 1)
    back_out[...] = jnp.where(lane == 0, back_rest, back_tail)

    def second_step(i):
        borders.wait(i)
        here = span(i * ROWS, ROWS)
        grad = grad_rows[:, here]
        top = grad.astype(BF16)
        wide = top.astype(F32)
        small = (wide * scale).astype(F8)
        tail = ((grad - wide) * (scale * TAIL_GAIN)).astype(F8)
        grads[:, here] = top
        grads8[:, here] = small
        tails8[:, here] = tail
        stores.start(i)
        border_sum[...] += back_block(top, small, tail, back_rest, back_tail, hrows[here, :], rrows[here, :])

    loop(steps, second_step)
    put_border(border_grad, border_sum[...], flags_t[layer : layer + 1, :])
    if layer == 1:
        border_grad[:, bound:, :] = grad_weight[...].reshape(parts, size, units)
    else:
        for core in range(2):
            block = grad_weight[span(place[1] * 128 + core * 64, 64), :]
            first = bound + core * size
            border_grad[:, first : first + size, :] = block.reshape(parts, size, units)

    def far_step(i):
        edges.next(i, steps)
        here = span(i * ROWS, ROWS)
        far[:, here] = back_block(grads, grads8, tails8, back_rest, back_tail, hbuf[:, here], rbuf[:, here])
        far_stores.start(i)

    if layer == 1:
        loop(steps, far_step)
        far_stores.wait_all(steps)
    stores.wait_all(steps)


def end_one_kernel(place, ret, ret_oth, send, sums_one, sums_two, sums_out, far_any, near_hbm, feat_hbm, out, out_one, out_two, out_three, second_chunk, near, far, feat_t, grad_first, in_sems):
    units, size = near.shape
    parts = ret.shape[0]
    bound = send.shape[0] // parts
    width = feat_t.shape[0]
    chunk = 64 // parts
    steps = size // ROWS
    base = place[0] * 2 * size + place[1] * size
    blocks = Stream(
        in_sems,
        (near_hbm, cols_at(ROWS), near, cols_at(ROWS)),
        (far_any, cols_at(ROWS), far, cols_at(ROWS)),
        (feat_hbm, cols_at(ROWS, base), feat_t, cols_at(ROWS)),
    )
    blocks.start_first(steps)
    terms = returned_terms(ret, ret_oth, bound, units)
    mine = pl.ds(bound + place[0] * chunk, chunk)
    second_chunk[...] = jnp.sum(ret[:, mine, :] + ret_oth[:, mine, :], axis=0)
    grad_first[...] = jnp.zeros(grad_first.shape, F32)

    def step(i):
        blocks.next(i, steps)
        here = span(i * ROWS, ROWS)
        d_z = round_gradient(near[:, here], far[:, here], terms, send[...], base + i * ROWS)
        grad_first[:, 0:width] += dot_nt(d_z, feat_t[:, here])

    loop(steps, step)
    lead = jnp.where(place[1] == 0, 1.0, 0.0)
    lane = lax.broadcasted_iota(I32, (64, 128), 1)
    column = lambda value: jnp.sum(value, axis=1, keepdims=True) * lead
    for k, ref in enumerate((out, out_one, out_two, out_three)):
        rows = span(jnp.bitwise_xor(place[0] + 2 * place[1], k) * 64, 64)
        value = grad_first[rows, :]
        value = jnp.where(lane == FLAG_LANE, column(sums_one[rows, :]), value)
        value = jnp.where(lane == FLAG_LANE + 1, column(sums_two[rows, :]), value)
        ref[...] = jnp.where(lane == FLAG_LANE + 2, column(sums_out[...]), value)


def gather_kernel(mine, one, two, three, second_chunk, last_chunk, out):
    total = mine[...] + one[...] + two[...] + three[...]
    size = second_chunk.shape[0]
    parts = [total]
    for chunk in (second_chunk, last_chunk):
        parts += [chunk[:, 0:128], chunk[:, 128:256]]
    value = jnp.concatenate(parts, axis=0)
    for p in range(out.shape[0]):
        out[p] = value


def adamw(weight, moment, square, gradient):
    moment = beta_one * moment + (1.0 - beta_one) * gradient
    square = beta_two * square + (1.0 - beta_two) * gradient * gradient
    moment_hat = moment / (1.0 - beta_one**STEP)
    square_hat = square / (1.0 - beta_two**STEP)
    weight = weight - rate_step * (
        moment_hat / (jnp.sqrt(square_hat) + epsilon) + decay_rate * weight
    )
    return (weight, moment, square)


def update_kernel(came, flags_t, *refs):
    params, outs = refs[0:15], refs[15:]
    parts = came.shape[0]
    size = 64 // parts
    width, kinds = params[0].shape[1], params[6].shape[0]
    total = jnp.sum(came[:, 0:64, :], axis=0)

    def chunks(first):
        halves = [
            came[:, first + k * size : first + (k + 1) * size, :].reshape(64, 128) for k in range(2)
        ]
        return jnp.concatenate(halves, axis=1)

    turned = jnp.concatenate([total, jnp.zeros((64, 128), F32)], axis=0).T
    gradients = (
        total[:, 0:width],
        chunks(64),
        chunks(64 + 2 * size)[0:kinds, :],
        turned[FLAG_LANE : FLAG_LANE + 2, 0:64],
        turned[FLAG_LANE + 2 : FLAG_LANE + 3, 0:kinds],
    )
    for k, gradient in enumerate(gradients):
        values = adamw(*[ref[...] for ref in params[3 * k : 3 * k + 3]], gradient)
        for ref, value in zip(outs[3 * k : 3 * k + 3], values):
            ref[...] = value
    padded = turned[FLAG_LANE + 2 : FLAG_LANE + 3, 48:49]
    outs[15][...] = jnp.broadcast_to(padded, (1, 128))
    outs[16][...] = jnp.broadcast_to(flags_t[3:4, 0:1], (1, 128))


def body(
    parts,
    reps,
    features,
    labels,
    train_mask,
    edge_src,
    edge_norm,
    send_rows,
    changed,
    cache_hidden,
    cache_out,
    first_weight,
    second_weight,
    last_weight,
    hidden_bias,
    out_bias,
    moment_first,
    moment_second,
    moment_last,
    moment_hidden,
    moment_out,
    square_first,
    square_second,
    square_last,
    square_hidden,
    square_out,
):
    nodes, in_width = features.shape
    half = nodes // 2
    bound = send_rows.shape[2]
    halo = parts * bound
    table = nodes + halo
    units, classes = last_weight.shape
    kinds = -(-classes // 16) * 16
    steps, fine = half // ROWS, half // FINE

    rep = lax.axis_index("rep")
    place = jnp.stack([lax.rem(rep, 2), lax.div(rep, 2)]).astype(I32)
    where = (place, SMEM)
    feat_t = features.T
    last_t = last_weight.T
    label_rows = labels.reshape(nodes // 128, 128)
    mask_rows = train_mask.reshape(nodes // 128, 128)

    def swap(x, k=1):
        return lax.ppermute(x, "rep", [(i, i ^ k) for i in range(reps)])

    def exchange(x):
        return lax.all_to_all(x, "dom", split_axis=0, concat_axis=0, tiled=True)

    def late(after, *arrays):
        return lax.optimization_barrier((*arrays, after))

    vm = pltpu.VMEM
    whole = lambda a: (a, whole_spec(a.shape))
    work = 2 * half * table * units
    pack_width = 256 + units + 2 * halo
    rows_out, pack, send = run(
        pack_kernel,
        "pack",
        [
            whole(feat_t),
            whole(send_rows.reshape(parts, bound)),
            (changed.T, SMEM),
            *[whole(a) for a in (mask_rows, first_weight.T, second_weight.T)],
            *[whole(a) for a in (jnp.transpose(cache_hidden, (0, 2, 1)), hidden_bias)],
        ],
        [
            ((parts, bound, 128), BF16, VMEM),
            ((units // reps, pack_width), BF16, VMEM),
            ((halo, 1), I32, VMEM),
        ],
        flops=2 * halo * nodes * 128,
        grid=(1,),
    )
    packs = [pack if k == 0 else swap(pack, k) for k in range(reps)]
    rows = exchange(rows_out)
    node_block = lambda size, rows: pl.BlockSpec((rows, size), lambda i: (0, i))
    block, fine_block = node_block(ROWS, units), node_block(FINE, units)
    scalar = pltpu.SMEM((1,), F32)
    high, rest = run(
        build_kernel,
        "build",
        [where, *placed(OWN, edge_src.T, edge_norm.T)],
        [((half, table), BF16, HBM), ((half, table), F8, HBM)],
        [vm((half, table), BF16), vm((half, table), F8), sems(2, half // 128)],
        flops=4 * 256 * table * half,
    )
    edge = placed(HBM, high, rest)

    packs, hidden_one, slope_one, z_own, z_send, flags_t = run(
        layer_one_kernel,
        "layer_one",
        [where, *placed(VMEM, rows), whole(feat_t), *placed(VMEM, *packs, send), *edge],
        [
            ((units, pack_width), BF16, whole_spec((units, pack_width))),
            ((units, half), BF16, block),
            ((units, half), F32, block),
            ((units, half), BF16, block),
            ((parts, bound, units), BF16, whole_spec((parts, bound, units))),
            ((8, halo), F32, whole_spec((8, halo))),
        ],
        [vm((units, table), BF16), vm((units, table), F8), scalar, *ring_scratch((ROWS, table), 2)],
        flops=work,
        grid=(steps,),
    )

    def own_part(z_own, z_oth, name):
        n = z_own.shape[0]
        return run(
            own_part_kernel,
            name,
            [where, *edge, whole(z_own), (z_oth, VMEM)],
            [((n, half), F32, node_block(FINE, n))],
            [vm((n, nodes), BF16), vm((n, nodes), F8), scalar, *ring_scratch((FINE, nodes))],
            flops=work,
            grid=(fine,),
        )[0]

    z_oth = swap(z_own)
    came = exchange(z_send)
    total = own_part(z_own, z_oth, "layer_two_own")
    came, total = late(total, came)
    came_oth = swap(came)
    border_block = lambda array: (array, pl.BlockSpec((ROWS, halo), lambda i: (i, nodes // halo)))
    hidden_two, slope_two, z_own, z_send = run(
        layer_two_end_kernel,
        "layer_two_end",
        [where, whole(flags_t), whole(packs), (send, VMEM), border_block(high), border_block(rest), (total, block)]
        + placed(VMEM, came, came_oth)
        + [whole(last_t)],
        [
            ((units, half), BF16, block),
            ((units, half), F32, block),
            ((kinds, half), BF16, node_block(ROWS, kinds)),
            ((parts, bound, 128), BF16, whole_spec((parts, bound, 128))),
        ],
        [vm((units, halo), BF16), vm((units, halo), F8), scalar],
        flops=work // 4,
        grid=(steps,),
    )
    z_oth = swap(z_own)
    came = exchange(z_send)
    total = own_part(z_own, z_oth, "layer_three_own")
    came, total = late(total, came)
    came_oth = swap(came)
    border_rows = [vm((half, halo), BF16), vm((half, halo), F8)]
    sums_out, back, border_grad, grads, grads8, far = run(
        functools.partial(loss_kernel, classes),
        "loss",
        [
            where,
            *placed(VMEM, flags_t, came, came_oth, cache_out.T, out_bias.reshape(1, classes), label_rows, mask_rows),
            (total, HBM),
            *edge,
        ],
        [
            ((64, 128), F32, VMEM),
            ((8, 128), F32, VMEM),
            ((parts, bound, 128), F32, VMEM),
            ((2 * kinds, half), BF16, HBM),
            ((kinds, half), F8, HBM),
            ((kinds, half), F32, HBM),
        ],
        [
            vm((128, halo), F32),
            *border_rows,
            vm((kinds, half), F32),
            vm((2 * kinds, half), BF16),
            vm((kinds, half), F8),
            vm((kinds, half), F32),
            vm((half, half), BF16),
            vm((half, half), F8),
            sems(3, steps),
            sems(2, steps),
            sems(2, steps),
            sems(1, steps),
        ],
        flops=work,
    )
    far = swap(far)
    ret = exchange(border_grad)
    near = run(
        back_three_kernel,
        "back_three",
        [where, *edge, whole(grads), whole(grads8), (back, VMEM)],
        [((kinds, half), F32, node_block(FINE, kinds))],
        ring_scratch((half, FINE)),
        flops=work // 2,
        grid=(fine,),
    )[0]
    ret, far, near = late(near, ret, far)
    ret_oth = swap(ret)
    chunk = 64 // parts

    def end(layer, name, ret, ret_oth, weight, near, far, hidden, slope):
        n = near.shape[0]
        with_far = layer == 1
        return run(
            functools.partial(end_kernel, layer),
            name,
            [
                where,
                *placed(VMEM, flags_t, ret, ret_oth, weight, send),
                (far, ANY),
                *placed(HBM, near, hidden, slope),
                *edge,
            ],
            [
                ((units, 128), F32, VMEM),
                ((8, 128), F32, VMEM),
                ((parts, bound + (1 if with_far else 2) * chunk, units), F32, VMEM),
                ((chunk, units), F32, VMEM),
                ((units, half), BF16, HBM),
                ((units, half), F8, HBM),
                ((units, half), F8, HBM),
                *([((units, half), F32, HBM)] if with_far else []),
            ],
            [
                vm((n, half), F32),
                vm((n, half), F32),
                vm((units, half), BF16),
                vm((units, half), F32),
                *border_rows,
                vm((units, half), F32),
                vm((max(n, 64), units), F32),
                vm((units, halo), F32),
                vm((units, half), BF16),
                vm((units, half), F8),
                vm((units, half), F8),
                sems(4, steps),
                sems(2, steps),
                sems(3, steps),
            ]
            + (
                [vm((units, half), F32), vm((half, half), BF16), vm((half, half), F8), sems(2, steps), sems(1, steps)]
                if with_far
                else []
            ),
            flops=work,
        )

    def back_part(halves, back, grads, grads8, tails8):
        each = fine // halves
        out_block = lambda k: pl.BlockSpec((units, FINE), lambda i: (0, jnp.clip(i - k * each, 0, each - 1)))
        return run(
            functools.partial(back_kernel, halves),
            "back",
            [where, *edge, whole(grads), whole(grads8), whole(tails8), (back, VMEM)],
            [((units, half // halves), F32, out_block(k)) for k in range(halves)],
            ring_scratch((half, FINE)),
            flops=work // 2,
            grid=(fine,),
        )

    sums_two, back, border_grad, _, grads, grads8, tails8, far = end(
        1, "end_three", ret, ret_oth, last_t, near, far, hidden_two, slope_two
    )
    far = swap(far)
    ret = exchange(border_grad)
    near = back_part(1, back, grads, grads8, tails8)[0]
    ret, far, near = late(near, ret, far)
    ret_oth = swap(ret)
    sums_one, back, border_grad, last_chunk, grads, grads8, tails8 = end(
        0, "end_two", ret, ret_oth, packs, near, far, hidden_one, slope_one
    )
    ret = exchange(border_grad)
    far, near = back_part(2, back, grads, grads8, tails8)
    far = swap(far)
    ret, near = late(near, ret)
    ret_oth = swap(ret)
    *pieces, second_chunk = run(
        end_one_kernel,
        "end_one",
        [where, *placed(VMEM, ret, ret_oth, send, sums_one, sums_two, sums_out), (far, ANY), *placed(HBM, near, feat_t)],
        [((64, 128), F32, VMEM)] * 4 + [((chunk, units), F32, VMEM)],
        [
            vm((units, half // 2), F32),
            vm((units, half // 2), F32),
            vm((in_width, half // 2), BF16),
            vm((units, 128), F32),
            sems(3, steps),
        ],
        flops=work // 8,
    )
    pieces = [piece if k == 0 else swap(piece, k) for k, piece in enumerate(pieces)]
    gathered = run(
        gather_kernel,
        "gather",
        placed(VMEM, *pieces, second_chunk, last_chunk),
        [((parts, 64 + 4 * chunk, 128), F32, VMEM)],
    )[0]
    came = exchange(gathered)

    turn = lambda x: x.T
    same = lambda x: x
    row = lambda x: x.reshape(1, -1)
    forms = (turn, turn, turn, same, row)
    weights = (first_weight, second_weight, last_weight, hidden_bias, out_bias)
    moments = (moment_first, moment_second, moment_last, moment_hidden, moment_out)
    squares = (square_first, square_second, square_last, square_hidden, square_out)
    params = [form(x) for form, triple in zip(forms, zip(weights, moments, squares)) for x in triple]
    outs = run(
        update_kernel,
        "update",
        placed(VMEM, came, flags_t, *params),
        [(p.shape, F32, VMEM) for p in params] + [((1, 128), F32, VMEM)] * 2,
    )
    undo = (turn, turn, turn, same, lambda x: x.reshape(-1))
    results = [undo[k // 3](x) for k, x in enumerate(outs[0:15])]
    return (outs[15][0, 0], outs[16][0, 0], *results)


def solution(mesh):
    placed = (
        P("dom", None),
        P("dom"),
        P("dom"),
        P("dom", None),
        P("dom", None),
        P("dom", None, None),
        P(None, "dom"),
        P(None, "dom", "rep"),
        P("dom", None),
        P(None, "rep"),
        P(None, "rep"),
        P(),
        P(None, "rep"),
        P(),
        P(None, "rep"),
        P(None, "rep"),
        P(),
        P(None, "rep"),
        P(),
        P(None, "rep"),
        P(None, "rep"),
        P(),
        P(None, "rep"),
        P(),
    )
    return jax.shard_map(
        functools.partial(body, mesh.shape["dom"], mesh.shape["rep"]),
        mesh=mesh,
        in_specs=placed,
        out_specs=(P(), P()) + (P(None, "rep"),) * 6 + (P(),) * 3 + (P(None, "rep"),) * 3 + (P(),) * 3,
        check_vma=False,
    )
```

time: 288 us -> 207 us (0.72)
  local copies, waits for them, and re-layouts: 75.8 us -> 1.2 us
  blocking collectives: 25.3 us -> 18.6 us
  waiting for transfers between devices: 9.15 us -> 12.8 us
    unnamed x155 -> x46, local copies, waits for them, and re-layouts: 72.9 us -> 1.2 us
    all_gather x1 -> x0, blocking collectives: 7.18 us -> none  [body(): packs = lax.all_gather(pack, 'rep', axis=0, tiled=True)]
    pallas_call x18 -> x15, Pallas kernels: 133 us -> 131 us  [run(): pl.pallas_call(kernel, grid=grid, in_specs=[spec for _, spec in args], ou...]
    ppermute x13 -> x16, starting transfers between devices: 3.9 us -> 6.33 us  [swap(): return lax.ppermute(x, 'rep', [(i, i ^ k) for i in range(reps)])]
    ppermute x13 -> x16, waiting for transfers between devices: 9.13 us -> 10.2 us  [swap(): return lax.ppermute(x, 'rep', [(i, i ^ k) for i in range(reps)])]
  transfers between devices with their start and end apart: 19 -> 22, of which waited for: 7 -> 10; matrix products, arithmetic and copies ran while one was open for 1% -> 0% of each run, Pallas kernels for 24% -> 34%
where the time goes in v2:
time: 207 us; the launch traced here: 206 us
  Pallas kernels  131 us (63%)
  starting transfers between devices  41.6 us (20%)
  blocking collectives  18.6 us (9%)
  waiting for transfers between devices  12.8 us (6%)
    pallas_call x15, Pallas kernels, run(): pl.pallas_call(kernel, grid=grid, in_specs=[spec for _, spec in args], ou...  131 us
    all_to_all x6, starting transfers between devices, exchange(): return lax.all_to_all(x, 'dom', split_axis=0, concat_axis=0, tiled=True)  35.3 us
    all_to_all x1, blocking collectives, exchange(): return lax.all_to_all(x, 'dom', split_axis=0, concat_axis=0, tiled=True)  18.6 us
    ppermute x16, waiting for transfers between devices, swap(): return lax.ppermute(x, 'rep', [(i, i ^ k) for i in range(reps)])  10.2 us
    ppermute x16, starting transfers between devices, swap(): return lax.ppermute(x, 'rep', [(i, i ^ k) for i in range(reps)])  6.33 us
  transfers between devices with their start and end apart: 22, of which 10 were waited for; matrix products, arithmetic and copies ran while one was open for 0% of the time, Pallas kernels for 34%

profile of v2, /device:TPU:0, one launch (start us, length us, event | category | flops | bytes accessed | tf_op | source)
XLA Modules:
  0.0 206.1 jit_solution(10993167628898428351)
XLA Ops:
  1.3 4.4 %pack.1 = (bf16[8,32,128]{2,1,0:T(8,128)(2,1)}, bf16[64,1024]{1,0:T(8,128)(2,1)S(1)}, s32[256,1]{1,0:T(8,128)S(1)}) custom-call(bf16[100,4096]{1,0:T(8,128)(2,1)} %bitcast.61, s32[8,32]{1,0:T(8,128)} %bitcast.65, s32[1,3]{1,0:T(1,128)S(1)} %bitcast.58, s32[32,128]{1,0:T(8,128)} %bitcast.48, f32[64,100]{1,0:T(8,128)} %bitcast.44, f32[64,256]{1,0:T(8,128)} %bitcast.42, ...), custom_call_target="tpu_custom_call" | custom-call | flops 268435456 | bytes 1048576 | tf_op jit(solution)/shard_map/pack/pallas_call | solution.py:46
  5.7 2.4 %collective-permute-start.2 = (bf16[64,1024]{1,0:T(8,128)(2,1)S(1)}, bf16[64,1024]{1,0:T(8,128)(2,1)S(1)}, u32[]{:S(2)}, u32[]{:S(2)}) collective-permute-start(bf16[64,1024]{1,0:T(8,128)(2,1)S(1)} %get-tuple-element.89.pack), channel_id=1, source_target_pairs={{0,3},{1,2},{2,1},{3,0},{4,7},{5,6},{6,5},{7,4},{8,11},{9,10},{10,... | collective-permute-start | bytes 393224 | tf_op jit(solution)/shard_map/ppermute | solution.py:810
  8.8 6.0 %all-to-all-start = ((bf16[8,32,128]{2,1,0:T(8,128)(2,1)}), bf16[8,32,128]{2,1,0:T(8,128)(2,1)S(1)}, u32[]{:S(2)}, u32[]{:S(2)}) async-start(bf16[8,32,128]{2,1,0:T(8,128)(2,1)} %get-tuple-element.88), calls=%async_computation | async-start | bytes 131072 | tf_op jit(solution)/shard_map/all_to_all | solution.py:813
  14.9 18.1 %build.1 = (bf16[2048,4352]{1,0:T(8,128)(2,1)}, f8e4m3fn[2048,4352]{1,0:T(32,128)(4,1)}) custom-call(s32[2]{0:T(128)S(1)} %pad_add_fusion.place, s32[16,4096]{1,0:T(8,128)} %bitcast.66, f32[16,4096]{1,0:T(8,128)} %bitcast.67), custom_call_target="tpu_custom_call" | custom-call | flops 9126805504 | bytes 1048576 | tf_op jit(solution)/shard_map/build/pallas_call | solution.py:46
  33.0 15.5 %layer_one.1 = (bf16[256,1024]{1,0:T(8,128)(2,1)}, bf16[256,2048]{1,0:T(8,128)(2,1)}, f32[256,2048]{1,0:T(8,128)}, bf16[256,2048]{1,0:T(8,128)(2,1)}, bf16[8,32,256]{2,1,0:T(8,128)(2,1)}, /*index=5*/f32[8,256]{1,0:T(8,128)}) custom-call(s32[2]{0:T(128)S(1)} %pad_add_fusion.place, bf16[8,32,128]{2,1,0:T(8,128)(2,1)S(1)} %all-to-all-done.rows, ...), custom_call_target="tpu_custom_call" | custom-call | flops 4563402752 | bytes 1048576 | tf_op jit(solution)/shard_map/layer_one/pallas_call | solution.py:46
  48.6 6.1 %all-to-all-start.1 = ((bf16[8,32,256]{2,1,0:T(8,128)(2,1)}), bf16[8,32,256]{2,1,0:T(8,128)(2,1)S(1)}, u32[]{:S(2)}, u32[]{:S(2)}) async-start(bf16[8,32,256]{2,1,0:T(8,128)(2,1)} %get-tuple-element.95), calls=%async_computation.1 | async-start | bytes 262144 | tf_op jit(solution)/shard_map/all_to_all | solution.py:813
  54.7 12.2 %layer_two_own.1.total = f32[256,2048]{1,0:T(8,128)} custom-call(s32[2]{0:T(128)S(1)} %pad_add_fusion.place, bf16[2048,4352]{1,0:T(8,128)(2,1)} %get-tuple-element.91.high, f8e4m3fn[2048,4352]{1,0:T(32,128)(4,1)} %get-tuple-element.92.rest, bf16[256,2048]{1,0:T(8,128)(2,1)} %get-tuple-element.96.z_own, bf16[256,2048]{1,0:T(8,128)(2,1)S(1)} %collective-permute-done.3.z_oth), custom_call_target="tpu_custom_call" | custom-call | flops 4563402752 | bytes 1048576 | tf_op jit(solution)/shard_map/layer_two_own/pallas_call | solution.py:46
  68.4 6.4 %layer_two_end.1 = (bf16[256,2048]{1,0:T(8,128)(2,1)}, f32[256,2048]{1,0:T(8,128)}, bf16[48,2048]{1,0:T(8,128)(2,1)}, bf16[8,32,128]{2,1,0:T(8,128)(2,1)}) custom-call(s32[2]{0:T(128)S(1)} %pad_add_fusion.place, f32[8,256]{1,0:T(8,128)} %get-tuple-element.93.flags_t, bf16[256,1024]{1,0:T(8,128)(2,1)} %get-tuple-element.94.packs.weight_ref, ...), custom_call_target="tpu_custom_call" | custom-call | flops 1140850688 | bytes 1048576 | tf_op jit(solution)/shard_map/layer_two_end/pallas_call | solution.py:46
  75.0 5.9 %all-to-all-start.2 = ((bf16[8,32,128]{2,1,0:T(8,128)(2,1)}), bf16[8,32,128]{2,1,0:T(8,128)(2,1)S(1)}, u32[]{:S(2)}, u32[]{:S(2)}) async-start(bf16[8,32,128]{2,1,0:T(8,128)(2,1)} %get-tuple-element.99), calls=%async_computation.2 | async-start | bytes 131072 | tf_op jit(solution)/shard_map/all_to_all | solution.py:813
  81.0 11.6 %layer_three_own.1.total_hbm = f32[48,2048]{1,0:T(8,128)} custom-call(s32[2]{0:T(128)S(1)} %pad_add_fusion.place, bf16[2048,4352]{1,0:T(8,128)(2,1)} %get-tuple-element.91.high, f8e4m3fn[2048,4352]{1,0:T(32,128)(4,1)} %get-tuple-element.92.rest, bf16[48,2048]{1,0:T(8,128)(2,1)} %get-tuple-element.100.z_own, bf16[48,2048]{1,0:T(8,128)(2,1)S(1)} %collective-permute-done.5.z_oth), custom_call_target="tpu_custom_call" | custom-call | flops 4563402752 | bytes 1048576 | tf_op jit(solution)/shard_map/layer_three_own/pallas_call | solution.py:46
  93.9 9.2 %loss.1 = (f32[64,128]{1,0:T(8,128)S(1)}, f32[8,128]{1,0:T(8,128)S(1)}, f32[8,32,128]{2,1,0:T(8,128)}, bf16[96,2048]{1,0:T(8,128)(2,1)}, f8e4m3fn[48,2048]{1,0:T(8,128)(4,1)}, /*index=5*/f32[48,2048]{1,0:T(8,128)}) custom-call(s32[2]{0:T(128)S(1)} %pad_add_fusion.place, f32[8,256]{1,0:T(8,128)S(1)} %copy-done.3, ...), custom_call_target="tpu_custom_call" | custom-call | flops 4563402752 | bytes 1048576 | tf_op jit(solution)/shard_map/loss/pallas_call | solution.py:46
  103.4 6.0 %all-to-all-start.3 = ((f32[8,32,128]{2,1,0:T(8,128)}), f32[8,32,128]{2,1,0:T(8,128)S(1)}, u32[]{:S(2)}, u32[]{:S(2)}) async-start(f32[8,32,128]{2,1,0:T(8,128)} %get-tuple-element.103), calls=%async_computation.3 | async-start | bytes 262144 | tf_op jit(solution)/shard_map/all_to_all | solution.py:813
  109.4 7.6 %back_three.1.near_hbm = f32[48,2048]{1,0:T(8,128)} custom-call(s32[2]{0:T(128)S(1)} %pad_add_fusion.place, bf16[2048,4352]{1,0:T(8,128)(2,1)} %get-tuple-element.91.high, f8e4m3fn[2048,4352]{1,0:T(32,128)(4,1)} %get-tuple-element.92.rest, bf16[96,2048]{1,0:T(8,128)(2,1)} %get-tuple-element.105.grads, f8e4m3fn[48,2048]{1,0:T(8,128)(4,1)} %get-tuple-element.106.grads8, ...), custom_call_target="tpu_custom_call" | custom-call | flops 2281701376 | bytes 1048576 | tf_op jit(solution)/shard_map/back_three/pallas_call | solution.py:46
  118.4 13.7 %end_three.1 = (f32[256,128]{1,0:T(8,128)S(1)}, f32[8,128]{1,0:T(8,128)S(1)}, f32[8,40,256]{2,1,0:T(8,128)}, f32[8,256]{1,0:T(8,128)}, bf16[256,2048]{1,0:T(8,12...) custom-call(s32[2]{0:T(128)S(1)} %pad_add_fusion.place, ...), custom_call_target="tpu_custom_call" | custom-call | flops 4563402752 | bytes 1048576 | tf_op jit(solution)/shard_map/end_three/pallas_call | solution.py:46
  132.4 6.0 %all-to-all-start.4 = ((f32[8,40,256]{2,1,0:T(8,128)}), f32[8,40,256]{2,1,0:T(8,128)S(1)}, u32[]{:S(2)}, u32[]{:S(2)}) async-start(f32[8,40,256]{2,1,0:T(8,128)} %get-tuple-element.113), calls=%async_computation.4 | async-start | bytes 655360 | tf_op jit(solution)/shard_map/all_to_all | solution.py:813
  138.3 9.9 %back.2.near_hbm = f32[256,2048]{1,0:T(8,128)} custom-call(s32[2]{0:T(128)S(1)} %pad_add_fusion.place, bf16[2048,4352]{1,0:T(8,128)(2,1)} %get-tuple-element.91.high, f8e4m3fn[2048,4352]{1,0:T(32,128)(4,1)} %get-tuple-element.92.rest, bf16[256,2048]{1,0:T(8,128)(2,1)} %get-tuple-element.115.grads, f8e4m3fn[256,2048]{1,0:T(32,128)(4,1)} %get-tuple-element.116.grads8, ...), custom_call_target="tpu_custom_call" | custom-call | flops 2281701376 | bytes 1048576 | tf_op jit(solution)/shard_map/back/pallas_call | solution.py:46
  149.1 1.6 collective-permute-done.10.ret_oth
  150.8 7.7 %end_two.1 = (f32[256,128]{1,0:T(8,128)S(1)}, f32[8,128]{1,0:T(8,128)S(1)}, f32[8,48,256]{2,1,0:T(8,128)}, f32[8,256]{1,0:T(8,128)S(1)}, bf16[256,2048]{1,0:T(8,...) custom-call(s32[2]{0:T(128)S(1)} %pad_add_fusion.place, f32[8,256]{1,0:T(8,128)S(1)} %copy-done.3, ...), custom_call_target="tpu_custom_call" | custom-call | flops 4563402752 | bytes 1048576 | tf_op jit(solution)/shard_map/end_two/pallas_call | solution.py:46
  158.5 5.2 %all-to-all-start.5 = ((f32[8,48,256]{2,1,0:T(8,128)}), f32[8,48,256]{2,1,0:T(8,128)S(1)}, u32[]{:S(2)}, u32[]{:S(2)}) async-start(f32[8,48,256]{2,1,0:T(8,128)} %get-tuple-element.124), calls=%async_computation.5 | async-start | bytes 786432 | tf_op jit(solution)/shard_map/all_to_all | solution.py:813
  163.7 10.2 %back.3 = (f32[256,1024]{1,0:T(8,128)}, f32[256,1024]{1,0:T(8,128)}) custom-call(s32[2]{0:T(128)S(1)} %pad_add_fusion.place, bf16[2048,4352]{1,0:T(8,128)(2,1)} %get-tuple-element.91.high, f8e4m3fn[2048,4352]{1,0:T(32,128)(4,1)} %get-tuple-element.92.rest, bf16[256,2048]{1,0:T(8,128)(2,1)} %get-tuple-element.125.grads, ...), custom_call_target="tpu_custom_call" | custom-call | flops 2281701376 | bytes 1048576 | tf_op jit(solution)/shard_map/back/pallas_call | solution.py:46
  174.0 1.7 all-to-all-done.5.ret
  178.0 3.1 %end_one.1 = (f32[64,128]{1,0:T(8,128)S(1)}, f32[64,128]{1,0:T(8,128)S(1)}, f32[64,128]{1,0:T(8,128)S(1)}, f32[64,128]{1,0:T(8,128)S(1)}, f32[8,256]{1,0:T(8,128)S(1)}) custom-call(s32[2]{0:T(128)S(1)} %pad_add_fusion.place, f32[8,48,256]{2,1,0:T(8,128)S(1)} %all-to-all-done.5.ret, f32[8,48,256]{2,1,0:T(8,128)S(1)} %collective-permute-done.11.ret_oth, ...), custom_call_target="tpu_custom_call" | custom-call | flops 570425344 | bytes 1048576 | tf_op jit(solution)/shard_map/end_one/pallas_call | solution.py:46
  183.0 2.2 %collective-permute-done.14.two = f32[64,128]{1,0:T(8,128)S(1)} collective-permute-done((f32[64,128]{1,0:T(8,128)S(1)}, f32[64,128]{1,0:T(8,128)S(1)}, u32[]{:S(2)}, u32[]{:S(2)}) %collective-permute-start.14) | collective-permute-done | bytes 32800 | tf_op jit(solution)/shard_map/ppermute | solution.py:810
  186.3 18.6 %all_to_all.35.came = f32[8,96,128]{2,1,0:T(8,128)S(1)} all-to-all(f32[8,96,128]{2,1,0:T(8,128)S(1)} %gather.1), channel_id=1, replica_groups=mesh['dom'=8,'rep'=4] {'dom'}, dimensions={0} | all-to-all | bytes 786432 | tf_op jit(solution)/shard_map/all_to_all | solution.py:813
  (83 shorter events, 13.5 us)
Async XLA Ops:
  5.7 27.3 %collective-permute-start.2 = (bf16[64,1024]{1,0:T(8,128)(2,1)S(1)}, bf16[64,1024]{1,0:T(8,128)(2,1)S(1)}, u32[]{:S(2)}, u32[]{:S(2)}) collective-permute-start(bf16[64,1024]{1,0:T(8,128)(2,1)S(1)} %get-tuple-element.89.pack), channel_id=1, source_target_pairs={{0,3},{1,2},{2,1},{3,0},{4,7},{5,6},{6,5},{7,4},{8,11},{9,10},{10,... | collective-permute-start | bytes 393224 | tf_op jit(solution)/shard_map/ppermute | solution.py:810
  8.1 24.9 %collective-permute-start.1 = (bf16[64,1024]{1,0:T(8,128)(2,1)S(1)}, bf16[64,1024]{1,0:T(8,128)(2,1)S(1)}, u32[]{:S(2)}, u32[]{:S(2)}) collective-permute-start(bf16[64,1024]{1,0:T(8,128)(2,1)S(1)} %get-tuple-element.89.pack), channel_id=1, source_target_pairs={{0,2},{1,3},{2,0},{3,1},{4,6},{5,7},{6,4},{7,5},{8,10},{9,11},{10,... | collective-permute-start | bytes 393224 | tf_op jit(solution)/shard_map/ppermute | solution.py:810
  8.7 24.3 %collective-permute-start = (bf16[64,1024]{1,0:T(8,128)(2,1)S(1)}, bf16[64,1024]{1,0:T(8,128)(2,1)S(1)}, u32[]{:S(2)}, u32[]{:S(2)}) collective-permute-start(bf16[64,1024]{1,0:T(8,128)(2,1)S(1)} %get-tuple-element.89.pack), channel_id=1, source_target_pairs={{0,1},{1,0},{2,3},{3,2},{4,5},{5,4},{6,7},{7,6},{8,9},{9,8},{10,11... | collective-permute-start | bytes 393224 | tf_op jit(solution)/shard_map/ppermute | solution.py:810
  8.8 24.2 %all-to-all-start = ((bf16[8,32,128]{2,1,0:T(8,128)(2,1)}), bf16[8,32,128]{2,1,0:T(8,128)(2,1)S(1)}, u32[]{:S(2)}, u32[]{:S(2)}) async-start(bf16[8,32,128]{2,1,0:T(8,128)(2,1)} %get-tuple-element.88), calls=%async_computation | async-start | bytes 131072 | tf_op jit(solution)/shard_map/all_to_all | solution.py:813
  48.5 6.2 %collective-permute-start.3 = (bf16[256,2048]{1,0:T(8,128)(2,1)}, bf16[256,2048]{1,0:T(8,128)(2,1)S(1)}, u32[]{:S(2)}, u32[]{:S(2)}) collective-permute-start(bf16[256,2048]{1,0:T(8,128)(2,1)} %get-tuple-element.96.z_own), channel_id=1, source_target_pairs={{0,1},{1,0},{2,3},{3,2},{4,5},{5,4},{6,7},{7,6},{8,9},{9,8},{10,11... | collective-permute-start | bytes 3145736 | tf_op jit(solution)/shard_map/ppermute | solution.py:810
  48.6 18.3 %all-to-all-start.1 = ((bf16[8,32,256]{2,1,0:T(8,128)(2,1)}), bf16[8,32,256]{2,1,0:T(8,128)(2,1)S(1)}, u32[]{:S(2)}, u32[]{:S(2)}) async-start(bf16[8,32,256]{2,1,0:T(8,128)(2,1)} %get-tuple-element.95), calls=%async_computation.1 | async-start | bytes 262144 | tf_op jit(solution)/shard_map/all_to_all | solution.py:813
  66.9 1.4 collective-permute-start.4
  74.8 6.2 %collective-permute-start.5 = (bf16[48,2048]{1,0:T(8,128)(2,1)}, bf16[48,2048]{1,0:T(8,128)(2,1)S(1)}, u32[]{:S(2)}, u32[]{:S(2)}) collective-permute-start(bf16[48,2048]{1,0:T(8,128)(2,1)} %get-tuple-element.100.z_own), channel_id=1, source_target_pairs={{0,1},{1,0},{2,3},{3,2},{4,5},{5,4},{6,7},{7,6},{8,9},{9,8},{10,11... | collective-permute-start | bytes 589832 | tf_op jit(solution)/shard_map/ppermute | solution.py:810
  75.0 17.6 %all-to-all-start.2 = ((bf16[8,32,128]{2,1,0:T(8,128)(2,1)}), bf16[8,32,128]{2,1,0:T(8,128)(2,1)S(1)}, u32[]{:S(2)}, u32[]{:S(2)}) async-start(bf16[8,32,128]{2,1,0:T(8,128)(2,1)} %get-tuple-element.99), calls=%async_computation.2 | async-start | bytes 131072 | tf_op jit(solution)/shard_map/all_to_all | solution.py:813
  92.6 1.3 collective-permute-start.6
  103.2 13.8 %collective-permute-start.7 = (f32[48,2048]{1,0:T(8,128)}, f32[48,2048]{1,0:T(8,128)S(1)}, u32[]{:S(2)}, u32[]{:S(2)}) collective-permute-start(f32[48,2048]{1,0:T(8,128)} %get-tuple-element.104), channel_id=1, source_target_pairs={{0,1},{1,0},{2,3},{3,2},{4,5},{5,4},{6,7},{7,6},{8,9},{9,8},{10,11... | collective-permute-start | bytes 1179656 | tf_op jit(solution)/shard_map/ppermute | solution.py:810
  103.4 13.6 %all-to-all-start.3 = ((f32[8,32,128]{2,1,0:T(8,128)}), f32[8,32,128]{2,1,0:T(8,128)S(1)}, u32[]{:S(2)}, u32[]{:S(2)}) async-start(f32[8,32,128]{2,1,0:T(8,128)} %get-tuple-element.103), calls=%async_computation.3 | async-start | bytes 262144 | tf_op jit(solution)/shard_map/all_to_all | solution.py:813
  117.0 1.4 collective-permute-start.8
  132.1 17.0 %collective-permute-start.9 = (f32[256,2048]{1,0:T(8,128)}, f32[256,2048]{1,0:T(8,128)S(1)}, u32[]{:S(2)}, u32[]{:S(2)}) collective-permute-start(f32[256,2048]{1,0:T(8,128)} %get-tuple-element.114), channel_id=1, source_target_pairs={{0,1},{1,0},{2,3},{3,2},{4,5},{5,4},{6,7},{7,6},{8,9},{9,8},{10,11... | collective-permute-start | bytes 6291464 | tf_op jit(solution)/shard_map/ppermute | solution.py:810
  132.4 16.8 %all-to-all-start.4 = ((f32[8,40,256]{2,1,0:T(8,128)}), f32[8,40,256]{2,1,0:T(8,128)S(1)}, u32[]{:S(2)}, u32[]{:S(2)}) async-start(f32[8,40,256]{2,1,0:T(8,128)} %get-tuple-element.113), calls=%async_computation.4 | async-start | bytes 655360 | tf_op jit(solution)/shard_map/all_to_all | solution.py:813
  149.1 1.6 collective-permute-start.10
  158.5 17.2 %all-to-all-start.5 = ((f32[8,48,256]{2,1,0:T(8,128)}), f32[8,48,256]{2,1,0:T(8,128)S(1)}, u32[]{:S(2)}, u32[]{:S(2)}) async-start(f32[8,48,256]{2,1,0:T(8,128)} %get-tuple-element.124), calls=%async_computation.5 | async-start | bytes 786432 | tf_op jit(solution)/shard_map/all_to_all | solution.py:813
  173.9 2.9 %collective-permute-start.12 = (f32[256,1024]{1,0:T(8,128)}, f32[256,1024]{1,0:T(8,128)S(1)}, u32[]{:S(2)}, u32[]{:S(2)}) collective-permute-start(f32[256,1024]{1,0:T(8,128)} %get-tuple-element.134), channel_id=1, source_target_pairs={{0,1},{1,0},{2,3},{3,2},{4,5},{5,4},{6,7},{7,6},{8,9},{9,8},{10,11... | collective-permute-start | bytes 3145736 | tf_op jit(solution)/shard_map/ppermute | solution.py:810
  175.7 1.7 collective-permute-start.11
  177.9 27.1 %copy-start.8 = (f32[256,47]{0,1:T(8,128)S(1)}, f32[256,47]{0,1:T(8,128)}, u32[]{:S(2)}) copy-start(f32[256,47]{0,1:T(8,128)} %param.40) | copy-start | bytes 144388
  177.9 27.1 %copy-start.9 = (f32[256,47]{0,1:T(8,128)S(1)}, f32[256,47]{0,1:T(8,128)}, u32[]{:S(2)}) copy-start(f32[256,47]{0,1:T(8,128)} %param.45) | copy-start | bytes 144388
  181.1 1.9 collective-permute-start.13
  181.3 3.9 %collective-permute-start.14 = (f32[64,128]{1,0:T(8,128)S(1)}, f32[64,128]{1,0:T(8,128)S(1)}, u32[]{:S(2)}, u32[]{:S(2)}) collective-permute-start(f32[64,128]{1,0:T(8,128)S(1)} %get-tuple-element.138), channel_id=1, source_target_pairs={{0,2},{1,3},{2,0},{3,1},{4,6},{5,7},{6,4},{7,5},{8,10},{9,11},{10,... | collective-permute-start | bytes 98312 | tf_op jit(solution)/shard_map/ppermute | solution.py:810
  182.8 3.4 %collective-permute-start.15 = (f32[64,128]{1,0:T(8,128)S(1)}, f32[64,128]{1,0:T(8,128)S(1)}, u32[]{:S(2)}, u32[]{:S(2)}) collective-permute-start(f32[64,128]{1,0:T(8,128)S(1)} %get-tuple-element.139), channel_id=1, source_target_pairs={{0,3},{1,2},{2,1},{3,0},{4,7},{5,6},{6,5},{7,4},{8,11},{9,10},{10,... | collective-permute-start | bytes 98312 | tf_op jit(solution)/shard_map/ppermute | solution.py:810
  (21 other events, 387.4 us)

commit v3 on v2

--- a/solution.py
+++ b/solution.py
@@ -22,6 +22,7 @@
 FINE = 256
 AHEAD = 3
 LIMIT = 52 << 20
+RESIDENT_BYTES = 30 << 20
 
 SMEM = pl.BlockSpec(memory_space=pltpu.SMEM)
 VMEM = pl.BlockSpec(memory_space=pltpu.VMEM)
@@ -200,7 +201,7 @@
     lane = lax.broadcasted_iota(I32, (halo, 128), 1)
     row = jnp.concatenate([total, jnp.zeros((halo, 128 - width), F32)], axis=1)
     for layer in range(3):
-        row = jnp.where(lane == FLAG_LANE + layer, changed[0, layer].astype(F32), row)
+        row = jnp.where(lane == FLAG_LANE + layer, changed[0:1, layer : layer + 1].astype(F32), row)
     row = jnp.where(lane == FLAG_LANE + 3, many, row)
     row = jnp.where(lane == FLAG_LANE + 4, count - 64.0 * many, row)
     rows_out[...] = row.astype(BF16).reshape(rows_out.shape)
@@ -234,16 +235,67 @@
     return packs[:, base : base + halo].astype(F32)
 
 
-def build_kernel(place, src_t, norm_t, high_hbm, rest_hbm, high, rest, out_sems):
+def table_kernel(place, pack, pack_one, pack_two, pack_three, feat_hbm, packs, most_out, table_hbm, feat_t, table, in_sems, out_sems):
+    width, nodes = feat_t.shape
+    steps = nodes // ROWS
+    blocks = Stream(in_sems, (feat_hbm, cols_at(ROWS), feat_t, cols_at(ROWS)))
+    stores = Stream(out_sems, (table, cols_at(ROWS), table_hbm, cols_at(ROWS)))
+    loop(steps, blocks.start)
+    for k, ref in enumerate((pack, pack_one, pack_two, pack_three)):
+        packs[span(jnp.bitwise_xor(place[0] + 2 * place[1], k) * 64, 64), :] = ref[...]
+    weight = packs[:, 0:width]
+
+    def step(i, most):
+        blocks.wait(i)
+        here = span(i * ROWS, ROWS)
+        z = dot_nn(weight, feat_t[:, here])
+        table[:, here] = z.astype(BF16)
+        stores.start(i)
+        return jnp.maximum(most, lane_most(z))
+
+    most = lax.fori_loop(0, steps, step, jnp.zeros((packs.shape[0], 128), F32))
+    most_out[...] = most
+    stores.wait_all(steps)
+
+
+def lane_most(value):
+    most = jnp.abs(value[:, 0:128])
+    for first in range(128, value.shape[1], 128):
+        most = jnp.maximum(most, jnp.abs(value[:, first : first + 128]))
+    return most
+
+
+def gelu_both(u):
+    square = u * u
+    t = jnp.tanh(0.79788456 * (u + 0.044715 * u * square))
+    half = 0.5 * (1.0 + t)
+    slope = half + 0.5 * u * (1.0 - t * t) * (0.79788456 * (1.0 + 3.0 * 0.044715 * square))
+    return u * half, slope
+
+
+def layer_one_kernel(place, src_t, norm_t, rows, send, most, packs_hbm, table_hbm, z_send, flags_t, high_hbm, rest_hbm, hidden_hbm, slope_hbm, z_hbm, packs, table, table8, high, rest, hidden_t, slope_t, z_own, in_sems, edge_sems, out_sems):
     slots = src_t.shape[0]
-    half = src_t.shape[1] // 2
+    units, half = hidden_t.shape
+    nodes = 2 * half
+    halo = send.shape[0]
     blocks = high.shape[1] // 256
     per_group = 256 // slots
+    steps = half // FINE
+    fetch = Stream(in_sems, (packs_hbm, all_of, packs, all_of), (table_hbm, all_of, table, lambda i: (slice(None), slice(0, nodes))))
+    fetch.start(0)
+    depth = high.shape[0] // FINE
+    around = lambda i, count: i if depth >= steps else lax.rem(i, count)
+    slot_of = lambda i: span(around(i, depth) * FINE, FINE)
+    slot_at = lambda i: (slot_of(i), slice(None))
+    edge_stores = Stream(edge_sems, (high, slot_at, high_hbm, rows_at(FINE)), (rest, slot_at, rest_hbm, rows_at(FINE)))
+    stores = Stream(
+        out_sems,
+        *[(a, cols_at(FINE), b, cols_at(FINE)) for a, b in ((hidden_t, hidden_hbm), (slope_t, slope_hbm), (z_own, z_hbm))],
+    )
     in_slot = lax.broadcasted_iota(I32, (8, 128), 1) // per_group == lax.broadcasted_iota(I32, (8, 128), 0)
     node_row = lax.broadcasted_iota(I32, (per_group, 256), 0)
     mine = lax.rem(lax.broadcasted_iota(I32, (per_group, 256), 1), per_group) == node_row
     inner = lax.broadcasted_iota(I32, (256, 256), 0)
-    stores = Stream(out_sems, (high, rows_at(128), high_hbm, rows_at(128)), (rest, rows_at(128), rest_hbm, rows_at(128)))
 
     def lean(tile):
         return [
@@ -268,7 +320,7 @@
         )
         return dot_nt(left, right), dot_nt(left, right_rest)
 
-    def step(i):
+    def build(i):
         here = span(place[0] * half + i * 128, 128)
         at, weight = src_t[:, here], norm_t[:, here]
         slot = lax.broadcasted_iota(I32, at.shape, 0)
@@ -279,79 +331,79 @@
             repeat = repeat | (same & (slot >= shift))
         source, weights = lean(at), lean(jnp.where(repeat, 0.0, merged))
         pairs = [one(flat(source, group), flat(weights, group)) for group in range(128 // per_group)]
-        rows = span(i * 128, 128)
+        rows = span(around(i, high.shape[0] // 128) * 128, 128)
         for j in range(blocks):
             cols = slice(256 * j, 256 * (j + 1))
             for ref, parts in zip((high, rest), zip(*pairs)):
                 piece = jnp.concatenate([p[per_group * j : per_group * (j + 1), :] for p in parts], axis=0)
                 ref[rows, cols] = piece.astype(ref.dtype)
+
+    def build_block(i):
+        for k in range(FINE // 128):
+            build(i * (FINE // 128) + k)
+        edge_stores.start(i)
+
+    flat_rows = rows[...].reshape(halo, 128)
+    flags = flat_rows.astype(F32).T[FLAG_LANE : FLAG_LANE + 8, :]
+    counts = jnp.sum(rows[...].astype(F32)[:, 0, :], axis=0, keepdims=True)
+    count = 64.0 * counts[:, FLAG_LANE + 3 : FLAG_LANE + 4] + counts[:, FLAG_LANE + 4 : FLAG_LANE + 5]
+    row = lax.broadcasted_iota(I32, flags.shape, 0)
+    flags_t[...] = jnp.where(row == 3, count, flags)
+    z_send[...] = jnp.zeros(z_send.shape, BF16)
+    loop(FINE // 128, build)
+    edge_stores.start(0)
+    fetch.wait(0)
+    border = dot_nt(packs[:, 0:FLAG_LANE], flat_rows[:, 0:FLAG_LANE]).astype(BF16).astype(F32)
+    border = jnp.where(flags[0:1, :] == 1.0, border, stale_columns(packs, 0, halo))
+    table[:, nodes : nodes + halo] = border.astype(BF16)
+    scale, back = scale_of(jnp.maximum(jnp.max(most[...]), jnp.max(jnp.abs(border))))
+    back = back * (1.0 / REST_GAIN)
+    bias = bias_column(packs, 0)
+
+    def small(i):
+        here = span(i * 256, 256)
+        table8[:, here] = (table[:, here].astype(F32) * scale).astype(F8)
+
+    loop((nodes + halo) // 256, small)
+
+    def sums(i):
+        here = slot_of(i)
+        return dot_nt(table[...], high[here, :]) + dot_nt(table8[...], rest[here, :]) * back
+
+    def finish(i):
+        here = span(i * FINE, FINE)
+        value, slope = gelu_both(slope_t[:, here] + bias)
+        value = value.astype(BF16)
+        hidden_t[:, here] = value
+        slope_t[:, here] = slope
+        z = dot_nn(packs[:, 128 : 128 + units], value).astype(BF16)
+        z_own[:, here] = z
         stores.start(i)
-
-    loop(half // 128, step)
-    stores.wait_all(half // 128)
-
-
-def gelu_both(u):
-    square = u * u
-    t = jnp.tanh(0.79788456 * (u + 0.044715 * u * square))
-    half = 0.5 * (1.0 + t)
-    slope = half + 0.5 * u * (1.0 - t * t) * (0.79788456 * (1.0 + 3.0 * 0.044715 * square))
-    return u * half, slope
-
-
-def layer_one_kernel(place, rows, feat_t, pack, pack_one, pack_two, pack_three, send, high, rest, packs, hidden_t, slope_t, z_own, z_send, flags_t, table, table8, back, hbuf, rbuf, sems):
-    width, nodes = feat_t.shape
-    halo = send.shape[0]
-    step = pl.program_id(0)
-    ring = Ring((high, rest), (hbuf, rbuf), sems, lambda i: (span(i * ROWS, ROWS), slice(None)))
-    ring.begin()
-
-    @pl.when(step == 0)
-    def _():
-        for k, ref in enumerate((pack, pack_one, pack_two, pack_three)):
-            packs[span(jnp.bitwise_xor(place[0] + 2 * place[1], k) * 64, 64), :] = ref[...]
-        weight = packs[:, 0:width]
-        flat = rows[...].reshape(halo, 128)
-        flags = flat.astype(F32).T[FLAG_LANE : FLAG_LANE + 8, :]
-        counts = jnp.sum(rows[...].astype(F32)[:, 0, :], axis=0, keepdims=True)
-        count = 64.0 * counts[:, FLAG_LANE + 3 : FLAG_LANE + 4] + counts[:, FLAG_LANE + 4 : FLAG_LANE + 5]
-        row = lax.broadcasted_iota(I32, flags.shape, 0)
-        flags_t[...] = jnp.where(row == 3, count, flags)
-
-        def first(i, most):
-            here = span(i * ROWS, ROWS)
-            z = dot_nn(weight, feat_t[:, here])
-            table[:, here] = z.astype(BF16)
-            return jnp.maximum(most, jnp.abs(z))
-
-        most = lax.fori_loop(0, nodes // ROWS, first, jnp.zeros((table.shape[0], ROWS), F32))
-        border = dot_nt(weight, flat[:, 0:width]).astype(BF16).astype(F32)
-        border = jnp.where(flags[0:1, :] == 1.0, border, stale_columns(packs, 0, halo))
-        table[:, nodes : nodes + halo] = border.astype(BF16)
-        scale, inverse = scale_of(jnp.maximum(jnp.max(most), jnp.max(jnp.abs(border))))
-        back[0] = inverse * (1.0 / REST_GAIN)
-
-        def small(i, carry):
-            here = span(i * 256, 256)
-            table8[:, here] = (table[:, here].astype(F32) * scale).astype(F8)
-            return carry
-
-        lax.fori_loop(0, (nodes + halo) // 256, small, 0)
-        z_send[...] = jnp.zeros(z_send.shape, BF16)
-
-    units = packs.shape[0]
-    top, low = ring.wait()
-    total = dot_nt(table[...], top[...]) + dot_nt(table8[...], low[...]) * back[0]
-    ring.end()
-    value, slope = gelu_both(total + bias_column(packs, 0))
-    value = value.astype(BF16)
-    hidden_t[...] = value
-    slope_t[...] = slope
-    z = dot_nn(packs[:, 128 : 128 + units], value).astype(BF16)
-    z_own[...] = z
-    half = nodes // 2
-    chosen = dot_nt(pick_rows(send[...], place[0] * half + step * ROWS, ROWS), z)
-    z_send[...] = (z_send[...].astype(F32) + chosen.reshape(z_send.shape)).astype(BF16)
+        chosen = dot_nt(pick_rows(send[...], place[0] * half + i * FINE, FINE), z)
+        z_send[...] = (z_send[...].astype(F32) + chosen.reshape(z_send.shape)).astype(BF16)
+
+    def step(i, carry):
+        if depth < steps:
+
+            @pl.when(i + 1 >= depth)
+            def _():
+                edge_stores.wait(i + 1 - depth)
+
+        total = sums(i)
+        finish(i - 1)
+        build_block(i + 1)
+        slope_t[:, span(i * FINE, FINE)] = total
+        return carry
+
+    slope_t[:, 0:FINE] = sums(0)
+    build_block(1)
+    lax.fori_loop(1, steps - 1, step, 0)
+    slope_t[:, span((steps - 1) * FINE, FINE)] = sums(steps - 1)
+    finish(steps - 2)
+    finish(steps - 1)
+    stores.wait_all(steps)
+    for i in range(steps - depth, steps):
+        edge_stores.wait(i)
 
 
 def own_part_kernel(place, high, rest, z_own, z_oth, total, table, table8, back, hbuf, rbuf, sems):
@@ -442,13 +494,14 @@
         (rest, cut, rrows, rows_at(ROWS)),
         (total_hbm, cols_at(ROWS), total, cols_at(ROWS)),
     )
-    others = cols_at(ROWS, (1 - place[0]) * half)
-    edges = Stream(edge_sems, (high, others, hbuf, cols_at(ROWS)), (rest, others, rbuf, cols_at(ROWS)))
+    others = rows_at(ROWS, span((1 - place[0]) * half, half))
+    edges = Stream(edge_sems, (high, others, hbuf, rows_at(ROWS)), (rest, others, rbuf, rows_at(ROWS)))
     stores = Stream(
         out_sems, *[(a, cols_at(ROWS), b, cols_at(ROWS)) for a, b in ((grads, grads_hbm), (grads8, grads8_hbm))]
     )
-    far_stores = Stream(far_sems, (far, cols_at(ROWS), far_hbm, cols_at(ROWS)))
+    far_stores = Stream(far_sems, (far, all_of, far_hbm, all_of))
     blocks.start_first(steps)
+    edges.start(0)
     both = came[...].reshape(halo, 128).astype(F32) + came_oth[...].reshape(halo, 128).astype(F32)
     old = jnp.concatenate([stale_t[...].astype(F32), jnp.zeros((kinds - classes, halo), F32)], axis=0)
     value = jnp.where(flags_t[2:3, :] == 1.0, both.T[0:kinds, :], old)
@@ -464,9 +517,14 @@
     inverse = (1.0 / (256.0 * REST_GAIN)) / count
     back_out[...] = jnp.broadcast_to(inverse, back_out.shape)
 
+    def far_step(i):
+        edges.wait(i)
+        here = span(i * ROWS, ROWS)
+        both = dot_nn(grads[:, here], hbuf[here, :])
+        low = dot_nn(grads8[:, here], rbuf[here, :]) * inverse
+        far[...] += both[0:kinds] + both[kinds : 2 * kinds] + low
+
     def step(i):
-        blocks.next(i, steps)
-        edges.start(i)
         here = span(i * ROWS, ROWS)
         logits = total[:, here] + dot_nt(border, hrows[here, :]) + dot_nt(border8, rrows[here, :]) * back
         logits = logits + bias_col
@@ -496,19 +554,27 @@
         low = dot_nn(small, rrows[here, :]) * inverse
         border_sum[0:kinds, :] += both[0:kinds] + both[kinds : 2 * kinds] + low
 
-    loop(steps, step)
+    far[...] = jnp.zeros(far.shape, F32)
+    blocks.next(0, steps)
+    edges.start(1)
+    step(0)
+
+    def both_steps(i):
+        blocks.next(i, steps)
+
+        @pl.when(i + 1 < steps)
+        def _():
+            edges.start(i + 1)
+
+        far_step(i - 1)
+        step(i)
+
+    lax.fori_loop(1, steps, lambda i, c: (both_steps(i), c)[1], 0)
+    far_step(steps - 1)
+    far_stores.start(0)
     put_border(border_grad, border_sum[...], flags_t[2:3, :])
-
-    def far_step(i):
-        edges.wait(i)
-        here = span(i * ROWS, ROWS)
-        both = dot_nn(grads[...], hbuf[:, here])
-        far[:, here] = both[0:kinds] + both[kinds : 2 * kinds] + dot_nn(grads8[...], rbuf[:, here]) * inverse
-        far_stores.start(i)
-
-    loop(steps, far_step)
     stores.wait_all(steps)
-    far_stores.wait_all(steps)
+    far_stores.wait(0)
 
 
 def lane_sums(value):
@@ -530,8 +596,8 @@
 
 
 def back_block(grads, grads8, tails8, back_rest, back_tail, top, low):
-    total = dot_nn(grads[...], top) + dot_nn(grads8[...], low) * back_rest
-    return total + dot_nn(tails8[...], top.astype(F8)) * back_tail
+    total = dot_nn(grads, top) + dot_nn(grads8, low) * back_rest
+    return total + dot_nn(tails8, top.astype(F8)) * back_tail
 
 
 def back_kernel(halves, place, high, rest, grads, grads8, tails8, back, *refs):
@@ -547,7 +613,7 @@
     ring = Ring((high, rest), (hbuf, rbuf), sems, cut)
     ring.begin()
     top, low = ring.wait()
-    total = back_block(grads, grads8, tails8, back[0:1, 0:1], back[0:1, 1:2], top[...], low[...])
+    total = back_block(grads[...], grads8[...], tails8[...], back[0:1, 0:1], back[0:1, 1:2], top[...], low[...])
     for k, out in enumerate(outs):
 
         @pl.when((ring.step >= k * steps) & (ring.step < (k + 1) * steps))
@@ -572,7 +638,7 @@
     return total.astype(BF16)
 
 
-def end_kernel(layer, place, flags_t, ret, ret_oth, weight_ref, send, far_in_any, near_hbm, hidden_hbm, slope_hbm, high, rest, sums, back_out, border_grad, chunk_out, grads_hbm, grads8_hbm, tails8_hbm, *more):
+def end_kernel(layer, place, flags_t, ret, ret_oth, weight_ref, send, far_in_any, near_hbm, hidden_hbm, slope_hbm, high, rest, sums, back_out, border_grad, grads_hbm, grads8_hbm, tails8_hbm, *more):
     if layer == 1:
         far_hbm, far, hbuf, rbuf, edge_sems, far_sems = more[0], *more[-5:]
         more = more[1:-5]
@@ -604,21 +670,22 @@
         others = cols_at(ROWS, (1 - place[0]) * half)
         edges = Stream(edge_sems, (high, others, hbuf, cols_at(ROWS)), (rest, others, rbuf, cols_at(ROWS)))
         far_stores = Stream(far_sems, (far, cols_at(ROWS), far_hbm, cols_at(ROWS)))
-    blocks.start_first(steps)
+    loop(steps, blocks.start)
+    loop(steps, borders.start)
+    if layer == 1:
+        loop(steps, edges.start)
     terms = returned_terms(ret, ret_oth, bound, kinds)
     if layer == 0:
-        chunk_out[...] = jnp.sum(ret[:, bound:, :] + ret_oth[:, bound:, :], axis=0)
+        chunk = jnp.sum(ret[:, bound:, :] + ret_oth[:, bound:, :], axis=0)
         weight = weight_ref[:, 128 : 128 + units]
     else:
-        chunk_out[...] = jnp.zeros(chunk_out.shape, F32)
         weight = padded_rows(weight_ref, kinds)
     sums[...] = jnp.zeros(sums.shape, F32)
     grad_weight[...] = jnp.zeros(grad_weight.shape, F32)
     border_sum[...] = jnp.zeros(border_sum.shape, F32)
 
     def first_step(i, most):
-        blocks.next(i, steps)
-        borders.start(i)
+        blocks.wait(i)
         here = span(i * ROWS, ROWS)
         d_z = round_gradient(near[:, here], far_in[:, here], terms, send[...], (place[0] * steps + i) * ROWS)
         grad_weight[0:kinds, :] += dot_nt(d_z, hidden_t[:, here])
@@ -628,8 +695,6 @@
         return jnp.maximum(most, jnp.max(jnp.abs(grad), axis=0, keepdims=True))
 
     most = lax.fori_loop(0, steps, first_step, jnp.zeros((1, ROWS), F32))
-    if layer == 1:
-        edges.start_first(steps)
     scale, back = scale_of(most)
     back_rest, back_tail = back * (1.0 / REST_GAIN), back * (1.0 / TAIL_GAIN)
     lane = lax.broadcasted_iota(I32, back_out.shape, 1)
@@ -658,11 +723,14 @@
             block = grad_weight[span(place[1] * 128 + core * 64, 64), :]
             first = bound + core * size
             border_grad[:, first : first + size, :] = block.reshape(parts, size, units)
+        border_grad[:, bound + 2 * size :, :] = jnp.broadcast_to(chunk[None], (parts, size, units))
 
     def far_step(i):
-        edges.next(i, steps)
+        edges.wait(i)
         here = span(i * ROWS, ROWS)
-        far[:, here] = back_block(grads, grads8, tails8, back_rest, back_tail, hbuf[:, here], rbuf[:, here])
+        far[:, here] = back_block(
+            grads[...], grads8[...], tails8[...], back_rest, back_tail, hbuf[:, here], rbuf[:, here]
+        )
         far_stores.start(i)
 
     if layer == 1:
@@ -671,7 +739,7 @@
     stores.wait_all(steps)
 
 
-def end_one_kernel(place, ret, ret_oth, send, sums_one, sums_two, sums_out, far_any, near_hbm, feat_hbm, out, out_one, out_two, out_three, second_chunk, near, far, feat_t, grad_first, in_sems):
+def end_one_kernel(place, ret, ret_oth, send, sums_one, sums_two, sums_out, far_any, near_hbm, feat_hbm, out, out_one, out_two, out_three, second_chunk, grad_last, near, far, feat_t, grad_first, in_sems):
     units, size = near.shape
     parts = ret.shape[0]
     bound = send.shape[0] // parts
@@ -689,6 +757,7 @@
     terms = returned_terms(ret, ret_oth, bound, units)
     mine = pl.ds(bound + place[0] * chunk, chunk)
     second_chunk[...] = jnp.sum(ret[:, mine, :] + ret_oth[:, mine, :], axis=0)
+    grad_last[...] = ret[:, bound + 2 * chunk :, :].reshape(64, units)
     grad_first[...] = jnp.zeros(grad_first.shape, F32)
 
     def step(i):
@@ -709,13 +778,9 @@
         ref[...] = jnp.where(lane == FLAG_LANE + 2, column(sums_out[...]), value)
 
 
-def gather_kernel(mine, one, two, three, second_chunk, last_chunk, out):
+def gather_kernel(mine, one, two, three, second_chunk, out):
     total = mine[...] + one[...] + two[...] + three[...]
-    size = second_chunk.shape[0]
-    parts = [total]
-    for chunk in (second_chunk, last_chunk):
-        parts += [chunk[:, 0:128], chunk[:, 128:256]]
-    value = jnp.concatenate(parts, axis=0)
+    value = jnp.concatenate([total, second_chunk[:, 0:128], second_chunk[:, 128:256]], axis=0)
     for p in range(out.shape[0]):
         out[p] = value
 
@@ -731,24 +796,19 @@
     return (weight, moment, square)
 
 
-def update_kernel(came, flags_t, *refs):
+def update_kernel(came, grad_last, flags_t, *refs):
     params, outs = refs[0:15], refs[15:]
     parts = came.shape[0]
     size = 64 // parts
     width, kinds = params[0].shape[1], params[6].shape[0]
     total = jnp.sum(came[:, 0:64, :], axis=0)
 
-    def chunks(first):
-        halves = [
-            came[:, first + k * size : first + (k + 1) * size, :].reshape(64, 128) for k in range(2)
-        ]
-        return jnp.concatenate(halves, axis=1)
-
+    halves = [came[:, 64 + k * size : 64 + (k + 1) * size, :].reshape(64, 128) for k in range(2)]
     turned = jnp.concatenate([total, jnp.zeros((64, 128), F32)], axis=0).T
     gradients = (
         total[:, 0:width],
-        chunks(64),
-        chunks(64 + 2 * size)[0:kinds, :],
+        jnp.concatenate(halves, axis=1),
+        grad_last[0:kinds, :],
         turned[FLAG_LANE : FLAG_LANE + 2, 0:64],
         turned[FLAG_LANE + 2 : FLAG_LANE + 3, 0:kinds],
     )
@@ -825,7 +885,7 @@
         [
             whole(feat_t),
             whole(send_rows.reshape(parts, bound)),
-            (changed.T, SMEM),
+            whole(changed.T),
             *[whole(a) for a in (mask_rows, first_weight.T, second_weight.T)],
             *[whole(a) for a in (jnp.transpose(cache_hidden, (0, 2, 1)), hidden_bias)],
         ],
@@ -842,32 +902,50 @@
     node_block = lambda size, rows: pl.BlockSpec((rows, size), lambda i: (0, i))
     block, fine_block = node_block(ROWS, units), node_block(FINE, units)
     scalar = pltpu.SMEM((1,), F32)
-    high, rest = run(
-        build_kernel,
-        "build",
-        [where, *placed(OWN, edge_src.T, edge_norm.T)],
-        [((half, table), BF16, HBM), ((half, table), F8, HBM)],
-        [vm((half, table), BF16), vm((half, table), F8), sems(2, half // 128)],
-        flops=4 * 256 * table * half,
-    )
-    edge = placed(HBM, high, rest)
-
-    packs, hidden_one, slope_one, z_own, z_send, flags_t = run(
+    packs, most, first_table = run(
+        table_kernel,
+        "table",
+        [where, *placed(VMEM, *packs), (feat_t, HBM)],
+        [((units, pack_width), BF16, OWN), ((units, 128), F32, VMEM), ((units, nodes), BF16, HBM)],
+        [
+            vm((in_width, nodes), BF16),
+            vm((units, nodes), BF16),
+            sems(1, nodes // ROWS),
+            sems(1, nodes // ROWS),
+        ],
+        flops=2 * units * nodes * in_width,
+    )
+    rows, most = late(most, rows)
+    held = fine if half * table * 3 <= RESIDENT_BYTES else min(fine, 4)
+    z_send, flags_t, high, rest, hidden_one, slope_one, z_own = run(
         layer_one_kernel,
         "layer_one",
-        [where, *placed(VMEM, rows), whole(feat_t), *placed(VMEM, *packs, send), *edge],
+        [where, *placed(OWN, edge_src.T, edge_norm.T), *placed(VMEM, rows, send, most), *placed(HBM, packs, first_table)],
         [
-            ((units, pack_width), BF16, whole_spec((units, pack_width))),
-            ((units, half), BF16, block),
-            ((units, half), F32, block),
-            ((units, half), BF16, block),
-            ((parts, bound, units), BF16, whole_spec((parts, bound, units))),
-            ((8, halo), F32, whole_spec((8, halo))),
-        ],
-        [vm((units, table), BF16), vm((units, table), F8), scalar, *ring_scratch((ROWS, table), 2)],
-        flops=work,
-        grid=(steps,),
-    )
+            ((parts, bound, units), BF16, VMEM),
+            ((8, halo), F32, OWN),
+            ((half, table), BF16, HBM),
+            ((half, table), F8, HBM),
+            ((units, half), BF16, HBM),
+            ((units, half), F32, HBM),
+            ((units, half), BF16, HBM),
+        ],
+        [
+            vm((units, pack_width), BF16),
+            vm((units, table), BF16),
+            vm((units, table), F8),
+            vm((held * FINE, table), BF16),
+            vm((held * FINE, table), F8),
+            vm((units, half), BF16),
+            vm((units, half), F32),
+            vm((units, half), BF16),
+            sems(2, 1),
+            sems(2, fine),
+            sems(3, fine),
+        ],
+        flops=2 * work,
+    )
+    edge = placed(HBM, high, rest)
 
     def own_part(z_own, z_oth, name):
         n = z_own.shape[0]
@@ -938,7 +1016,7 @@
             sems(3, steps),
             sems(2, steps),
             sems(2, steps),
-            sems(1, steps),
+            sems(1, 1),
         ],
         flops=work,
     )
@@ -973,8 +1051,7 @@
             [
                 ((units, 128), F32, VMEM),
                 ((8, 128), F32, VMEM),
-                ((parts, bound + (1 if with_far else 2) * chunk, units), F32, VMEM),
-                ((chunk, units), F32, VMEM),
+                ((parts, bound + (1 if with_far else 3) * chunk, units), F32, VMEM),
                 ((units, half), BF16, HBM),
                 ((units, half), F8, HBM),
                 ((units, half), F8, HBM),
@@ -1017,7 +1094,7 @@
             grid=(fine,),
         )
 
-    sums_two, back, border_grad, _, grads, grads8, tails8, far = end(
+    sums_two, back, border_grad, grads, grads8, tails8, far = end(
         1, "end_three", ret, ret_oth, last_t, near, far, hidden_two, slope_two
     )
     far = swap(far)
@@ -1025,7 +1102,7 @@
     near = back_part(1, back, grads, grads8, tails8)[0]
     ret, far, near = late(near, ret, far)
     ret_oth = swap(ret)
-    sums_one, back, border_grad, last_chunk, grads, grads8, tails8 = end(
+    sums_one, back, border_grad, grads, grads8, tails8 = end(
         0, "end_two", ret, ret_oth, packs, near, far, hidden_one, slope_one
     )
     ret = exchange(border_grad)
@@ -1033,11 +1110,11 @@
     far = swap(far)
     ret, near = late(near, ret)
     ret_oth = swap(ret)
-    *pieces, second_chunk = run(
+    *pieces, second_chunk, grad_last = run(
         end_one_kernel,
         "end_one",
         [where, *placed(VMEM, ret, ret_oth, send, sums_one, sums_two, sums_out), (far, ANY), *placed(HBM, near, feat_t)],
-        [((64, 128), F32, VMEM)] * 4 + [((chunk, units), F32, VMEM)],
+        [((64, 128), F32, VMEM)] * 4 + [((chunk, units), F32, VMEM), ((64, units), F32, VMEM)],
         [
             vm((units, half // 2), F32),
             vm((units, half // 2), F32),
@@ -1051,8 +1128,8 @@
     gathered = run(
         gather_kernel,
         "gather",
-        placed(VMEM, *pieces, second_chunk, last_chunk),
-        [((parts, 64 + 4 * chunk, 128), F32, VMEM)],
+        placed(VMEM, *pieces, second_chunk),
+        [((parts, 64 + 2 * chunk, 128), F32, VMEM)],
     )[0]
     came = exchange(gathered)
 
@@ -1067,7 +1144,7 @@
     outs = run(
         update_kernel,
         "update",
-        placed(VMEM, came, flags_t, *params),
+        placed(VMEM, came, grad_last, flags_t, *params),
         [(p.shape, F32, VMEM) for p in params] + [((1, 128), F32, VMEM)] * 2,
     )
     undo = (turn, turn, turn, same, lambda x: x.reshape(-1))

time: 207 us -> 200 us (0.966)
  Pallas kernels: 131 us -> 125 us
  waiting for transfers between devices: 12.8 us -> 16.3 us
  blocking collectives: 18.6 us -> 15.9 us
    pallas_call x15, Pallas kernels: 131 us -> 125 us  [run(): pl.pallas_call(kernel, grid=grid, in_specs=[spec for _, spec in args], ou...]
    all_to_all x6, waiting for transfers between devices: 2.6 us -> 5.88 us  [exchange(): return lax.all_to_all(x, 'dom', split_axis=0, concat_axis=0, tiled=True)]
    all_to_all x1, blocking collectives: 18.6 us -> 15.9 us  [exchange(): return lax.all_to_all(x, 'dom', split_axis=0, concat_axis=0, tiled=True)]
  transfers between devices with their start and end apart: 22 -> 22, of which waited for: 10 -> 11; matrix products, arithmetic and copies ran while one was open for 0% -> 0% of each run, Pallas kernels for 34% -> 28%
where the time goes in v3:
time: 200 us; the launch traced here: 199 us
  Pallas kernels  125 us (62%)
  starting transfers between devices  40.3 us (20%)
  waiting for transfers between devices  16.3 us (8%)
  blocking collectives  15.9 us (8%)
    pallas_call x15, Pallas kernels, run(): pl.pallas_call(kernel, grid=grid, in_specs=[spec for _, spec in args], ou...  125 us
    all_to_all x6, starting transfers between devices, exchange(): return lax.all_to_all(x, 'dom', split_axis=0, concat_axis=0, tiled=True)  33.9 us
    all_to_all x1, blocking collectives, exchange(): return lax.all_to_all(x, 'dom', split_axis=0, concat_axis=0, tiled=True)  15.9 us
    ppermute x16, waiting for transfers between devices, swap(): return lax.ppermute(x, 'rep', [(i, i ^ k) for i in range(reps)])  10.4 us
    ppermute x16, starting transfers between devices, swap(): return lax.ppermute(x, 'rep', [(i, i ^ k) for i in range(reps)])  6.34 us
    all_to_all x6, waiting for transfers between devices, exchange(): return lax.all_to_all(x, 'dom', split_axis=0, concat_axis=0, tiled=True)  5.88 us
  transfers between devices with their start and end apart: 22, of which 11 were waited for; matrix products, arithmetic and copies ran while one was open for 0% of the time, Pallas kernels for 28%

profile of v3, /device:TPU:0, one launch (start us, length us, event | category | flops | bytes accessed | tf_op | source)
XLA Modules:
  0.0 198.8 jit_solution(15564032694595596131)
XLA Ops:
  0.7 4.4 %pack.1 = (bf16[8,32,128]{2,1,0:T(8,128)(2,1)}, bf16[64,1024]{1,0:T(8,128)(2,1)S(1)}, s32[256,1]{1,0:T(8,128)S(1)}) custom-call(bf16[100,4096]{1,0:T(8,128)(2,1)} %bitcast.60, s32[8,32]{1,0:T(8,128)} %bitcast.64, s32[1,3]{1,0:T(1,128)} %bitcast.65, s32[32,128]{1,0:T(8,128)} %bitcast.48, f32[64,100]{1,0:T(8,128)} %bitcast.44, f32[64,256]{1,0:T(8,128)} %bitcast.42, ...), custom_call_target="tpu_custom_call" | custom-call | flops 268435456 | bytes 1048576 | tf_op jit(solution)/shard_map/pack/pallas_call | solution.py:47
  5.0 2.4 %collective-permute-start.2 = (bf16[64,1024]{1,0:T(8,128)(2,1)S(1)}, bf16[64,1024]{1,0:T(8,128)(2,1)S(1)}, u32[]{:S(2)}, u32[]{:S(2)}) collective-permute-start(bf16[64,1024]{1,0:T(8,128)(2,1)S(1)} %get-tuple-element.93.pack), channel_id=1, source_target_pairs={{0,3},{1,2},{2,1},{3,0},{4,7},{5,6},{6,5},{7,4},{8,11},{9,10},{10,... | collective-permute-start | bytes 393224 | tf_op jit(solution)/shard_map/ppermute | solution.py:870
  8.1 6.0 %all-to-all-start = ((bf16[8,32,128]{2,1,0:T(8,128)(2,1)}), bf16[8,32,128]{2,1,0:T(8,128)(2,1)S(1)}, u32[]{:S(2)}, u32[]{:S(2)}) async-start(bf16[8,32,128]{2,1,0:T(8,128)(2,1)} %get-tuple-element.92), calls=%async_computation | async-start | bytes 131072 | tf_op jit(solution)/shard_map/all_to_all | solution.py:873
  14.3 4.9 %table.1 = (bf16[256,1024]{1,0:T(8,128)(2,1)}, f32[256,128]{1,0:T(8,128)S(1)}, bf16[256,4096]{1,0:T(8,128)(2,1)}) custom-call(s32[2]{0:T(128)S(1)} %pad_add_fusion.place, bf16[64,1024]{1,0:T(8,128)(2,1)S(1)} %get-tuple-element.93.pack, bf16[64,1024]{1,0:T(8,128)(2,1)S(1)} %collective-permute-done.pack_one, ...), custom_call_target="tpu_custom_call" | custom-call | flops 209715200 | bytes 1048576 | tf_op jit(solution)/shard_map/table/pallas_call | solution.py:47
  19.2 1.9 all-to-all-done.rows
  21.1 25.3 %layer_one.1 = (bf16[8,32,256]{2,1,0:T(8,128)(2,1)}, f32[8,256]{1,0:T(8,128)}, bf16[2048,4352]{1,0:T(8,128)(2,1)}, f8e4m3fn[2048,4352]{1,0:T(32,128)(4,1)}, bf16...) custom-call(s32[2]{0:T(128)S(1)} %pad_add_fusion.place, s32[16,4096]{1,0:T(8,128)} %bitcast.66, ...), custom_call_target="tpu_custom_call" | custom-call | flops 9126805504 | bytes 1048576 | tf_op jit(solution)/shard_map/layer_one/pallas_call | solution.py:47
  46.4 4.8 %all-to-all-start.1 = ((bf16[8,32,256]{2,1,0:T(8,128)(2,1)}), bf16[8,32,256]{2,1,0:T(8,128)(2,1)S(1)}, u32[]{:S(2)}, u32[]{:S(2)}) async-start(bf16[8,32,256]{2,1,0:T(8,128)(2,1)} %get-tuple-element.103), calls=%async_computation.1 | async-start | bytes 262144 | tf_op jit(solution)/shard_map/all_to_all | solution.py:873
  51.2 12.2 %layer_two_own.1.total = f32[256,2048]{1,0:T(8,128)} custom-call(s32[2]{0:T(128)S(1)} %pad_add_fusion.place, bf16[2048,4352]{1,0:T(8,128)(2,1)} %get-tuple-element.101.high, f8e4m3fn[2048,4352]{1,0:T(32,128)(4,1)} %get-tuple-element.102.rest, bf16[256,2048]{1,0:T(8,128)(2,1)} %get-tuple-element.104.z_own, bf16[256,2048]{1,0:T(8,128)(2,1)S(1)} %collective-permute-done.3.z_oth), custom_call_target="tpu_custom_call" | custom-call | flops 4563402752 | bytes 1048576 | tf_op jit(solution)/shard_map/layer_two_own/pallas_call | solution.py:47
  64.8 6.4 %layer_two_end.1 = (bf16[256,2048]{1,0:T(8,128)(2,1)}, f32[256,2048]{1,0:T(8,128)}, bf16[48,2048]{1,0:T(8,128)(2,1)}, bf16[8,32,128]{2,1,0:T(8,128)(2,1)}) custom-call(s32[2]{0:T(128)S(1)} %pad_add_fusion.place, f32[8,256]{1,0:T(8,128)} %get-tuple-element.100.flags_t, bf16[256,1024]{1,0:T(8,128)(2,1)} %get-tuple-element.98.packs_hbm.packs.weight_ref, ...), custom_call_target="tpu_custom_call" | custom-call | flops 1140850688 | bytes 1048576 | tf_op jit(solution)/shard_map/layer_two_end/pallas_call | solution.py:47
  71.4 6.0 %all-to-all-start.2 = ((bf16[8,32,128]{2,1,0:T(8,128)(2,1)}), bf16[8,32,128]{2,1,0:T(8,128)(2,1)S(1)}, u32[]{:S(2)}, u32[]{:S(2)}) async-start(bf16[8,32,128]{2,1,0:T(8,128)(2,1)} %get-tuple-element.107), calls=%async_computation.2 | async-start | bytes 131072 | tf_op jit(solution)/shard_map/all_to_all | solution.py:873
  77.5 11.5 %layer_three_own.1.total_hbm = f32[48,2048]{1,0:T(8,128)} custom-call(s32[2]{0:T(128)S(1)} %pad_add_fusion.place, bf16[2048,4352]{1,0:T(8,128)(2,1)} %get-tuple-element.101.high, f8e4m3fn[2048,4352]{1,0:T(32,128)(4,1)} %get-tuple-element.102.rest, bf16[48,2048]{1,0:T(8,128)(2,1)} %get-tuple-element.108.z_own, bf16[48,2048]{1,0:T(8,128)(2,1)S(1)} %collective-permute-done.5.z_oth), custom_call_target="tpu_custom_call" | custom-call | flops 4563402752 | bytes 1048576 | tf_op jit(solution)/shard_map/layer_three_own/pallas_call | solution.py:47
  90.4 8.4 %loss.1 = (f32[64,128]{1,0:T(8,128)S(1)}, f32[8,128]{1,0:T(8,128)S(1)}, f32[8,32,128]{2,1,0:T(8,128)}, bf16[96,2048]{1,0:T(8,128)(2,1)}, f8e4m3fn[48,2048]{1,0:T(8,128)(4,1)}, /*index=5*/f32[48,2048]{1,0:T(8,128)}) custom-call(s32[2]{0:T(128)S(1)} %pad_add_fusion.place, f32[8,256]{1,0:T(8,128)S(1)} %copy-done.3, ...), custom_call_target="tpu_custom_call" | custom-call | flops 4563402752 | bytes 1048576 | tf_op jit(solution)/shard_map/loss/pallas_call | solution.py:47
  99.0 6.0 %all-to-all-start.3 = ((f32[8,32,128]{2,1,0:T(8,128)}), f32[8,32,128]{2,1,0:T(8,128)S(1)}, u32[]{:S(2)}, u32[]{:S(2)}) async-start(f32[8,32,128]{2,1,0:T(8,128)} %get-tuple-element.111), calls=%async_computation.3 | async-start | bytes 262144 | tf_op jit(solution)/shard_map/all_to_all | solution.py:873
  105.0 7.5 %back_three.1.near_hbm = f32[48,2048]{1,0:T(8,128)} custom-call(s32[2]{0:T(128)S(1)} %pad_add_fusion.place, bf16[2048,4352]{1,0:T(8,128)(2,1)} %get-tuple-element.101.high, f8e4m3fn[2048,4352]{1,0:T(32,128)(4,1)} %get-tuple-element.102.rest, bf16[96,2048]{1,0:T(8,128)(2,1)} %get-tuple-element.113.grads, f8e4m3fn[48,2048]{1,0:T(8,128)(4,1)} %get-tuple-element.114.grads8, ...), custom_call_target="tpu_custom_call" | custom-call | flops 2281701376 | bytes 1048576 | tf_op jit(solution)/shard_map/back_three/pallas_call | solution.py:47
  114.0 12.5 %end_three.1 = (f32[256,128]{1,0:T(8,128)S(1)}, f32[8,128]{1,0:T(8,128)S(1)}, f32[8,40,256]{2,1,0:T(8,128)}, bf16[256,2048]{1,0:T(8,128)(2,1)}, f8e4m3fn[256,204...) custom-call(s32[2]{0:T(128)S(1)} %pad_add_fusion.place, f32[8,256]{1,0:T(8,128)S(1)} %copy-done.3, ...), custom_call_target="tpu_custom_call" | custom-call | flops 4563402752 | bytes 1048576 | tf_op jit(solution)/shard_map/end_three/pallas_call | solution.py:47
  126.7 6.0 %all-to-all-start.4 = ((f32[8,40,256]{2,1,0:T(8,128)}), f32[8,40,256]{2,1,0:T(8,128)S(1)}, u32[]{:S(2)}, u32[]{:S(2)}) async-start(f32[8,40,256]{2,1,0:T(8,128)} %get-tuple-element.121), calls=%async_computation.4 | async-start | bytes 655360 | tf_op jit(solution)/shard_map/all_to_all | solution.py:873
  132.7 9.9 %back.2.near_hbm = f32[256,2048]{1,0:T(8,128)} custom-call(s32[2]{0:T(128)S(1)} %pad_add_fusion.place, bf16[2048,4352]{1,0:T(8,128)(2,1)} %get-tuple-element.101.high, f8e4m3fn[2048,4352]{1,0:T(32,128)(4,1)} %get-tuple-element.102.rest, bf16[256,2048]{1,0:T(8,128)(2,1)} %get-tuple-element.123.grads, f8e4m3fn[256,2048]{1,0:T(32,128)(4,1)} %get-tuple-element.124.grads8, ...), custom_call_target="tpu_custom_call" | custom-call | flops 2281701376 | bytes 1048576 | tf_op jit(solution)/shard_map/back/pallas_call | solution.py:47
  145.2 7.7 %end_two.1 = (f32[256,128]{1,0:T(8,128)S(1)}, f32[8,128]{1,0:T(8,128)S(1)}, f32[8,56,256]{2,1,0:T(8,128)}, bf16[256,2048]{1,0:T(8,128)(2,1)}, f8e4m3fn[256,2048]...) custom-call(s32[2]{0:T(128)S(1)} %pad_add_fusion.place, f32[8,256]{1,0:T(8,128)S(1)} %copy-done.3, ...), custom_call_target="tpu_custom_call" | custom-call | flops 4563402752 | bytes 1048576 | tf_op jit(solution)/shard_map/end_two/pallas_call | solution.py:47
  152.9 5.2 %all-to-all-start.5 = ((f32[8,56,256]{2,1,0:T(8,128)}), f32[8,56,256]{2,1,0:T(8,128)S(1)}, u32[]{:S(2)}, u32[]{:S(2)}) async-start(f32[8,56,256]{2,1,0:T(8,128)} %get-tuple-element.132), calls=%async_computation.5 | async-start | bytes 917504 | tf_op jit(solution)/shard_map/all_to_all | solution.py:873
  158.0 10.2 %back.3 = (f32[256,1024]{1,0:T(8,128)}, f32[256,1024]{1,0:T(8,128)}) custom-call(s32[2]{0:T(128)S(1)} %pad_add_fusion.place, bf16[2048,4352]{1,0:T(8,128)(2,1)} %get-tuple-element.101.high, f8e4m3fn[2048,4352]{1,0:T(32,128)(4,1)} %get-tuple-element.102.rest, bf16[256,2048]{1,0:T(8,128)(2,1)} %get-tuple-element.133.grads, ...), custom_call_target="tpu_custom_call" | custom-call | flops 2281701376 | bytes 1048576 | tf_op jit(solution)/shard_map/back/pallas_call | solution.py:47
  168.3 3.1 %all-to-all-done.5.ret = f32[8,56,256]{2,1,0:T(8,128)S(1)} async-done(((f32[8,56,256]{2,1,0:T(8,128)}), f32[8,56,256]{2,1,0:T(8,128)S(1)}, u32[]{:S(2)}, u32[]{:S(2)}) %all-to-all-start.5) | async-done | bytes 458784 | tf_op jit(solution)/shard_map/all_to_all | solution.py:873
  173.4 3.1 %end_one.1 = (f32[64,128]{1,0:T(8,128)S(1)}, f32[64,128]{1,0:T(8,128)S(1)}, f32[64,128]{1,0:T(8,128)S(1)}, f32[64,128]{1,0:T(8,128)S(1)}, f32[8,256]{1,0:T(8,128)S(1)}, /*index=5*/f32[64,256]{1,0:T(8,128)S(1)}) custom-call(s32[2]{0:T(128)S(1)} %pad_add_fusion.place, f32[8,56,256]{2,1,0:T(8,128)S(1)} %all-to-all-done.5.ret, ...), custom_call_target="tpu_custom_call" | custom-call | flops 570425344 | bytes 1048576 | tf_op jit(solution)/shard_map/end_one/pallas_call | solution.py:47
  178.4 2.2 %collective-permute-done.14.two = f32[64,128]{1,0:T(8,128)S(1)} collective-permute-done((f32[64,128]{1,0:T(8,128)S(1)}, f32[64,128]{1,0:T(8,128)S(1)}, u32[]{:S(2)}, u32[]{:S(2)}) %collective-permute-start.14) | collective-permute-done | bytes 32800 | tf_op jit(solution)/shard_map/ppermute | solution.py:870
  181.7 15.9 %all_to_all.35.came = f32[8,80,128]{2,1,0:T(8,128)S(1)} all-to-all(f32[8,80,128]{2,1,0:T(8,128)S(1)} %gather.1), channel_id=1, replica_groups=mesh['dom'=8,'rep'=4] {'dom'}, dimensions={0} | all-to-all | bytes 655360 | tf_op jit(solution)/shard_map/all_to_all | solution.py:873
  (79 shorter events, 14.2 us)
Async XLA Ops:
  5.0 9.2 %collective-permute-start.2 = (bf16[64,1024]{1,0:T(8,128)(2,1)S(1)}, bf16[64,1024]{1,0:T(8,128)(2,1)S(1)}, u32[]{:S(2)}, u32[]{:S(2)}) collective-permute-start(bf16[64,1024]{1,0:T(8,128)(2,1)S(1)} %get-tuple-element.93.pack), channel_id=1, source_target_pairs={{0,3},{1,2},{2,1},{3,0},{4,7},{5,6},{6,5},{7,4},{8,11},{9,10},{10,... | collective-permute-start | bytes 393224 | tf_op jit(solution)/shard_map/ppermute | solution.py:870
  7.4 6.9 %collective-permute-start.1 = (bf16[64,1024]{1,0:T(8,128)(2,1)S(1)}, bf16[64,1024]{1,0:T(8,128)(2,1)S(1)}, u32[]{:S(2)}, u32[]{:S(2)}) collective-permute-start(bf16[64,1024]{1,0:T(8,128)(2,1)S(1)} %get-tuple-element.93.pack), channel_id=1, source_target_pairs={{0,2},{1,3},{2,0},{3,1},{4,6},{5,7},{6,4},{7,5},{8,10},{9,11},{10,... | collective-permute-start | bytes 393224 | tf_op jit(solution)/shard_map/ppermute | solution.py:870
  8.0 6.3 %collective-permute-start = (bf16[64,1024]{1,0:T(8,128)(2,1)S(1)}, bf16[64,1024]{1,0:T(8,128)(2,1)S(1)}, u32[]{:S(2)}, u32[]{:S(2)}) collective-permute-start(bf16[64,1024]{1,0:T(8,128)(2,1)S(1)} %get-tuple-element.93.pack), channel_id=1, source_target_pairs={{0,1},{1,0},{2,3},{3,2},{4,5},{5,4},{6,7},{7,6},{8,9},{9,8},{10,11... | collective-permute-start | bytes 393224 | tf_op jit(solution)/shard_map/ppermute | solution.py:870
  8.1 12.9 %all-to-all-start = ((bf16[8,32,128]{2,1,0:T(8,128)(2,1)}), bf16[8,32,128]{2,1,0:T(8,128)(2,1)S(1)}, u32[]{:S(2)}, u32[]{:S(2)}) async-start(bf16[8,32,128]{2,1,0:T(8,128)(2,1)} %get-tuple-element.92), calls=%async_computation | async-start | bytes 131072 | tf_op jit(solution)/shard_map/all_to_all | solution.py:873
  46.3 4.9 %collective-permute-start.3 = (bf16[256,2048]{1,0:T(8,128)(2,1)}, bf16[256,2048]{1,0:T(8,128)(2,1)S(1)}, u32[]{:S(2)}, u32[]{:S(2)}) collective-permute-start(bf16[256,2048]{1,0:T(8,128)(2,1)} %get-tuple-element.104.z_own), channel_id=1, source_target_pairs={{0,1},{1,0},{2,3},{3,2},{4,5},{5,4},{6,7},{7,6},{8,9},{9,8},{10,11... | collective-permute-start | bytes 3145736 | tf_op jit(solution)/shard_map/ppermute | solution.py:870
  46.4 17.0 %all-to-all-start.1 = ((bf16[8,32,256]{2,1,0:T(8,128)(2,1)}), bf16[8,32,256]{2,1,0:T(8,128)(2,1)S(1)}, u32[]{:S(2)}, u32[]{:S(2)}) async-start(bf16[8,32,256]{2,1,0:T(8,128)(2,1)} %get-tuple-element.103), calls=%async_computation.1 | async-start | bytes 262144 | tf_op jit(solution)/shard_map/all_to_all | solution.py:873
  63.4 1.4 collective-permute-start.4
  71.2 6.2 %collective-permute-start.5 = (bf16[48,2048]{1,0:T(8,128)(2,1)}, bf16[48,2048]{1,0:T(8,128)(2,1)S(1)}, u32[]{:S(2)}, u32[]{:S(2)}) collective-permute-start(bf16[48,2048]{1,0:T(8,128)(2,1)} %get-tuple-element.108.z_own), channel_id=1, source_target_pairs={{0,1},{1,0},{2,3},{3,2},{4,5},{5,4},{6,7},{7,6},{8,9},{9,8},{10,11... | collective-permute-start | bytes 589832 | tf_op jit(solution)/shard_map/ppermute | solution.py:870
  71.4 17.6 %all-to-all-start.2 = ((bf16[8,32,128]{2,1,0:T(8,128)(2,1)}), bf16[8,32,128]{2,1,0:T(8,128)(2,1)S(1)}, u32[]{:S(2)}, u32[]{:S(2)}) async-start(bf16[8,32,128]{2,1,0:T(8,128)(2,1)} %get-tuple-element.107), calls=%async_computation.2 | async-start | bytes 131072 | tf_op jit(solution)/shard_map/all_to_all | solution.py:873
  89.0 1.3 collective-permute-start.6
  98.8 13.8 %collective-permute-start.7 = (f32[48,2048]{1,0:T(8,128)}, f32[48,2048]{1,0:T(8,128)S(1)}, u32[]{:S(2)}, u32[]{:S(2)}) collective-permute-start(f32[48,2048]{1,0:T(8,128)} %get-tuple-element.112), channel_id=1, source_target_pairs={{0,1},{1,0},{2,3},{3,2},{4,5},{5,4},{6,7},{7,6},{8,9},{9,8},{10,11... | collective-permute-start | bytes 1179656 | tf_op jit(solution)/shard_map/ppermute | solution.py:870
  99.0 13.5 %all-to-all-start.3 = ((f32[8,32,128]{2,1,0:T(8,128)}), f32[8,32,128]{2,1,0:T(8,128)S(1)}, u32[]{:S(2)}, u32[]{:S(2)}) async-start(f32[8,32,128]{2,1,0:T(8,128)} %get-tuple-element.111), calls=%async_computation.3 | async-start | bytes 262144 | tf_op jit(solution)/shard_map/all_to_all | solution.py:873
  112.6 1.4 collective-permute-start.8
  126.5 17.0 %collective-permute-start.9 = (f32[256,2048]{1,0:T(8,128)}, f32[256,2048]{1,0:T(8,128)}, u32[]{:S(2)}, u32[]{:S(2)}) collective-permute-start(f32[256,2048]{1,0:T(8,128)} %get-tuple-element.122), channel_id=1, source_target_pairs={{0,1},{1,0},{2,3},{3,2},{4,5},{5,4},{6,7},{7,6},{8,9},{9,8},{10,11... | collective-permute-start | bytes 6291464 | tf_op jit(solution)/shard_map/ppermute | solution.py:870
  126.7 16.8 %all-to-all-start.4 = ((f32[8,40,256]{2,1,0:T(8,128)}), f32[8,40,256]{2,1,0:T(8,128)S(1)}, u32[]{:S(2)}, u32[]{:S(2)}) async-start(f32[8,40,256]{2,1,0:T(8,128)} %get-tuple-element.121), calls=%async_computation.4 | async-start | bytes 655360 | tf_op jit(solution)/shard_map/all_to_all | solution.py:873
  143.5 1.6 collective-permute-start.10
  152.9 18.6 %all-to-all-start.5 = ((f32[8,56,256]{2,1,0:T(8,128)}), f32[8,56,256]{2,1,0:T(8,128)S(1)}, u32[]{:S(2)}, u32[]{:S(2)}) async-start(f32[8,56,256]{2,1,0:T(8,128)} %get-tuple-element.132), calls=%async_computation.5 | async-start | bytes 917504 | tf_op jit(solution)/shard_map/all_to_all | solution.py:873
  168.2 3.2 %collective-permute-start.12 = (f32[256,1024]{1,0:T(8,128)}, f32[256,1024]{1,0:T(8,128)S(1)}, u32[]{:S(2)}, u32[]{:S(2)}) collective-permute-start(f32[256,1024]{1,0:T(8,128)} %get-tuple-element.142), channel_id=1, source_target_pairs={{0,1},{1,0},{2,3},{3,2},{4,5},{5,4},{6,7},{7,6},{8,9},{9,8},{10,11... | collective-permute-start | bytes 3145736 | tf_op jit(solution)/shard_map/ppermute | solution.py:870
  171.4 1.8 collective-permute-start.11
  173.3 24.4 %copy-start.4 = (f32[100,64]{0,1:T(8,128)S(1)}, f32[100,64]{0,1:T(8,128)}, u32[]{:S(2)}) copy-start(f32[100,64]{0,1:T(8,128)} %param.33) | copy-start | bytes 76804
  173.3 24.4 %copy-start.5 = (f32[256,64]{0,1:T(8,128)S(1)}, f32[256,64]{0,1:T(8,128)}, u32[]{:S(2)}) copy-start(f32[256,64]{0,1:T(8,128)} %param.39) | copy-start | bytes 196612
  176.5 1.9 collective-permute-start.13
  176.7 3.9 %collective-permute-start.14 = (f32[64,128]{1,0:T(8,128)S(1)}, f32[64,128]{1,0:T(8,128)S(1)}, u32[]{:S(2)}, u32[]{:S(2)}) collective-permute-start(f32[64,128]{1,0:T(8,128)S(1)} %get-tuple-element.146), channel_id=1, source_target_pairs={{0,2},{1,3},{2,0},{3,1},{4,6},{5,7},{6,4},{7,5},{8,10},{9,11},{10,... | collective-permute-start | bytes 98312 | tf_op jit(solution)/shard_map/ppermute | solution.py:870
  178.3 3.4 %collective-permute-start.15 = (f32[64,128]{1,0:T(8,128)S(1)}, f32[64,128]{1,0:T(8,128)S(1)}, u32[]{:S(2)}, u32[]{:S(2)}) collective-permute-start(f32[64,128]{1,0:T(8,128)S(1)} %get-tuple-element.147), channel_id=1, source_target_pairs={{0,3},{1,2},{2,1},{3,0},{4,7},{5,6},{6,5},{7,4},{8,11},{9,10},{10,... | collective-permute-start | bytes 98312 | tf_op jit(solution)/shard_map/ppermute | solution.py:870
  (19 other events, 355.9 us)

commit v4 on v3

--- a/solution.py
+++ b/solution.py
@@ -23,6 +23,7 @@
 AHEAD = 3
 LIMIT = 52 << 20
 RESIDENT_BYTES = 30 << 20
+FEAT_SCALE = 32.0
 
 SMEM = pl.BlockSpec(memory_space=pltpu.SMEM)
 VMEM = pl.BlockSpec(memory_space=pltpu.VMEM)
@@ -237,6 +238,8 @@
 
 def table_kernel(place, pack, pack_one, pack_two, pack_three, feat_hbm, packs, most_out, table_hbm, feat_t, table, in_sems, out_sems):
     width, nodes = feat_t.shape
+    units = packs.shape[0]
+    extra = jnp.zeros((table.shape[0] - units - width, ROWS), BF16)
     steps = nodes // ROWS
     blocks = Stream(in_sems, (feat_hbm, cols_at(ROWS), feat_t, cols_at(ROWS)))
     stores = Stream(out_sems, (table, cols_at(ROWS), table_hbm, cols_at(ROWS)))
@@ -249,7 +252,8 @@
         blocks.wait(i)
         here = span(i * ROWS, ROWS)
         z = dot_nn(weight, feat_t[:, here])
-        table[:, here] = z.astype(BF16)
+        table[0:units, here] = z.astype(BF16)
+        table[units:, here] = jnp.concatenate([feat_t[:, here], extra], axis=0)
         stores.start(i)
         return jnp.maximum(most, lane_most(z))
 
@@ -273,7 +277,7 @@
     return u * half, slope
 
 
-def layer_one_kernel(place, src_t, norm_t, rows, send, most, packs_hbm, table_hbm, z_send, flags_t, high_hbm, rest_hbm, hidden_hbm, slope_hbm, z_hbm, packs, table, table8, high, rest, hidden_t, slope_t, z_own, in_sems, edge_sems, out_sems):
+def layer_one_kernel(place, src_t, norm_t, rows, send, most, packs_hbm, table_hbm, z_send, flags_t, high_hbm, rest_hbm, hidden_hbm, slope_hbm, z_hbm, near_hbm, packs, table, table8, high, rest, hidden_t, slope_t, z_own, near_feat, in_sems, edge_sems, out_sems):
     slots = src_t.shape[0]
     units, half = hidden_t.shape
     nodes = 2 * half
@@ -290,7 +294,10 @@
     edge_stores = Stream(edge_sems, (high, slot_at, high_hbm, rows_at(FINE)), (rest, slot_at, rest_hbm, rows_at(FINE)))
     stores = Stream(
         out_sems,
-        *[(a, cols_at(FINE), b, cols_at(FINE)) for a, b in ((hidden_t, hidden_hbm), (slope_t, slope_hbm), (z_own, z_hbm))],
+        *[
+            (a, cols_at(FINE), b, cols_at(FINE))
+            for a, b in ((hidden_t, hidden_hbm), (slope_t, slope_hbm), (z_own, z_hbm), (near_feat, near_hbm))
+        ],
     )
     in_slot = lax.broadcasted_iota(I32, (8, 128), 1) // per_group == lax.broadcasted_iota(I32, (8, 128), 0)
     node_row = lax.broadcasted_iota(I32, (per_group, 256), 0)
@@ -344,7 +351,8 @@
         edge_stores.start(i)
 
     flat_rows = rows[...].reshape(halo, 128)
-    flags = flat_rows.astype(F32).T[FLAG_LANE : FLAG_LANE + 8, :]
+    turned = flat_rows.astype(F32).T
+    flags = turned[FLAG_LANE : FLAG_LANE + 8, :]
     counts = jnp.sum(rows[...].astype(F32)[:, 0, :], axis=0, keepdims=True)
     count = 64.0 * counts[:, FLAG_LANE + 3 : FLAG_LANE + 4] + counts[:, FLAG_LANE + 4 : FLAG_LANE + 5]
     row = lax.broadcasted_iota(I32, flags.shape, 0)
@@ -355,20 +363,37 @@
     fetch.wait(0)
     border = dot_nt(packs[:, 0:FLAG_LANE], flat_rows[:, 0:FLAG_LANE]).astype(BF16).astype(F32)
     border = jnp.where(flags[0:1, :] == 1.0, border, stale_columns(packs, 0, halo))
-    table[:, nodes : nodes + halo] = border.astype(BF16)
+    table[0:units, nodes : nodes + halo] = border.astype(BF16)
+    extra = table.shape[0] - units
+    kept = lax.broadcasted_iota(I32, (extra, halo), 0) < FLAG_LANE
+    kept = kept & (flags[0:1, :] == 1.0)
+    table[units:, nodes : nodes + halo] = jnp.where(kept, turned[0:extra, :], 0.0).astype(BF16)
     scale, back = scale_of(jnp.maximum(jnp.max(most[...]), jnp.max(jnp.abs(border))))
-    back = back * (1.0 / REST_GAIN)
+    row = lax.broadcasted_iota(I32, (table.shape[0], 1), 0)
+    scale = jnp.where(row < units, scale, FEAT_SCALE)
+    back = jnp.where(row < units, back, 1.0 / FEAT_SCALE) * (1.0 / REST_GAIN)
     bias = bias_column(packs, 0)
+    unused = jnp.zeros((table8.shape[0] - table.shape[0], 256), F32)
 
     def small(i):
         here = span(i * 256, 256)
-        table8[:, here] = (table[:, here].astype(F32) * scale).astype(F8)
+        value = table[:, here].astype(F32) * scale
+        table8[:, here] = jnp.concatenate([value, unused], axis=0).astype(F8)
 
     loop((nodes + halo) // 256, small)
 
     def sums(i):
         here = slot_of(i)
-        return dot_nt(table[...], high[here, :]) + dot_nt(table8[...], rest[here, :]) * back
+        low = dot_nt(table8[...], rest[here, :])[0 : table.shape[0]]
+        return dot_nt(table[...], high[here, :]) + low * back
+
+    def keep(i, total):
+        here = span(i * FINE, FINE)
+        slope_t[:, here] = total[0:units]
+        value = total[units:]
+        top = value.astype(BF16)
+        near_feat[0:extra, here] = top
+        near_feat[extra:, here] = (value - top.astype(F32)).astype(BF16)
 
     def finish(i):
         here = span(i * FINE, FINE)
@@ -392,13 +417,13 @@
         total = sums(i)
         finish(i - 1)
         build_block(i + 1)
-        slope_t[:, span(i * FINE, FINE)] = total
+        keep(i, total)
         return carry
 
-    slope_t[:, 0:FINE] = sums(0)
+    keep(0, sums(0))
     build_block(1)
     lax.fori_loop(1, steps - 1, step, 0)
-    slope_t[:, span((steps - 1) * FINE, FINE)] = sums(steps - 1)
+    keep(steps - 1, sums(steps - 1))
     finish(steps - 2)
     finish(steps - 1)
     stores.wait_all(steps)
@@ -600,27 +625,36 @@
     return total + dot_nn(tails8, top.astype(F8)) * back_tail
 
 
-def back_kernel(halves, place, high, rest, grads, grads8, tails8, back, *refs):
-    *outs, hbuf, rbuf, sems = refs
-    size = outs[0].shape[1]
-    steps = pl.num_programs(0) // len(outs)
-    base = place[1] * size * steps if halves == 2 else 0
-
-    def cut(i):
-        owner = jnp.where(i < steps * (len(outs) - 1), 1 - place[0], place[0])
-        return slice(None), span(owner * size * steps * halves + base + lax.rem(i, steps) * size, size)
-
-    ring = Ring((high, rest), (hbuf, rbuf), sems, cut)
-    ring.begin()
-    top, low = ring.wait()
-    total = back_block(grads[...], grads8[...], tails8[...], back[0:1, 0:1], back[0:1, 1:2], top[...], low[...])
-    for k, out in enumerate(outs):
-
-        @pl.when((ring.step >= k * steps) & (ring.step < (k + 1) * steps))
+def back_kernel(place, back, grads_hbm, grads8_hbm, tails8_hbm, high, rest, out_hbm, out, grads, grads8, tails8, hbuf, rbuf, in_sems, edge_sems, out_sems):
+    half = out.shape[1]
+    steps = half // ROWS
+    mine = cols_at(ROWS, place[0] * half)
+    fetch = Stream(
+        in_sems,
+        *[(a, all_of, b, all_of) for a, b in ((grads_hbm, grads), (grads8_hbm, grads8), (tails8_hbm, tails8))],
+    )
+    edges = Stream(edge_sems, (high, mine, hbuf, cols_at(ROWS)), (rest, mine, rbuf, cols_at(ROWS)))
+    stores = Stream(out_sems, (out, cols_at(ROWS), out_hbm, cols_at(ROWS)))
+    fetch.start(0)
+    edges.start(0)
+    fetch.wait(0)
+    for i in range(1, min(AHEAD, steps)):
+        edges.start(i)
+
+    def step(i):
+        edges.wait(i)
+        here = span(i * ROWS, ROWS)
+        out[:, here] = back_block(
+            grads[...], grads8[...], tails8[...], back[0:1, 0:1], back[0:1, 1:2], hbuf[:, here], rbuf[:, here]
+        )
+        stores.start(i)
+
+        @pl.when(i + AHEAD < steps)
         def _():
-            out[...] = total
-
-    ring.end()
+            edges.start(i + AHEAD)
+
+    loop(steps, step)
+    stores.wait_all(steps)
 
 
 def returned_terms(ret, ret_oth, bound, kinds):
@@ -638,18 +672,13 @@
     return total.astype(BF16)
 
 
-def end_kernel(layer, place, flags_t, ret, ret_oth, weight_ref, send, far_in_any, near_hbm, hidden_hbm, slope_hbm, high, rest, sums, back_out, border_grad, grads_hbm, grads8_hbm, tails8_hbm, *more):
-    if layer == 1:
-        far_hbm, far, hbuf, rbuf, edge_sems, far_sems = more[0], *more[-5:]
-        more = more[1:-5]
-    near, far_in, hidden_t, slope_t, hrows, rrows, grad_rows, grad_weight, border_sum, grads, grads8, tails8, in_sems, row_sems, out_sems = more
+def end_three_kernel(place, flags_t, ret, ret_oth, last_t, send, far_in_any, near_hbm, hidden_hbm, slope_hbm, high, rest, sums, back_out, border_grad, grads_hbm, grads8_hbm, tails8_hbm, far_hbm, near, far_in, hidden_t, slope_t, hrows, rrows, grad_rows, grad_last, border_sum, grads, grads8, tails8, far, hbuf, rbuf, in_sems, row_sems, out_sems, edge_sems, far_sems):
     kinds, half = near.shape
     units = slope_t.shape[0]
     parts = ret.shape[0]
     bound = send.shape[0] // parts
     halo = send.shape[0]
     steps = half // ROWS
-    size = 64 // parts
     cut = border_cut(2 * half, halo)
     blocks = Stream(
         in_sems,
@@ -666,29 +695,22 @@
             for a, b in ((grads, grads_hbm), (grads8, grads8_hbm), (tails8, tails8_hbm))
         ],
     )
-    if layer == 1:
-        others = cols_at(ROWS, (1 - place[0]) * half)
-        edges = Stream(edge_sems, (high, others, hbuf, cols_at(ROWS)), (rest, others, rbuf, cols_at(ROWS)))
-        far_stores = Stream(far_sems, (far, cols_at(ROWS), far_hbm, cols_at(ROWS)))
-    loop(steps, blocks.start)
-    loop(steps, borders.start)
-    if layer == 1:
-        loop(steps, edges.start)
+    others = cols_at(ROWS, (1 - place[0]) * half)
+    edges = Stream(edge_sems, (high, others, hbuf, cols_at(ROWS)), (rest, others, rbuf, cols_at(ROWS)))
+    far_stores = Stream(far_sems, (far, cols_at(ROWS), far_hbm, cols_at(ROWS)))
+    for stream in (blocks, borders, edges):
+        loop(steps, stream.start)
     terms = returned_terms(ret, ret_oth, bound, kinds)
-    if layer == 0:
-        chunk = jnp.sum(ret[:, bound:, :] + ret_oth[:, bound:, :], axis=0)
-        weight = weight_ref[:, 128 : 128 + units]
-    else:
-        weight = padded_rows(weight_ref, kinds)
+    weight = padded_rows(last_t, kinds)
     sums[...] = jnp.zeros(sums.shape, F32)
-    grad_weight[...] = jnp.zeros(grad_weight.shape, F32)
+    grad_last[...] = jnp.zeros(grad_last.shape, F32)
     border_sum[...] = jnp.zeros(border_sum.shape, F32)
 
     def first_step(i, most):
         blocks.wait(i)
         here = span(i * ROWS, ROWS)
         d_z = round_gradient(near[:, here], far_in[:, here], terms, send[...], (place[0] * steps + i) * ROWS)
-        grad_weight[0:kinds, :] += dot_nt(d_z, hidden_t[:, here])
+        grad_last[0:kinds, :] += dot_nt(d_z, hidden_t[:, here])
         grad = dot_tn(weight, d_z) * slope_t[:, here]
         sums[...] += lane_sums(grad)
         grad_rows[:, here] = grad
@@ -715,15 +737,8 @@
         border_sum[...] += back_block(top, small, tail, back_rest, back_tail, hrows[here, :], rrows[here, :])
 
     loop(steps, second_step)
-    put_border(border_grad, border_sum[...], flags_t[layer : layer + 1, :])
-    if layer == 1:
-        border_grad[:, bound:, :] = grad_weight[...].reshape(parts, size, units)
-    else:
-        for core in range(2):
-            block = grad_weight[span(place[1] * 128 + core * 64, 64), :]
-            first = bound + core * size
-            border_grad[:, first : first + size, :] = block.reshape(parts, size, units)
-        border_grad[:, bound + 2 * size :, :] = jnp.broadcast_to(chunk[None], (parts, size, units))
+    put_border(border_grad, border_sum[...], flags_t[1:2, :])
+    border_grad[:, bound:, :] = grad_last[...].reshape(parts, 64 // parts, units)
 
     def far_step(i):
         edges.wait(i)
@@ -733,56 +748,82 @@
         )
         far_stores.start(i)
 
-    if layer == 1:
-        loop(steps, far_step)
-        far_stores.wait_all(steps)
+    loop(steps, far_step)
+    far_stores.wait_all(steps)
     stores.wait_all(steps)
 
 
-def end_one_kernel(place, ret, ret_oth, send, sums_one, sums_two, sums_out, far_any, near_hbm, feat_hbm, out, out_one, out_two, out_three, second_chunk, grad_last, near, far, feat_t, grad_first, in_sems):
-    units, size = near.shape
+def end_two_kernel(place, ret, ret_oth, packs, send, sums_two, sums_out, far_any, near_hbm, hidden_hbm, slope_hbm, feat_hbm, out, out_one, last_chunk, near, far, hidden_t, slope_t, near_feat, grad_first, grad_second, sums_one, in_sems):
+    units, half = near.shape
     parts = ret.shape[0]
     bound = send.shape[0] // parts
-    width = feat_t.shape[0]
-    chunk = 64 // parts
-    steps = size // ROWS
-    base = place[0] * 2 * size + place[1] * size
+    steps = half // ROWS
+    extra = near_feat.shape[0] // 2
     blocks = Stream(
         in_sems,
-        (near_hbm, cols_at(ROWS), near, cols_at(ROWS)),
-        (far_any, cols_at(ROWS), far, cols_at(ROWS)),
-        (feat_hbm, cols_at(ROWS, base), feat_t, cols_at(ROWS)),
-    )
-    blocks.start_first(steps)
+        *[
+            (a, cols_at(ROWS), b, cols_at(ROWS))
+            for a, b in (
+                (near_hbm, near),
+                (far_any, far),
+                (hidden_hbm, hidden_t),
+                (slope_hbm, slope_t),
+                (feat_hbm, near_feat),
+            )
+        ],
+    )
+    loop(steps, blocks.start)
     terms = returned_terms(ret, ret_oth, bound, units)
-    mine = pl.ds(bound + place[0] * chunk, chunk)
-    second_chunk[...] = jnp.sum(ret[:, mine, :] + ret_oth[:, mine, :], axis=0)
-    grad_last[...] = ret[:, bound + 2 * chunk :, :].reshape(64, units)
-    grad_first[...] = jnp.zeros(grad_first.shape, F32)
+    last_chunk[...] = jnp.sum(ret[:, bound:, :] + ret_oth[:, bound:, :], axis=0)
+    weight = packs[:, 128 : 128 + units]
+    for ref in (grad_first, grad_second, sums_one):
+        ref[...] = jnp.zeros(ref.shape, F32)
 
     def step(i):
-        blocks.next(i, steps)
+        blocks.wait(i)
         here = span(i * ROWS, ROWS)
-        d_z = round_gradient(near[:, here], far[:, here], terms, send[...], base + i * ROWS)
-        grad_first[:, 0:width] += dot_nt(d_z, feat_t[:, here])
+        d_z = round_gradient(near[:, here], far[:, here], terms, send[...], (place[0] * steps + i) * ROWS)
+        grad_second[...] += dot_nt(d_z, hidden_t[:, here])
+        grad = dot_tn(weight, d_z) * slope_t[:, here]
+        sums_one[...] += lane_sums(grad)
+        top = grad.astype(BF16)
+        tail = (grad - top.astype(F32)).astype(BF16)
+        high, low = near_feat[0:extra, here], near_feat[extra:, here]
+        grad_first[:, 0:extra] += dot_nt(top, high) + (dot_nt(tail, high) + dot_nt(top, low))
 
     loop(steps, step)
-    lead = jnp.where(place[1] == 0, 1.0, 0.0)
     lane = lax.broadcasted_iota(I32, (64, 128), 1)
-    column = lambda value: jnp.sum(value, axis=1, keepdims=True) * lead
-    for k, ref in enumerate((out, out_one, out_two, out_three)):
+    column = lambda value: jnp.sum(value, axis=1, keepdims=True)
+    for k, ref in enumerate((out, out_one)):
         rows = span(jnp.bitwise_xor(place[0] + 2 * place[1], k) * 64, 64)
-        value = grad_first[rows, :]
+        value = jnp.where(lane < FLAG_LANE, grad_first[rows, :], 0.0)
         value = jnp.where(lane == FLAG_LANE, column(sums_one[rows, :]), value)
         value = jnp.where(lane == FLAG_LANE + 1, column(sums_two[rows, :]), value)
-        ref[...] = jnp.where(lane == FLAG_LANE + 2, column(sums_out[...]), value)
-
-
-def gather_kernel(mine, one, two, three, second_chunk, out):
-    total = mine[...] + one[...] + two[...] + three[...]
-    value = jnp.concatenate([total, second_chunk[:, 0:128], second_chunk[:, 128:256]], axis=0)
-    for p in range(out.shape[0]):
+        ref[0:64, :] = jnp.where(lane == FLAG_LANE + 2, column(sums_out[...]), value)
+        ref[64:128, :] = grad_second[rows, 0:128]
+        ref[128:192, :] = grad_second[rows, 128:256]
+
+
+def scatter_kernel(mine, came, last_chunk, out):
+    total = mine[...] + came[...]
+    parts, size = out.shape[0], last_chunk.shape[0]
+    for q in range(parts):
+        pieces = [total[64 * k + q * size : 64 * k + (q + 1) * size, :] for k in range(3)]
+        pieces += [last_chunk[:, 0:128], last_chunk[:, 128:256]]
+        out[q] = jnp.concatenate(pieces, axis=0)
+
+
+def joined(came, first, size):
+    return came[:, first : first + size, :].reshape(64, 128)
+
+
+def gather_kernel(came, out, grad_last):
+    parts = came.shape[0]
+    size = 64 // parts
+    value = jnp.sum(came[:, 0 : 3 * size, :], axis=0)
+    for p in range(parts):
         out[p] = value
+    grad_last[...] = jnp.concatenate([joined(came, 3 * size, size), joined(came, 4 * size, size)], axis=1)
 
 
 def adamw(weight, moment, square, gradient):
@@ -801,9 +842,8 @@
     parts = came.shape[0]
     size = 64 // parts
     width, kinds = params[0].shape[1], params[6].shape[0]
-    total = jnp.sum(came[:, 0:64, :], axis=0)
-
-    halves = [came[:, 64 + k * size : 64 + (k + 1) * size, :].reshape(64, 128) for k in range(2)]
+    total = joined(came, 0, size)
+    halves = [joined(came, size, size), joined(came, 2 * size, size)]
     turned = jnp.concatenate([total, jnp.zeros((64, 128), F32)], axis=0).T
     gradients = (
         total[:, 0:width],
@@ -879,6 +919,8 @@
     whole = lambda a: (a, whole_spec(a.shape))
     work = 2 * half * table * units
     pack_width = 256 + units + 2 * halo
+    extra = -(-in_width // 16) * 16
+    both = units + extra
     rows_out, pack, send = run(
         pack_kernel,
         "pack",
@@ -906,10 +948,10 @@
         table_kernel,
         "table",
         [where, *placed(VMEM, *packs), (feat_t, HBM)],
-        [((units, pack_width), BF16, OWN), ((units, 128), F32, VMEM), ((units, nodes), BF16, HBM)],
+        [((units, pack_width), BF16, OWN), ((units, 128), F32, VMEM), ((units + extra, nodes), BF16, HBM)],
         [
             vm((in_width, nodes), BF16),
-            vm((units, nodes), BF16),
+            vm((units + extra, nodes), BF16),
             sems(1, nodes // ROWS),
             sems(1, nodes // ROWS),
         ],
@@ -917,7 +959,7 @@
     )
     rows, most = late(most, rows)
     held = fine if half * table * 3 <= RESIDENT_BYTES else min(fine, 4)
-    z_send, flags_t, high, rest, hidden_one, slope_one, z_own = run(
+    z_send, flags_t, high, rest, hidden_one, slope_one, z_own, near_feat = run(
         layer_one_kernel,
         "layer_one",
         [where, *placed(OWN, edge_src.T, edge_norm.T), *placed(VMEM, rows, send, most), *placed(HBM, packs, first_table)],
@@ -929,19 +971,21 @@
             ((units, half), BF16, HBM),
             ((units, half), F32, HBM),
             ((units, half), BF16, HBM),
+            ((2 * extra, half), BF16, HBM),
         ],
         [
             vm((units, pack_width), BF16),
-            vm((units, table), BF16),
-            vm((units, table), F8),
+            vm((both, table), BF16),
+            vm((-(-both // 32) * 32, table), F8),
             vm((held * FINE, table), BF16),
             vm((held * FINE, table), F8),
             vm((units, half), BF16),
             vm((units, half), F32),
             vm((units, half), BF16),
+            vm((2 * extra, half), BF16),
             sems(2, 1),
             sems(2, fine),
-            sems(3, fine),
+            sems(4, fine),
         ],
         flops=2 * work,
     )
@@ -1035,102 +1079,96 @@
     ret_oth = swap(ret)
     chunk = 64 // parts
 
-    def end(layer, name, ret, ret_oth, weight, near, far, hidden, slope):
-        n = near.shape[0]
-        with_far = layer == 1
-        return run(
-            functools.partial(end_kernel, layer),
-            name,
-            [
-                where,
-                *placed(VMEM, flags_t, ret, ret_oth, weight, send),
-                (far, ANY),
-                *placed(HBM, near, hidden, slope),
-                *edge,
-            ],
-            [
-                ((units, 128), F32, VMEM),
-                ((8, 128), F32, VMEM),
-                ((parts, bound + (1 if with_far else 3) * chunk, units), F32, VMEM),
-                ((units, half), BF16, HBM),
-                ((units, half), F8, HBM),
-                ((units, half), F8, HBM),
-                *([((units, half), F32, HBM)] if with_far else []),
-            ],
-            [
-                vm((n, half), F32),
-                vm((n, half), F32),
-                vm((units, half), BF16),
-                vm((units, half), F32),
-                *border_rows,
-                vm((units, half), F32),
-                vm((max(n, 64), units), F32),
-                vm((units, halo), F32),
-                vm((units, half), BF16),
-                vm((units, half), F8),
-                vm((units, half), F8),
-                sems(4, steps),
-                sems(2, steps),
-                sems(3, steps),
-            ]
-            + (
-                [vm((units, half), F32), vm((half, half), BF16), vm((half, half), F8), sems(2, steps), sems(1, steps)]
-                if with_far
-                else []
-            ),
-            flops=work,
-        )
-
-    def back_part(halves, back, grads, grads8, tails8):
-        each = fine // halves
-        out_block = lambda k: pl.BlockSpec((units, FINE), lambda i: (0, jnp.clip(i - k * each, 0, each - 1)))
-        return run(
-            functools.partial(back_kernel, halves),
-            "back",
-            [where, *edge, whole(grads), whole(grads8), whole(tails8), (back, VMEM)],
-            [((units, half // halves), F32, out_block(k)) for k in range(halves)],
-            ring_scratch((half, FINE)),
-            flops=work // 2,
-            grid=(fine,),
-        )
-
-    sums_two, back, border_grad, grads, grads8, tails8, far = end(
-        1, "end_three", ret, ret_oth, last_t, near, far, hidden_two, slope_two
+    sums_two, back, border_grad, grads, grads8, tails8, far = run(
+        end_three_kernel,
+        "end_three",
+        [where, *placed(VMEM, flags_t, ret, ret_oth, last_t, send), (far, ANY)]
+        + [*placed(HBM, near, hidden_two, slope_two), *edge],
+        [
+            ((units, 128), F32, VMEM),
+            ((8, 128), F32, VMEM),
+            ((parts, bound + chunk, units), F32, VMEM),
+            ((units, half), BF16, HBM),
+            ((units, half), F8, HBM),
+            ((units, half), F8, HBM),
+            ((units, half), F32, HBM),
+        ],
+        [
+            vm((kinds, half), F32),
+            vm((kinds, half), F32),
+            vm((units, half), BF16),
+            vm((units, half), F32),
+            *border_rows,
+            vm((units, half), F32),
+            vm((64, units), F32),
+            vm((units, halo), F32),
+            vm((units, half), BF16),
+            vm((units, half), F8),
+            vm((units, half), F8),
+            vm((units, half), F32),
+            vm((half, half), BF16),
+            vm((half, half), F8),
+            sems(4, steps),
+            sems(2, steps),
+            sems(3, steps),
+            sems(2, steps),
+            sems(1, steps),
+        ],
+        flops=work,
     )
     far = swap(far)
     ret = exchange(border_grad)
-    near = back_part(1, back, grads, grads8, tails8)[0]
+    near = run(
+        back_kernel,
+        "back",
+        [where, (back, VMEM), *placed(HBM, grads, grads8, tails8), *edge],
+        [((units, half), F32, HBM)],
+        [
+            vm((units, half), F32),
+            vm((units, half), BF16),
+            vm((units, half), F8),
+            vm((units, half), F8),
+            vm((half, half), BF16),
+            vm((half, half), F8),
+            sems(3, 1),
+            sems(2, steps),
+            sems(1, steps),
+        ],
+        flops=work // 2,
+    )[0]
     ret, far, near = late(near, ret, far)
     ret_oth = swap(ret)
-    sums_one, back, border_grad, grads, grads8, tails8 = end(
-        0, "end_two", ret, ret_oth, packs, near, far, hidden_one, slope_one
-    )
-    ret = exchange(border_grad)
-    far, near = back_part(2, back, grads, grads8, tails8)
-    far = swap(far)
-    ret, near = late(near, ret)
-    ret_oth = swap(ret)
-    *pieces, second_chunk, grad_last = run(
-        end_one_kernel,
-        "end_one",
-        [where, *placed(VMEM, ret, ret_oth, send, sums_one, sums_two, sums_out), (far, ANY), *placed(HBM, near, feat_t)],
-        [((64, 128), F32, VMEM)] * 4 + [((chunk, units), F32, VMEM), ((64, units), F32, VMEM)],
+    mine, theirs, last_chunk = run(
+        end_two_kernel,
+        "end_two",
+        [where, *placed(VMEM, ret, ret_oth), (packs, OWN), *placed(VMEM, send, sums_two, sums_out), (far, ANY)]
+        + placed(HBM, near, hidden_one, slope_one, near_feat),
+        [((192, 128), F32, VMEM)] * 2 + [((chunk, units), F32, VMEM)],
         [
-            vm((units, half // 2), F32),
-            vm((units, half // 2), F32),
-            vm((in_width, half // 2), BF16),
+            vm((units, half), F32),
+            vm((units, half), F32),
+            vm((units, half), BF16),
+            vm((units, half), F32),
+            vm((2 * extra, half), BF16),
             vm((units, 128), F32),
-            sems(3, steps),
-        ],
-        flops=work // 8,
-    )
-    pieces = [piece if k == 0 else swap(piece, k) for k, piece in enumerate(pieces)]
-    gathered = run(
+            vm((units, units), F32),
+            vm((units, 128), F32),
+            sems(5, steps),
+        ],
+        flops=work // 4,
+    )
+    scattered = run(
+        scatter_kernel,
+        "scatter",
+        placed(VMEM, mine, swap(theirs), last_chunk),
+        [((parts, 5 * chunk, 128), F32, VMEM)],
+    )[0]
+    gathered, grad_last = run(
         gather_kernel,
         "gather",
-        placed(VMEM, *pieces, second_chunk),
-        [((parts, 64 + 2 * chunk, 128), F32, VMEM)],
-    )[0]
+        placed(VMEM, exchange(scattered)),
+        [((parts, 3 * chunk, 128), F32, VMEM), ((64, units), F32, VMEM)],
+    )
     came = exchange(gathered)
 
     turn = lambda x: x.T

time: 200 us -> 181 us (0.905)
  Pallas kernels: 125 us -> 114 us
  starting transfers between devices: 40.3 us -> 33.4 us
  waiting for transfers between devices: 16.3 us -> 9.92 us
  blocking collectives: 15.9 us -> 21.9 us
    pallas_call x15 -> x14, Pallas kernels: 125 us -> 114 us  [run(): pl.pallas_call(kernel, grid=grid, in_specs=[spec for _, spec in args], ou...]
    all_to_all x1 -> x2, blocking collectives: 15.9 us -> 21.9 us  [exchange(): return lax.all_to_all(x, 'dom', split_axis=0, concat_axis=0, tiled=True)]
    all_to_all x6 -> x5, starting transfers between devices: 33.9 us -> 28.8 us  [exchange(): return lax.all_to_all(x, 'dom', split_axis=0, concat_axis=0, tiled=True)]
    ppermute x16 -> x12, waiting for transfers between devices: 10.4 us -> 6.49 us  [swap(): return lax.ppermute(x, 'rep', [(i, i ^ k) for i in range(reps)])]
    all_to_all x6 -> x5, waiting for transfers between devices: 5.88 us -> 3.44 us  [exchange(): return lax.all_to_all(x, 'dom', split_axis=0, concat_axis=0, tiled=True)]
    ppermute x16 -> x12, starting transfers between devices: 6.34 us -> 4.58 us  [swap(): return lax.ppermute(x, 'rep', [(i, i ^ k) for i in range(reps)])]
  transfers between devices with their start and end apart: 22 -> 17, of which waited for: 11 -> 8; matrix products, arithmetic and copies ran while one was open for 0% -> 0% of each run, Pallas kernels for 28% -> 25%
where the time goes in v4:
time: 181 us; the launch traced here: 180 us
  Pallas kernels  114 us (63%)
  starting transfers between devices  33.4 us (18%)
  blocking collectives  21.9 us (12%)
  waiting for transfers between devices  9.92 us (5%)
    pallas_call x14, Pallas kernels, run(): pl.pallas_call(kernel, grid=grid, in_specs=[spec for _, spec in args], ou...  114 us
    all_to_all x5, starting transfers between devices, exchange(): return lax.all_to_all(x, 'dom', split_axis=0, concat_axis=0, tiled=True)  28.8 us
    all_to_all x2, blocking collectives, exchange(): return lax.all_to_all(x, 'dom', split_axis=0, concat_axis=0, tiled=True)  21.9 us
    ppermute x12, waiting for transfers between devices, swap(): return lax.ppermute(x, 'rep', [(i, i ^ k) for i in range(reps)])  6.49 us
    ppermute x12, starting transfers between devices, swap(): return lax.ppermute(x, 'rep', [(i, i ^ k) for i in range(reps)])  4.58 us
  transfers between devices with their start and end apart: 17, of which 8 were waited for; matrix products, arithmetic and copies ran while one was open for 0% of the time, Pallas kernels for 25%

profile of v4, /device:TPU:0, one launch (start us, length us, event | category | flops | bytes accessed | tf_op | source)
XLA Modules:
  0.0 180.3 jit_solution(10342322263893053368)
XLA Ops:
  0.7 4.4 %pack.1 = (bf16[8,32,128]{2,1,0:T(8,128)(2,1)}, bf16[64,1024]{1,0:T(8,128)(2,1)S(1)}, s32[256,1]{1,0:T(8,128)S(1)}) custom-call(bf16[100,4096]{1,0:T(8,128)(2,1)} %bitcast.60, s32[8,32]{1,0:T(8,128)} %bitcast.63, s32[1,3]{1,0:T(1,128)} %bitcast.64, s32[32,128]{1,0:T(8,128)} %bitcast.48, f32[64,100]{1,0:T(8,128)} %bitcast.44, f32[64,256]{1,0:T(8,128)} %bitcast.42, ...), custom_call_target="tpu_custom_call" | custom-call | flops 268435456 | bytes 1048576 | tf_op jit(solution)/shard_map/pack/pallas_call | solution.py:48
  5.0 2.4 %collective-permute-start.2 = (bf16[64,1024]{1,0:T(8,128)(2,1)S(1)}, bf16[64,1024]{1,0:T(8,128)(2,1)S(1)}, u32[]{:S(2)}, u32[]{:S(2)}) collective-permute-start(bf16[64,1024]{1,0:T(8,128)(2,1)S(1)} %get-tuple-element.83.pack), channel_id=1, source_target_pairs={{0,3},{1,2},{2,1},{3,0},{4,7},{5,6},{6,5},{7,4},{8,11},{9,10},{10,... | collective-permute-start | bytes 393224 | tf_op jit(solution)/shard_map/ppermute | solution.py:910
  8.1 6.0 %all-to-all-start = ((bf16[8,32,128]{2,1,0:T(8,128)(2,1)}), bf16[8,32,128]{2,1,0:T(8,128)(2,1)S(1)}, u32[]{:S(2)}, u32[]{:S(2)}) async-start(bf16[8,32,128]{2,1,0:T(8,128)(2,1)} %get-tuple-element.82), calls=%async_computation | async-start | bytes 131072 | tf_op jit(solution)/shard_map/all_to_all | solution.py:913
  14.3 5.0 %table.1 = (bf16[256,1024]{1,0:T(8,128)(2,1)}, f32[256,128]{1,0:T(8,128)S(1)}, bf16[368,4096]{1,0:T(8,128)(2,1)}) custom-call(s32[2]{0:T(128)S(1)} %pad_add_fusion.place, bf16[64,1024]{1,0:T(8,128)(2,1)S(1)} %get-tuple-element.83.pack, bf16[64,1024]{1,0:T(8,128)(2,1)S(1)} %collective-permute-done.pack_one, ...), custom_call_target="tpu_custom_call" | custom-call | flops 209715200 | bytes 1048576 | tf_op jit(solution)/shard_map/table/pallas_call | solution.py:48
  19.3 1.8 all-to-all-done.rows
  21.1 29.2 %layer_one.1 = (bf16[8,32,256]{2,1,0:T(8,128)(2,1)}, f32[8,256]{1,0:T(8,128)}, bf16[2048,4352]{1,0:T(8,128)(2,1)}, f8e4m3fn[2048,4352]{1,0:T(32,128)(4,1)}, bf16...) custom-call(s32[2]{0:T(128)S(1)} %pad_add_fusion.place, ...), custom_call_target="tpu_custom_call" | custom-call | flops 9126805504 | bytes 1048576 | tf_op jit(solution)/shard_map/layer_one/pallas_call | solution.py:48
  50.3 4.9 %all-to-all-start.1 = ((bf16[8,32,256]{2,1,0:T(8,128)(2,1)}), bf16[8,32,256]{2,1,0:T(8,128)(2,1)S(1)}, u32[]{:S(2)}, u32[]{:S(2)}) async-start(bf16[8,32,256]{2,1,0:T(8,128)(2,1)} %get-tuple-element.93), calls=%async_computation.1 | async-start | bytes 262144 | tf_op jit(solution)/shard_map/all_to_all | solution.py:913
  55.2 12.2 %layer_two_own.1.total = f32[256,2048]{1,0:T(8,128)} custom-call(s32[2]{0:T(128)S(1)} %pad_add_fusion.place, bf16[2048,4352]{1,0:T(8,128)(2,1)} %get-tuple-element.91.high, f8e4m3fn[2048,4352]{1,0:T(32,128)(4,1)} %get-tuple-element.92.rest, bf16[256,2048]{1,0:T(8,128)(2,1)} %get-tuple-element.94.z_own, bf16[256,2048]{1,0:T(8,128)(2,1)S(1)} %collective-permute-done.3.z_oth), custom_call_target="tpu_custom_call" | custom-call | flops 4563402752 | bytes 1048576 | tf_op jit(solution)/shard_map/layer_two_own/pallas_call | solution.py:48
  68.8 6.4 %layer_two_end.1 = (bf16[256,2048]{1,0:T(8,128)(2,1)}, f32[256,2048]{1,0:T(8,128)}, bf16[48,2048]{1,0:T(8,128)(2,1)}, bf16[8,32,128]{2,1,0:T(8,128)(2,1)}) custom-call(s32[2]{0:T(128)S(1)} %pad_add_fusion.place, f32[8,256]{1,0:T(8,128)} %get-tuple-element.90.flags_t, bf16[256,1024]{1,0:T(8,128)(2,1)} %get-tuple-element.88.packs_hbm.packs, ...), custom_call_target="tpu_custom_call" | custom-call | flops 1140850688 | bytes 1048576 | tf_op jit(solution)/shard_map/layer_two_end/pallas_call | solution.py:48
  75.4 6.0 %all-to-all-start.2 = ((bf16[8,32,128]{2,1,0:T(8,128)(2,1)}), bf16[8,32,128]{2,1,0:T(8,128)(2,1)S(1)}, u32[]{:S(2)}, u32[]{:S(2)}) async-start(bf16[8,32,128]{2,1,0:T(8,128)(2,1)} %get-tuple-element.97), calls=%async_computation.2 | async-start | bytes 131072 | tf_op jit(solution)/shard_map/all_to_all | solution.py:913
  81.5 11.5 %layer_three_own.1.total_hbm = f32[48,2048]{1,0:T(8,128)} custom-call(s32[2]{0:T(128)S(1)} %pad_add_fusion.place, bf16[2048,4352]{1,0:T(8,128)(2,1)} %get-tuple-element.91.high, f8e4m3fn[2048,4352]{1,0:T(32,128)(4,1)} %get-tuple-element.92.rest, bf16[48,2048]{1,0:T(8,128)(2,1)} %get-tuple-element.98.z_own, bf16[48,2048]{1,0:T(8,128)(2,1)S(1)} %collective-permute-done.5.z_oth), custom_call_target="tpu_custom_call" | custom-call | flops 4563402752 | bytes 1048576 | tf_op jit(solution)/shard_map/layer_three_own/pallas_call | solution.py:48
  93.2 1.2 collective-permute-done.6.came_oth
  94.4 8.4 %loss.1 = (f32[64,128]{1,0:T(8,128)S(1)}, f32[8,128]{1,0:T(8,128)S(1)}, f32[8,32,128]{2,1,0:T(8,128)}, bf16[96,2048]{1,0:T(8,128)(2,1)}, f8e4m3fn[48,2048]{1,0:T(8,128)(4,1)}, /*index=5*/f32[48,2048]{1,0:T(8,128)}) custom-call(s32[2]{0:T(128)S(1)} %pad_add_fusion.place, f32[8,256]{1,0:T(8,128)S(1)} %copy-done.2, ...), custom_call_target="tpu_custom_call" | custom-call | flops 4563402752 | bytes 1048576 | tf_op jit(solution)/shard_map/loss/pallas_call | solution.py:48
  103.0 6.0 %all-to-all-start.3 = ((f32[8,32,128]{2,1,0:T(8,128)}), f32[8,32,128]{2,1,0:T(8,128)S(1)}, u32[]{:S(2)}, u32[]{:S(2)}) async-start(f32[8,32,128]{2,1,0:T(8,128)} %get-tuple-element.101), calls=%async_computation.3 | async-start | bytes 262144 | tf_op jit(solution)/shard_map/all_to_all | solution.py:913
  109.0 7.5 %back_three.1.near_hbm = f32[48,2048]{1,0:T(8,128)} custom-call(s32[2]{0:T(128)S(1)} %pad_add_fusion.place, bf16[2048,4352]{1,0:T(8,128)(2,1)} %get-tuple-element.91.high, f8e4m3fn[2048,4352]{1,0:T(32,128)(4,1)} %get-tuple-element.92.rest, bf16[96,2048]{1,0:T(8,128)(2,1)} %get-tuple-element.103.grads, f8e4m3fn[48,2048]{1,0:T(8,128)(4,1)} %get-tuple-element.104.grads8, ...), custom_call_target="tpu_custom_call" | custom-call | flops 2281701376 | bytes 1048576 | tf_op jit(solution)/shard_map/back_three/pallas_call | solution.py:48
  116.7 1.3 collective-permute-done.8.ret_oth
  118.0 12.5 %end_three.1 = (f32[256,128]{1,0:T(8,128)S(1)}, f32[8,128]{1,0:T(8,128)S(1)}, f32[8,40,256]{2,1,0:T(8,128)}, bf16[256,2048]{1,0:T(8,128)(2,1)}, f8e4m3fn[256,204...) custom-call(s32[2]{0:T(128)S(1)} %pad_add_fusion.place, f32[8,256]{1,0:T(8,128)S(1)} %copy-done.2, ...), custom_call_target="tpu_custom_call" | custom-call | flops 4563402752 | bytes 1048576 | tf_op jit(solution)/shard_map/end_three/pallas_call | solution.py:48
  130.7 6.0 %all-to-all-start.4 = ((f32[8,40,256]{2,1,0:T(8,128)}), f32[8,40,256]{2,1,0:T(8,128)S(1)}, u32[]{:S(2)}, u32[]{:S(2)}) async-start(f32[8,40,256]{2,1,0:T(8,128)} %get-tuple-element.111), calls=%async_computation.4 | async-start | bytes 655360 | tf_op jit(solution)/shard_map/all_to_all | solution.py:913
  136.7 9.1 %back.1.near_hbm = f32[256,2048]{1,0:T(8,128)} custom-call(s32[2]{0:T(128)S(1)} %pad_add_fusion.place, f32[8,128]{1,0:T(8,128)S(1)} %get-tuple-element.113.back, bf16[256,2048]{1,0:T(8,128)(2,1)} %get-tuple-element.114.grads_hbm, f8e4m3fn[256,2048]{1,0:T(32,128)(4,1)} %get-tuple-element.115.grads8_hbm, f8e4m3fn[256,2048]{1,0:T(32,128)(4,1)} %get-tuple-element.116.tails8_hbm, ...), custom_call_target="tpu_custom_call" | custom-call | flops 2281701376 | bytes 1048576 | tf_op jit(solution)/shard_map/back/pallas_call | solution.py:48
  145.8 1.7 all-to-all-done.4.ret
  147.5 1.6 collective-permute-done.10.ret_oth
  149.2 6.6 %end_two.1 = (f32[192,128]{1,0:T(8,128)S(1)}, f32[192,128]{1,0:T(8,128)S(1)}, f32[8,256]{1,0:T(8,128)S(1)}) custom-call(s32[2]{0:T(128)S(1)} %pad_add_fusion.place, f32[8,40,256]{2,1,0:T(8,128)S(1)} %all-to-all-done.4.ret, f32[8,40,256]{2,1,0:T(8,128)S(1)} %collective-permute-done.10.ret_oth, bf16[256,1024]{1,0:T(8,128)(2,1)} %get-tuple-element.88.packs_hbm.packs, ...), custom_call_target="tpu_custom_call" | custom-call | flops 1140850688 | bytes 1048576 | tf_op jit(solution)/shard_map/end_two/pallas_call | solution.py:48
  157.2 12.0 %all_to_all.35.came = f32[8,40,128]{2,1,0:T(8,128)S(1)} all-to-all(f32[8,40,128]{2,1,0:T(8,128)S(1)} %scatter.1), channel_id=1, replica_groups=mesh['dom'=8,'rep'=4] {'dom'}, dimensions={0} | all-to-all | bytes 327680 | tf_op jit(solution)/shard_map/all_to_all | solution.py:913
  169.3 9.9 %all_to_all.36.came = f32[8,24,128]{2,1,0:T(8,128)S(1)} all-to-all(f32[8,24,128]{2,1,0:T(8,128)S(1)} %get-tuple-element.128), channel_id=1, replica_groups=mesh['dom'=8,'rep'=4] {'dom'}, dimensions={0} | all-to-all | bytes 196608 | tf_op jit(solution)/shard_map/all_to_all | solution.py:913
  (65 shorter events, 5.7 us)
Async XLA Ops:
  5.0 9.2 %collective-permute-start.2 = (bf16[64,1024]{1,0:T(8,128)(2,1)S(1)}, bf16[64,1024]{1,0:T(8,128)(2,1)S(1)}, u32[]{:S(2)}, u32[]{:S(2)}) collective-permute-start(bf16[64,1024]{1,0:T(8,128)(2,1)S(1)} %get-tuple-element.83.pack), channel_id=1, source_target_pairs={{0,3},{1,2},{2,1},{3,0},{4,7},{5,6},{6,5},{7,4},{8,11},{9,10},{10,... | collective-permute-start | bytes 393224 | tf_op jit(solution)/shard_map/ppermute | solution.py:910
  7.4 6.9 %collective-permute-start.1 = (bf16[64,1024]{1,0:T(8,128)(2,1)S(1)}, bf16[64,1024]{1,0:T(8,128)(2,1)S(1)}, u32[]{:S(2)}, u32[]{:S(2)}) collective-permute-start(bf16[64,1024]{1,0:T(8,128)(2,1)S(1)} %get-tuple-element.83.pack), channel_id=1, source_target_pairs={{0,2},{1,3},{2,0},{3,1},{4,6},{5,7},{6,4},{7,5},{8,10},{9,11},{10,... | collective-permute-start | bytes 393224 | tf_op jit(solution)/shard_map/ppermute | solution.py:910
  8.0 6.3 %collective-permute-start = (bf16[64,1024]{1,0:T(8,128)(2,1)S(1)}, bf16[64,1024]{1,0:T(8,128)(2,1)S(1)}, u32[]{:S(2)}, u32[]{:S(2)}) collective-permute-start(bf16[64,1024]{1,0:T(8,128)(2,1)S(1)} %get-tuple-element.83.pack), channel_id=1, source_target_pairs={{0,1},{1,0},{2,3},{3,2},{4,5},{5,4},{6,7},{7,6},{8,9},{9,8},{10,11... | collective-permute-start | bytes 393224 | tf_op jit(solution)/shard_map/ppermute | solution.py:910
  8.1 12.9 %all-to-all-start = ((bf16[8,32,128]{2,1,0:T(8,128)(2,1)}), bf16[8,32,128]{2,1,0:T(8,128)(2,1)S(1)}, u32[]{:S(2)}, u32[]{:S(2)}) async-start(bf16[8,32,128]{2,1,0:T(8,128)(2,1)} %get-tuple-element.82), calls=%async_computation | async-start | bytes 131072 | tf_op jit(solution)/shard_map/all_to_all | solution.py:913
  50.2 4.9 %collective-permute-start.3 = (bf16[256,2048]{1,0:T(8,128)(2,1)}, bf16[256,2048]{1,0:T(8,128)(2,1)S(1)}, u32[]{:S(2)}, u32[]{:S(2)}) collective-permute-start(bf16[256,2048]{1,0:T(8,128)(2,1)} %get-tuple-element.94.z_own), channel_id=1, source_target_pairs={{0,1},{1,0},{2,3},{3,2},{4,5},{5,4},{6,7},{7,6},{8,9},{9,8},{10,11... | collective-permute-start | bytes 3145736 | tf_op jit(solution)/shard_map/ppermute | solution.py:910
  50.3 17.1 %all-to-all-start.1 = ((bf16[8,32,256]{2,1,0:T(8,128)(2,1)}), bf16[8,32,256]{2,1,0:T(8,128)(2,1)S(1)}, u32[]{:S(2)}, u32[]{:S(2)}) async-start(bf16[8,32,256]{2,1,0:T(8,128)(2,1)} %get-tuple-element.93), calls=%async_computation.1 | async-start | bytes 262144 | tf_op jit(solution)/shard_map/all_to_all | solution.py:913
  67.4 1.4 collective-permute-start.4
  75.2 6.3 %collective-permute-start.5 = (bf16[48,2048]{1,0:T(8,128)(2,1)}, bf16[48,2048]{1,0:T(8,128)(2,1)S(1)}, u32[]{:S(2)}, u32[]{:S(2)}) collective-permute-start(bf16[48,2048]{1,0:T(8,128)(2,1)} %get-tuple-element.98.z_own), channel_id=1, source_target_pairs={{0,1},{1,0},{2,3},{3,2},{4,5},{5,4},{6,7},{7,6},{8,9},{9,8},{10,11... | collective-permute-start | bytes 589832 | tf_op jit(solution)/shard_map/ppermute | solution.py:910
  75.4 17.6 %all-to-all-start.2 = ((bf16[8,32,128]{2,1,0:T(8,128)(2,1)}), bf16[8,32,128]{2,1,0:T(8,128)(2,1)S(1)}, u32[]{:S(2)}, u32[]{:S(2)}) async-start(bf16[8,32,128]{2,1,0:T(8,128)(2,1)} %get-tuple-element.97), calls=%async_computation.2 | async-start | bytes 131072 | tf_op jit(solution)/shard_map/all_to_all | solution.py:913
  93.0 1.3 collective-permute-start.6
  102.8 13.8 %collective-permute-start.7 = (f32[48,2048]{1,0:T(8,128)}, f32[48,2048]{1,0:T(8,128)S(1)}, u32[]{:S(2)}, u32[]{:S(2)}) collective-permute-start(f32[48,2048]{1,0:T(8,128)} %get-tuple-element.102), channel_id=1, source_target_pairs={{0,1},{1,0},{2,3},{3,2},{4,5},{5,4},{6,7},{7,6},{8,9},{9,8},{10,11... | collective-permute-start | bytes 1179656 | tf_op jit(solution)/shard_map/ppermute | solution.py:910
  103.0 13.5 %all-to-all-start.3 = ((f32[8,32,128]{2,1,0:T(8,128)}), f32[8,32,128]{2,1,0:T(8,128)S(1)}, u32[]{:S(2)}, u32[]{:S(2)}) async-start(f32[8,32,128]{2,1,0:T(8,128)} %get-tuple-element.101), calls=%async_computation.3 | async-start | bytes 262144 | tf_op jit(solution)/shard_map/all_to_all | solution.py:913
  116.6 1.4 collective-permute-start.8
  130.5 17.0 %collective-permute-start.9 = (f32[256,2048]{1,0:T(8,128)}, f32[256,2048]{1,0:T(8,128)}, u32[]{:S(2)}, u32[]{:S(2)}) collective-permute-start(f32[256,2048]{1,0:T(8,128)} %get-tuple-element.112), channel_id=1, source_target_pairs={{0,1},{1,0},{2,3},{3,2},{4,5},{5,4},{6,7},{7,6},{8,9},{9,8},{10,11... | collective-permute-start | bytes 6291464 | tf_op jit(solution)/shard_map/ppermute | solution.py:910
  130.7 16.8 %all-to-all-start.4 = ((f32[8,40,256]{2,1,0:T(8,128)}), f32[8,40,256]{2,1,0:T(8,128)S(1)}, u32[]{:S(2)}, u32[]{:S(2)}) async-start(f32[8,40,256]{2,1,0:T(8,128)} %get-tuple-element.111), calls=%async_computation.4 | async-start | bytes 655360 | tf_op jit(solution)/shard_map/all_to_all | solution.py:913
  147.5 1.6 collective-permute-start.10
  149.1 30.0 %copy-start.4 = (f32[256,64]{0,1:T(8,128)S(1)}, f32[256,64]{0,1:T(8,128)}, u32[]{:S(2)}) copy-start(f32[256,64]{0,1:T(8,128)} %param.39) | copy-start | bytes 196612
  149.1 30.0 %copy-start.5 = (f32[256,64]{0,1:T(8,128)S(1)}, f32[256,64]{0,1:T(8,128)}, u32[]{:S(2)}) copy-start(f32[256,64]{0,1:T(8,128)} %param.44) | copy-start | bytes 196612
  149.1 30.0 %copy-start.7 = (f32[256,47]{0,1:T(8,128)S(1)}, f32[256,47]{0,1:T(8,128)}, u32[]{:S(2)}) copy-start(f32[256,47]{0,1:T(8,128)} %param.40) | copy-start | bytes 144388
  149.1 30.0 %copy-start.8 = (f32[256,47]{0,1:T(8,128)S(1)}, f32[256,47]{0,1:T(8,128)}, u32[]{:S(2)}) copy-start(f32[256,47]{0,1:T(8,128)} %param.45) | copy-start | bytes 144388
  149.1 30.0 %copy-start.9 = (f32[100,64]{0,1:T(8,128)S(1)}, f32[100,64]{0,1:T(8,128)}, u32[]{:S(2)}) copy-start(f32[100,64]{0,1:T(8,128)} %param.38) | copy-start | bytes 76804
  149.2 30.0 %copy-start.10 = (f32[100,64]{0,1:T(8,128)S(1)}, f32[100,64]{0,1:T(8,128)}, u32[]{:S(2)}) copy-start(f32[100,64]{0,1:T(8,128)} %param.43) | copy-start | bytes 76804
  149.2 30.0 %copy-start.13 = (f32[2,64]{1,0:T(2,128)S(1)}, f32[2,64]{1,0:T(2,128)}, u32[]{:S(2)}) copy-start(f32[2,64]{1,0:T(2,128)} %refs_9_.1) | copy-start | bytes 1540
  155.9 1.4 collective-permute-start.11
  (12 other events, 253.8 us)

commit v5 on v4

--- a/solution.py
+++ b/solution.py
@@ -22,6 +22,7 @@
 FINE = 256
 AHEAD = 3
 LIMIT = 52 << 20
+LOW_LIMIT = 34 << 20
 RESIDENT_BYTES = 30 << 20
 FEAT_SCALE = 32.0
 
@@ -40,7 +41,7 @@
     return [(a, spec) for a in arrays]
 
 
-def run(kernel, name, args, outs, scratch=(), flops=0, grid=()):
+def run(kernel, name, args, outs, scratch=(), flops=0, grid=(), limit=LIMIT):
     pinned = [
         a if any(spec is s for s in (SMEM, VMEM, ANY)) else pltpu.with_memory_space_constraint(a, pltpu.HBM)
         for a, spec in args
@@ -57,7 +58,7 @@
         scratch_shapes=list(scratch),
         name=name,
         cost_estimate=pl.CostEstimate(flops=flops, bytes_accessed=1 << 20, transcendentals=0),
-        compiler_params=pltpu.CompilerParams(vmem_limit_bytes=LIMIT),
+        compiler_params=pltpu.CompilerParams(vmem_limit_bytes=limit),
     )(*pinned)
 
 
@@ -277,7 +278,7 @@
     return u * half, slope
 
 
-def layer_one_kernel(place, src_t, norm_t, rows, send, most, packs_hbm, table_hbm, z_send, flags_t, high_hbm, rest_hbm, hidden_hbm, slope_hbm, z_hbm, near_hbm, packs, table, table8, high, rest, hidden_t, slope_t, z_own, near_feat, in_sems, edge_sems, out_sems):
+def layer_one_kernel(place, src_t, norm_t, rows, send, most, packs_hbm, table_hbm, z_send, later, flags_t, high_hbm, rest_hbm, hidden_hbm, slope_hbm, z_hbm, near_hbm, packs, table, table8, high, rest, hidden_t, slope_t, z_own, near_feat, in_sems, edge_sems, out_sems):
     slots = src_t.shape[0]
     units, half = hidden_t.shape
     nodes = 2 * half
@@ -357,7 +358,6 @@
     count = 64.0 * counts[:, FLAG_LANE + 3 : FLAG_LANE + 4] + counts[:, FLAG_LANE + 4 : FLAG_LANE + 5]
     row = lax.broadcasted_iota(I32, flags.shape, 0)
     flags_t[...] = jnp.where(row == 3, count, flags)
-    z_send[...] = jnp.zeros(z_send.shape, BF16)
     loop(FINE // 128, build)
     edge_stores.start(0)
     fetch.wait(0)
@@ -404,8 +404,6 @@
         z = dot_nn(packs[:, 128 : 128 + units], value).astype(BF16)
         z_own[:, here] = z
         stores.start(i)
-        chosen = dot_nt(pick_rows(send[...], place[0] * half + i * FINE, FINE), z)
-        z_send[...] = (z_send[...].astype(F32) + chosen.reshape(z_send.shape)).astype(BF16)
 
     def step(i, carry):
         if depth < steps:
@@ -426,6 +424,29 @@
     keep(steps - 1, sums(steps - 1))
     finish(steps - 2)
     finish(steps - 1)
+
+    bound = z_send.shape[1]
+    group = 256 // bound
+
+    def send_some(c):
+        chosen = pick_rows(send[span(c * 256, 256), :], place[0] * half, half)
+        to = pl.ds(c * group, group)
+
+        def put(ref, first, rows):
+            value = dot_nt(chosen, rows).astype(BF16)
+            ref[to, :, first : first + value.shape[1]] = value.reshape(group, bound, value.shape[1])
+
+        slope = slope_t[...]
+        top = slope.astype(BF16)
+        put(z_send, 0, z_own[...])
+        put(z_send, units, hidden_t[...])
+        put(z_send, 2 * units, top)
+        put(later, 0, (slope - top.astype(F32)).astype(BF16))
+        later[to, :, units:] = jnp.zeros((group, bound, 256), BF16)
+        put(later, units, near_feat[0:extra, :])
+        put(later, units + 128, near_feat[extra:, :])
+
+    loop(halo // 256, send_some)
     stores.wait_all(steps)
     for i in range(steps - depth, steps):
         edge_stores.wait(i)
@@ -473,7 +494,7 @@
     return lambda i: (span(i * ROWS, ROWS), slice(nodes, nodes + halo))
 
 
-def layer_two_end_kernel(place, flags_t, packs, send, high, rest, total, came, came_oth, last_t, hidden_t, slope_t, z_own, z_send, border, border8, back):
+def layer_two_end_kernel(place, flags_t, packs, send, high, rest, total, came, came_oth, later, last_t, hidden_t, slope_t, z_own, z_send, border, border8, back):
     halo = send.shape[0]
     width = hidden_t.shape[0]
     kinds = z_own.shape[0]
@@ -482,13 +503,15 @@
 
     @pl.when(step == 0)
     def _():
-        both = came[...].reshape(halo, width).astype(F32) + came_oth[...].reshape(halo, width).astype(F32)
+        flat = lambda ref: ref[:, :, 0:width].reshape(halo, width).astype(F32)
+        both = flat(came) + flat(came_oth)
         value = jnp.where(flags_t[1:2, :] == 1.0, both.T, stale_columns(packs, 1, halo))
         scale, inverse = scale_of(value)
         border[...] = value.astype(BF16)
         border8[...] = (value * scale).astype(F8)
         back[0] = inverse * (1.0 / REST_GAIN)
-        z_send[...] = jnp.zeros(z_send.shape, BF16)
+        z_send[:, :, 0:128] = jnp.zeros((*z_send.shape[0:2], 128), BF16)
+        z_send[:, :, 128:] = later[...]
 
     sums = total[...] + dot_nt(border[...], high[...]) + dot_nt(border8[...], rest[...]) * back[0]
     value, slope = gelu_both(sums + bias_column(packs, 1))
@@ -499,7 +522,8 @@
     z_own[...] = z
     chosen = dot_nt(pick_rows(send[...], place[0] * half + step * ROWS, ROWS), z)
     chosen = jnp.concatenate([chosen, jnp.zeros((halo, 128 - kinds), F32)], axis=1)
-    z_send[...] = (z_send[...].astype(F32) + chosen.reshape(z_send.shape)).astype(BF16)
+    sent = z_send[:, :, 0:128]
+    z_send[:, :, 0:128] = (sent.astype(F32) + chosen.reshape(sent.shape)).astype(BF16)
 
 
 def put_border(border_grad, total, keep):
@@ -527,7 +551,8 @@
     far_stores = Stream(far_sems, (far, all_of, far_hbm, all_of))
     blocks.start_first(steps)
     edges.start(0)
-    both = came[...].reshape(halo, 128).astype(F32) + came_oth[...].reshape(halo, 128).astype(F32)
+    flat = lambda ref: ref[:, :, 0:128].reshape(halo, 128).astype(F32)
+    both = flat(came) + flat(came_oth)
     old = jnp.concatenate([stale_t[...].astype(F32), jnp.zeros((kinds - classes, halo), F32)], axis=0)
     value = jnp.where(flags_t[2:3, :] == 1.0, both.T[0:kinds, :], old)
     scale, back = scale_of(value)
@@ -625,36 +650,21 @@
     return total + dot_nn(tails8, top.astype(F8)) * back_tail
 
 
-def back_kernel(place, back, grads_hbm, grads8_hbm, tails8_hbm, high, rest, out_hbm, out, grads, grads8, tails8, hbuf, rbuf, in_sems, edge_sems, out_sems):
+def back_kernel(place, back, grads, grads8, tails8, high, rest, out, hbuf, rbuf, edge_sems):
     half = out.shape[1]
     steps = half // ROWS
     mine = cols_at(ROWS, place[0] * half)
-    fetch = Stream(
-        in_sems,
-        *[(a, all_of, b, all_of) for a, b in ((grads_hbm, grads), (grads8_hbm, grads8), (tails8_hbm, tails8))],
-    )
     edges = Stream(edge_sems, (high, mine, hbuf, cols_at(ROWS)), (rest, mine, rbuf, cols_at(ROWS)))
-    stores = Stream(out_sems, (out, cols_at(ROWS), out_hbm, cols_at(ROWS)))
-    fetch.start(0)
-    edges.start(0)
-    fetch.wait(0)
-    for i in range(1, min(AHEAD, steps)):
-        edges.start(i)
+    edges.start_first(steps)
 
     def step(i):
-        edges.wait(i)
+        edges.next(i, steps)
         here = span(i * ROWS, ROWS)
         out[:, here] = back_block(
             grads[...], grads8[...], tails8[...], back[0:1, 0:1], back[0:1, 1:2], hbuf[:, here], rbuf[:, here]
         )
-        stores.start(i)
-
-        @pl.when(i + AHEAD < steps)
-        def _():
-            edges.start(i + AHEAD)
 
     loop(steps, step)
-    stores.wait_all(steps)
 
 
 def returned_terms(ret, ret_oth, bound, kinds):
@@ -672,7 +682,7 @@
     return total.astype(BF16)
 
 
-def end_three_kernel(place, flags_t, ret, ret_oth, last_t, send, far_in_any, near_hbm, hidden_hbm, slope_hbm, high, rest, sums, back_out, border_grad, grads_hbm, grads8_hbm, tails8_hbm, far_hbm, near, far_in, hidden_t, slope_t, hrows, rrows, grad_rows, grad_last, border_sum, grads, grads8, tails8, far, hbuf, rbuf, in_sems, row_sems, out_sems, edge_sems, far_sems):
+def end_three_kernel(place, flags_t, ret, ret_oth, last_t, send, far_in_any, near_hbm, hidden_hbm, slope_hbm, high, rest, sums, back_out, border_sum, grad_last, grads, grads8, tails8, far, near, far_in, hidden_t, slope_t, hrows, rrows, grad_rows, hbuf, rbuf, in_sems, row_sems, edge_sems):
     kinds, half = near.shape
     units = slope_t.shape[0]
     parts = ret.shape[0]
@@ -688,16 +698,8 @@
         ],
     )
     borders = Stream(row_sems, (high, cut, hrows, rows_at(ROWS)), (rest, cut, rrows, rows_at(ROWS)))
-    stores = Stream(
-        out_sems,
-        *[
-            (a, cols_at(ROWS), b, cols_at(ROWS))
-            for a, b in ((grads, grads_hbm), (grads8, grads8_hbm), (tails8, tails8_hbm))
-        ],
-    )
     others = cols_at(ROWS, (1 - place[0]) * half)
     edges = Stream(edge_sems, (high, others, hbuf, cols_at(ROWS)), (rest, others, rbuf, cols_at(ROWS)))
-    far_stores = Stream(far_sems, (far, cols_at(ROWS), far_hbm, cols_at(ROWS)))
     for stream in (blocks, borders, edges):
         loop(steps, stream.start)
     terms = returned_terms(ret, ret_oth, bound, kinds)
@@ -733,12 +735,10 @@
         grads[:, here] = top
         grads8[:, here] = small
         tails8[:, here] = tail
-        stores.start(i)
         border_sum[...] += back_block(top, small, tail, back_rest, back_tail, hrows[here, :], rrows[here, :])
 
     loop(steps, second_step)
-    put_border(border_grad, border_sum[...], flags_t[1:2, :])
-    border_grad[:, bound:, :] = grad_last[...].reshape(parts, 64 // parts, units)
+    border_sum[...] = border_sum[...] * flags_t[1:2, :]
 
     def far_step(i):
         edges.wait(i)
@@ -746,52 +746,54 @@
         far[:, here] = back_block(
             grads[...], grads8[...], tails8[...], back_rest, back_tail, hbuf[:, here], rbuf[:, here]
         )
-        far_stores.start(i)
 
     loop(steps, far_step)
-    far_stores.wait_all(steps)
-    stores.wait_all(steps)
-
-
-def end_two_kernel(place, ret, ret_oth, packs, send, sums_two, sums_out, far_any, near_hbm, hidden_hbm, slope_hbm, feat_hbm, out, out_one, last_chunk, near, far, hidden_t, slope_t, near_feat, grad_first, grad_second, sums_one, in_sems):
+
+
+def end_two_kernel(place, border, border_oth, packs, sums_two, sums_out, near, far, came_hbm, late_hbm, hidden_hbm, slope_hbm, feat_hbm, out, out_one, came, came_late, hidden_t, slope_t, near_feat, grad_first, grad_second, sums_one, came_sems, in_sems):
     units, half = near.shape
-    parts = ret.shape[0]
-    bound = send.shape[0] // parts
+    halo = border.shape[1]
     steps = half // ROWS
     extra = near_feat.shape[0] // 2
+    every = lambda i: (slice(None), slice(None), slice(None))
+    fetch = Stream(came_sems, (came_hbm, every, came, every), (late_hbm, every, came_late, every))
     blocks = Stream(
         in_sems,
         *[
             (a, cols_at(ROWS), b, cols_at(ROWS))
-            for a, b in (
-                (near_hbm, near),
-                (far_any, far),
-                (hidden_hbm, hidden_t),
-                (slope_hbm, slope_t),
-                (feat_hbm, near_feat),
-            )
+            for a, b in ((hidden_hbm, hidden_t), (slope_hbm, slope_t), (feat_hbm, near_feat))
         ],
     )
     loop(steps, blocks.start)
-    terms = returned_terms(ret, ret_oth, bound, units)
-    last_chunk[...] = jnp.sum(ret[:, bound:, :] + ret_oth[:, bound:, :], axis=0)
+    fetch.start(0)
     weight = packs[:, 128 : 128 + units]
     for ref in (grad_first, grad_second, sums_one):
         ref[...] = jnp.zeros(ref.shape, F32)
 
+    def through(d_z, slope):
+        grad = dot_tn(weight, d_z) * slope
+        sums_one[...] += lane_sums(grad)
+        top = grad.astype(BF16)
+        return top, (grad - top.astype(F32)).astype(BF16)
+
     def step(i):
         blocks.wait(i)
         here = span(i * ROWS, ROWS)
-        d_z = round_gradient(near[:, here], far[:, here], terms, send[...], (place[0] * steps + i) * ROWS)
+        d_z = (near[:, here] + far[:, here]).astype(BF16)
         grad_second[...] += dot_nt(d_z, hidden_t[:, here])
-        grad = dot_tn(weight, d_z) * slope_t[:, here]
-        sums_one[...] += lane_sums(grad)
-        top = grad.astype(BF16)
-        tail = (grad - top.astype(F32)).astype(BF16)
+        top, tail = through(d_z, slope_t[:, here])
         high, low = near_feat[0:extra, here], near_feat[extra:, here]
         grad_first[:, 0:extra] += dot_nt(top, high) + (dot_nt(tail, high) + dot_nt(top, low))
 
     loop(steps, step)
+    fetch.wait(0)
+    lanes = lambda ref, first, size: ref[:, :, first : first + size].reshape(halo, size)
+    d_z = (border[...] + border_oth[...]).astype(BF16)
+    grad_second[...] += dot_nn(d_z, lanes(came, units, units))
+    slope = lanes(came, 2 * units, units).astype(F32) + lanes(came_late, 128, units).astype(F32)
+    top, tail = through(d_z, slope.T)
+    high, low = lanes(came_late, 128 + units, 128), lanes(came_late, 256 + units, 128)
+    grad_first[...] += dot_nn(top, high) + (dot_nn(tail, high) + dot_nn(top, low))
     lane = lax.broadcasted_iota(I32, (64, 128), 1)
     column = lambda value: jnp.sum(value, axis=1, keepdims=True)
     for k, ref in enumerate((out, out_one)):
@@ -804,26 +806,25 @@
         ref[128:192, :] = grad_second[rows, 128:256]
 
 
-def scatter_kernel(mine, came, last_chunk, out):
+def scatter_kernel(mine, came, last, last_came, out):
     total = mine[...] + came[...]
-    parts, size = out.shape[0], last_chunk.shape[0]
+    last_total = last[...] + last_came[...]
+    parts = out.shape[0]
+    size = 64 // parts
     for q in range(parts):
         pieces = [total[64 * k + q * size : 64 * k + (q + 1) * size, :] for k in range(3)]
-        pieces += [last_chunk[:, 0:128], last_chunk[:, 128:256]]
-        out[q] = jnp.concatenate(pieces, axis=0)
+        chunk = last_total[q * size : (q + 1) * size, :]
+        out[q] = jnp.concatenate(pieces + [chunk[:, 0:128], chunk[:, 128:256]], axis=0)
 
 
 def joined(came, first, size):
     return came[:, first : first + size, :].reshape(64, 128)
 
 
-def gather_kernel(came, out, grad_last):
-    parts = came.shape[0]
-    size = 64 // parts
-    value = jnp.sum(came[:, 0 : 3 * size, :], axis=0)
-    for p in range(parts):
+def gather_kernel(came, out):
+    value = jnp.sum(came[...], axis=0)
+    for p in range(came.shape[0]):
         out[p] = value
-    grad_last[...] = jnp.concatenate([joined(came, 3 * size, size), joined(came, 4 * size, size)], axis=1)
 
 
 def adamw(weight, moment, square, gradient):
@@ -837,7 +838,7 @@
     return (weight, moment, square)
 
 
-def update_kernel(came, grad_last, flags_t, *refs):
+def update_kernel(came, flags_t, *refs):
     params, outs = refs[0:15], refs[15:]
     parts = came.shape[0]
     size = 64 // parts
@@ -848,7 +849,7 @@
     gradients = (
         total[:, 0:width],
         jnp.concatenate(halves, axis=1),
-        grad_last[0:kinds, :],
+        jnp.concatenate([joined(came, 3 * size, size), joined(came, 4 * size, size)], axis=1)[0:kinds, :],
         turned[FLAG_LANE : FLAG_LANE + 2, 0:64],
         turned[FLAG_LANE + 2 : FLAG_LANE + 3, 0:kinds],
     )
@@ -959,12 +960,13 @@
     )
     rows, most = late(most, rows)
     held = fine if half * table * 3 <= RESIDENT_BYTES else min(fine, 4)
-    z_send, flags_t, high, rest, hidden_one, slope_one, z_own, near_feat = run(
+    z_send, later, flags_t, high, rest, hidden_one, slope_one, z_own, near_feat = run(
         layer_one_kernel,
         "layer_one",
         [where, *placed(OWN, edge_src.T, edge_norm.T), *placed(VMEM, rows, send, most), *placed(HBM, packs, first_table)],
         [
-            ((parts, bound, units), BF16, VMEM),
+            ((parts, bound, 3 * units), BF16, VMEM),
+            ((parts, bound, units + 256), BF16, OWN),
             ((8, halo), F32, OWN),
             ((half, table), BF16, HBM),
             ((half, table), F8, HBM),
@@ -1007,6 +1009,7 @@
     came = exchange(z_send)
     total = own_part(z_own, z_oth, "layer_two_own")
     came, total = late(total, came)
+    came_one = came
     came_oth = swap(came)
     border_block = lambda array: (array, pl.BlockSpec((ROWS, halo), lambda i: (i, nodes // halo)))
     hidden_two, slope_two, z_own, z_send = run(
@@ -1014,12 +1017,12 @@
         "layer_two_end",
         [where, whole(flags_t), whole(packs), (send, VMEM), border_block(high), border_block(rest), (total, block)]
         + placed(VMEM, came, came_oth)
-        + [whole(last_t)],
+        + [whole(later), whole(last_t)],
         [
             ((units, half), BF16, block),
             ((units, half), F32, block),
             ((kinds, half), BF16, node_block(ROWS, kinds)),
-            ((parts, bound, 128), BF16, whole_spec((parts, bound, 128))),
+            ((parts, bound, 128 + units + 256), BF16, whole_spec((parts, bound, 128 + units + 256))),
         ],
         [vm((units, halo), BF16), vm((units, halo), F8), scalar],
         flops=work // 4,
@@ -1029,6 +1032,7 @@
     came = exchange(z_send)
     total = own_part(z_own, z_oth, "layer_three_own")
     came, total = late(total, came)
+    came_two = came
     came_oth = swap(came)
     border_rows = [vm((half, halo), BF16), vm((half, halo), F8)]
     sums_out, back, border_grad, grads, grads8, far = run(
@@ -1077,9 +1081,7 @@
     )[0]
     ret, far, near = late(near, ret, far)
     ret_oth = swap(ret)
-    chunk = 64 // parts
-
-    sums_two, back, border_grad, grads, grads8, tails8, far = run(
+    sums_two, back, border, last, grads, grads8, tails8, far = run(
         end_three_kernel,
         "end_three",
         [where, *placed(VMEM, flags_t, ret, ret_oth, last_t, send), (far, ANY)]
@@ -1087,11 +1089,12 @@
         [
             ((units, 128), F32, VMEM),
             ((8, 128), F32, VMEM),
-            ((parts, bound + chunk, units), F32, VMEM),
-            ((units, half), BF16, HBM),
-            ((units, half), F8, HBM),
-            ((units, half), F8, HBM),
-            ((units, half), F32, HBM),
+            ((units, halo), F32, VMEM),
+            ((64, units), F32, VMEM),
+            ((units, half), BF16, VMEM),
+            ((units, half), F8, VMEM),
+            ((units, half), F8, VMEM),
+            ((units, half), F32, VMEM),
         ],
         [
             vm((kinds, half), F32),
@@ -1100,75 +1103,58 @@
             vm((units, half), F32),
             *border_rows,
             vm((units, half), F32),
-            vm((64, units), F32),
-            vm((units, halo), F32),
-            vm((units, half), BF16),
-            vm((units, half), F8),
-            vm((units, half), F8),
-            vm((units, half), F32),
             vm((half, half), BF16),
             vm((half, half), F8),
             sems(4, steps),
             sems(2, steps),
-            sems(3, steps),
             sems(2, steps),
-            sems(1, steps),
         ],
         flops=work,
-    )
-    far = swap(far)
-    ret = exchange(border_grad)
+        limit=LOW_LIMIT,
+    )
+    far, border_oth, last_oth = swap(far), swap(border), swap(last)
     near = run(
         back_kernel,
         "back",
-        [where, (back, VMEM), *placed(HBM, grads, grads8, tails8), *edge],
-        [((units, half), F32, HBM)],
-        [
-            vm((units, half), F32),
-            vm((units, half), BF16),
-            vm((units, half), F8),
-            vm((units, half), F8),
-            vm((half, half), BF16),
-            vm((half, half), F8),
-            sems(3, 1),
-            sems(2, steps),
-            sems(1, steps),
-        ],
+        [where, *placed(VMEM, back, grads, grads8, tails8), *edge],
+        [((units, half), F32, VMEM)],
+        [vm((half, half), BF16), vm((half, half), F8), sems(2, steps)],
         flops=work // 2,
+        limit=LOW_LIMIT,
     )[0]
-    ret, far, near = late(near, ret, far)
-    ret_oth = swap(ret)
-    mine, theirs, last_chunk = run(
+    mine, theirs = run(
         end_two_kernel,
         "end_two",
-        [where, *placed(VMEM, ret, ret_oth), (packs, OWN), *placed(VMEM, send, sums_two, sums_out), (far, ANY)]
-        + placed(HBM, near, hidden_one, slope_one, near_feat),
-        [((192, 128), F32, VMEM)] * 2 + [((chunk, units), F32, VMEM)],
+        [where, *placed(VMEM, border, border_oth), (packs, OWN), *placed(VMEM, sums_two, sums_out, near, far)]
+        + [*placed(HBM, came_one, came_two, hidden_one, slope_one, near_feat)],
+        [((192, 128), F32, VMEM)] * 2,
         [
-            vm((units, half), F32),
-            vm((units, half), F32),
+            vm(came_one.shape, BF16),
+            vm(came_two.shape, BF16),
             vm((units, half), BF16),
             vm((units, half), F32),
             vm((2 * extra, half), BF16),
             vm((units, 128), F32),
             vm((units, units), F32),
             vm((units, 128), F32),
-            sems(5, steps),
+            sems(2, 1),
+            sems(3, steps),
         ],
         flops=work // 4,
+        limit=LOW_LIMIT,
     )
     scattered = run(
         scatter_kernel,
         "scatter",
-        placed(VMEM, mine, swap(theirs), last_chunk),
-        [((parts, 5 * chunk, 128), F32, VMEM)],
+        placed(VMEM, mine, swap(theirs), last, last_oth),
+        [((parts, 5 * 64 // parts, 128), F32, VMEM)],
     )[0]
-    gathered, grad_last = run(
+    gathered = run(
         gather_kernel,
         "gather",
         placed(VMEM, exchange(scattered)),
-        [((parts, 3 * chunk, 128), F32, VMEM), ((64, units), F32, VMEM)],
-    )
+        [(scattered.shape, F32, VMEM)],
+    )[0]
     came = exchange(gathered)
 
     turn = lambda x: x.T
@@ -1182,7 +1168,7 @@
     outs = run(
         update_kernel,
         "update",
-        placed(VMEM, came, grad_last, flags_t, *params),
+        placed(VMEM, came, flags_t, *params),
         [(p.shape, F32, VMEM) for p in params] + [((1, 128), F32, VMEM)] * 2,
     )
     undo = (turn, turn, turn, same, lambda x: x.reshape(-1))

time: 181 us -> 172 us (0.950)
  starting transfers between devices: 33.4 us -> 28 us
  Pallas kernels: 114 us -> 110 us
  waiting for transfers between devices: 9.92 us -> 7.35 us
  blocking collectives: 21.9 us -> 24.1 us
    all_to_all x5 -> x4, starting transfers between devices: 28.8 us -> 22.8 us  [exchange(): return lax.all_to_all(x, 'dom', split_axis=0, concat_axis=0, tiled=True)]
    pallas_call x14, Pallas kernels: 114 us -> 110 us  [run(): pl.pallas_call(kernel, grid=grid, in_specs=[spec for _, spec in args], ou...]
    all_to_all x2, blocking collectives: 21.9 us -> 24.1 us  [exchange(): return lax.all_to_all(x, 'dom', split_axis=0, concat_axis=0, tiled=True)]
    ppermute x12 -> x13, waiting for transfers between devices: 6.49 us -> 5.42 us  [swap(): return lax.ppermute(x, 'rep', [(i, i ^ k) for i in range(reps)])]
    ppermute x12 -> x13, starting transfers between devices: 4.58 us -> 5.11 us  [swap(): return lax.ppermute(x, 'rep', [(i, i ^ k) for i in range(reps)])]
  transfers between devices with their start and end apart: 17 -> 17, of which waited for: 8 -> 7; matrix products, arithmetic and copies ran while one was open for 0% -> 0% of each run, Pallas kernels for 25% -> 26%
where the time goes in v5:
time: 172 us; the launch traced here: 171 us
  Pallas kernels  110 us (64%)
  starting transfers between devices  28 us (16%)
  blocking collectives  24.1 us (14%)
  waiting for transfers between devices  7.35 us (4%)
    pallas_call x14, Pallas kernels, run(): pl.pallas_call(kernel, grid=grid, in_specs=[spec for _, spec in args], ou...  110 us
    all_to_all x2, blocking collectives, exchange(): return lax.all_to_all(x, 'dom', split_axis=0, concat_axis=0, tiled=True)  24.1 us
    all_to_all x4, starting transfers between devices, exchange(): return lax.all_to_all(x, 'dom', split_axis=0, concat_axis=0, tiled=True)  22.8 us
    ppermute x13, waiting for transfers between devices, swap(): return lax.ppermute(x, 'rep', [(i, i ^ k) for i in range(reps)])  5.42 us
    ppermute x13, starting transfers between devices, swap(): return lax.ppermute(x, 'rep', [(i, i ^ k) for i in range(reps)])  5.11 us
  transfers between devices with their start and end apart: 17, of which 7 were waited for; matrix products, arithmetic and copies ran while one was open for 0% of the time, Pallas kernels for 26%

profile of v5, /device:TPU:0, one launch (start us, length us, event | category | flops | bytes accessed | tf_op | source)
XLA Modules:
  0.0 170.7 jit_solution(11973196634906628729)
XLA Ops:
  0.7 4.4 %pack.1 = (bf16[8,32,128]{2,1,0:T(8,128)(2,1)}, bf16[64,1024]{1,0:T(8,128)(2,1)S(1)}, s32[256,1]{1,0:T(8,128)S(1)}) custom-call(bf16[100,4096]{1,0:T(8,128)(2,1)} %bitcast.60, s32[8,32]{1,0:T(8,128)} %bitcast.63, s32[1,3]{1,0:T(1,128)} %bitcast.64, s32[32,128]{1,0:T(8,128)} %bitcast.48, f32[64,100]{1,0:T(8,128)} %bitcast.44, f32[64,256]{1,0:T(8,128)} %bitcast.42, ...), custom_call_target="tpu_custom_call" | custom-call | flops 268435456 | bytes 1048576 | tf_op jit(solution)/shard_map/pack/pallas_call | solution.py:49
  5.0 2.4 %collective-permute-start.2 = (bf16[64,1024]{1,0:T(8,128)(2,1)S(1)}, bf16[64,1024]{1,0:T(8,128)(2,1)S(1)}, u32[]{:S(2)}, u32[]{:S(2)}) collective-permute-start(bf16[64,1024]{1,0:T(8,128)(2,1)S(1)} %get-tuple-element.79.pack), channel_id=1, source_target_pairs={{0,3},{1,2},{2,1},{3,0},{4,7},{5,6},{6,5},{7,4},{8,11},{9,10},{10,... | collective-permute-start | bytes 393224 | tf_op jit(solution)/shard_map/ppermute | solution.py:911
  8.1 6.0 %all-to-all-start = ((bf16[8,32,128]{2,1,0:T(8,128)(2,1)}), bf16[8,32,128]{2,1,0:T(8,128)(2,1)S(1)}, u32[]{:S(2)}, u32[]{:S(2)}) async-start(bf16[8,32,128]{2,1,0:T(8,128)(2,1)} %get-tuple-element.78), calls=%async_computation | async-start | bytes 131072 | tf_op jit(solution)/shard_map/all_to_all | solution.py:914
  14.3 5.0 %table.1 = (bf16[256,1024]{1,0:T(8,128)(2,1)}, f32[256,128]{1,0:T(8,128)S(1)}, bf16[368,4096]{1,0:T(8,128)(2,1)}) custom-call(s32[2]{0:T(128)S(1)} %pad_add_fusion.place, bf16[64,1024]{1,0:T(8,128)(2,1)S(1)} %get-tuple-element.79.pack, bf16[64,1024]{1,0:T(8,128)(2,1)S(1)} %collective-permute-done.pack_one, ...), custom_call_target="tpu_custom_call" | custom-call | flops 209715200 | bytes 1048576 | tf_op jit(solution)/shard_map/table/pallas_call | solution.py:49
  19.3 1.8 %all-to-all-done.rows = bf16[8,32,128]{2,1,0:T(8,128)(2,1)S(1)} async-done(((bf16[8,32,128]{2,1,0:T(8,128)(2,1)}), bf16[8,32,128]{2,1,0:T(8,128)(2,1)S(1)}, u32[]{:S(2)}, u32[]{:S(2)}) %all-to-all-start) | async-done | bytes 65568 | tf_op jit(solution)/shard_map/all_to_all | solution.py:914
  21.1 29.6 %layer_one.1 = (bf16[8,32,768]{2,1,0:T(8,128)(2,1)}, bf16[8,32,512]{2,1,0:T(8,128)(2,1)}, f32[8,256]{1,0:T(8,128)}, bf16[2048,4352]{1,0:T(8,128)(2,1)}, f8e4m3fn...) custom-call(s32[2]{0:T(128)S(1)} %pad_add_fusion.place, ...), custom_call_target="tpu_custom_call" | custom-call | flops 9126805504 | bytes 1048576 | tf_op jit(solution)/shard_map/layer_one/pallas_call | solution.py:49
  50.8 4.9 %all-to-all-start.1 = ((bf16[8,32,768]{2,1,0:T(8,128)(2,1)}), bf16[8,32,768]{2,1,0:T(8,128)(2,1)S(1)}, u32[]{:S(2)}, u32[]{:S(2)}) async-start(bf16[8,32,768]{2,1,0:T(8,128)(2,1)} %get-tuple-element.89), calls=%async_computation.1 | async-start | bytes 786432 | tf_op jit(solution)/shard_map/all_to_all | solution.py:914
  55.7 12.2 %layer_two_own.1.total = f32[256,2048]{1,0:T(8,128)} custom-call(s32[2]{0:T(128)S(1)} %pad_add_fusion.place, bf16[2048,4352]{1,0:T(8,128)(2,1)} %get-tuple-element.87.high, f8e4m3fn[2048,4352]{1,0:T(32,128)(4,1)} %get-tuple-element.88.rest, bf16[256,2048]{1,0:T(8,128)(2,1)} %get-tuple-element.90.z_own, bf16[256,2048]{1,0:T(8,128)(2,1)S(1)} %collective-permute-done.3.z_oth), custom_call_target="tpu_custom_call" | custom-call | flops 4563402752 | bytes 1048576 | tf_op jit(solution)/shard_map/layer_two_own/pallas_call | solution.py:49
  68.1 1.6 collective-permute-done.4.came_oth
  69.7 6.6 %layer_two_end.1 = (bf16[256,2048]{1,0:T(8,128)(2,1)}, f32[256,2048]{1,0:T(8,128)}, bf16[48,2048]{1,0:T(8,128)(2,1)}, bf16[8,32,640]{2,1,0:T(8,128)(2,1)}) custom-call(s32[2]{0:T(128)S(1)} %pad_add_fusion.place, f32[8,256]{1,0:T(8,128)} %get-tuple-element.86.flags_t, bf16[256,1024]{1,0:T(8,128)(2,1)} %get-tuple-element.84.packs_hbm.packs, ...), custom_call_target="tpu_custom_call" | custom-call | flops 1140850688 | bytes 1048576 | tf_op jit(solution)/shard_map/layer_two_end/pallas_call | solution.py:49
  76.5 5.9 %all-to-all-start.2 = ((bf16[8,32,640]{2,1,0:T(8,128)(2,1)}), bf16[8,32,640]{2,1,0:T(8,128)(2,1)S(1)}, u32[]{:S(2)}, u32[]{:S(2)}) async-start(bf16[8,32,640]{2,1,0:T(8,128)(2,1)} %get-tuple-element.94), calls=%async_computation.2 | async-start | bytes 655360 | tf_op jit(solution)/shard_map/all_to_all | solution.py:914
  82.5 11.6 %layer_three_own.1.total_hbm = f32[48,2048]{1,0:T(8,128)} custom-call(s32[2]{0:T(128)S(1)} %pad_add_fusion.place, bf16[2048,4352]{1,0:T(8,128)(2,1)} %get-tuple-element.87.high, f8e4m3fn[2048,4352]{1,0:T(32,128)(4,1)} %get-tuple-element.88.rest, bf16[48,2048]{1,0:T(8,128)(2,1)} %get-tuple-element.95.z_own, bf16[48,2048]{1,0:T(8,128)(2,1)S(1)} %collective-permute-done.5.z_oth), custom_call_target="tpu_custom_call" | custom-call | flops 4563402752 | bytes 1048576 | tf_op jit(solution)/shard_map/layer_three_own/pallas_call | solution.py:49
  94.2 1.5 collective-permute-done.6.came_oth
  95.8 8.4 %loss.1 = (f32[64,128]{1,0:T(8,128)S(1)}, f32[8,128]{1,0:T(8,128)S(1)}, f32[8,32,128]{2,1,0:T(8,128)}, bf16[96,2048]{1,0:T(8,128)(2,1)}, f8e4m3fn[48,2048]{1,0:T(8,128)(4,1)}, /*index=5*/f32[48,2048]{1,0:T(8,128)}) custom-call(s32[2]{0:T(128)S(1)} %pad_add_fusion.place, f32[8,256]{1,0:T(8,128)S(1)} %copy-done.4, ...), custom_call_target="tpu_custom_call" | custom-call | flops 4563402752 | bytes 1048576 | tf_op jit(solution)/shard_map/loss/pallas_call | solution.py:49
  104.4 6.0 %all-to-all-start.3 = ((f32[8,32,128]{2,1,0:T(8,128)}), f32[8,32,128]{2,1,0:T(8,128)S(1)}, u32[]{:S(2)}, u32[]{:S(2)}) async-start(f32[8,32,128]{2,1,0:T(8,128)} %get-tuple-element.98), calls=%async_computation.3 | async-start | bytes 262144 | tf_op jit(solution)/shard_map/all_to_all | solution.py:914
  110.4 7.6 %back_three.1.near_hbm = f32[48,2048]{1,0:T(8,128)} custom-call(s32[2]{0:T(128)S(1)} %pad_add_fusion.place, bf16[2048,4352]{1,0:T(8,128)(2,1)} %get-tuple-element.87.high, f8e4m3fn[2048,4352]{1,0:T(32,128)(4,1)} %get-tuple-element.88.rest, bf16[96,2048]{1,0:T(8,128)(2,1)} %get-tuple-element.100.grads, f8e4m3fn[48,2048]{1,0:T(8,128)(4,1)} %get-tuple-element.101.grads8, ...), custom_call_target="tpu_custom_call" | custom-call | flops 2281701376 | bytes 1048576 | tf_op jit(solution)/shard_map/back_three/pallas_call | solution.py:49
  118.1 1.3 collective-permute-done.8.ret_oth
  119.4 10.7 %end_three.1 = (f32[256,128]{1,0:T(8,128)S(1)}, f32[8,128]{1,0:T(8,128)S(1)}, f32[256,256]{1,0:T(8,128)S(1)}, f32[64,256]{1,0:T(8,128)S(1)}, bf16[256,2048]{1,0:...) custom-call(s32[2]{0:T(128)S(1)} %pad_add_fusion.place, ...), custom_call_target="tpu_custom_call" | custom-call | flops 4563402752 | bytes 1048576 | tf_op jit(solution)/shard_map/end_three/pallas_call | solution.py:49
  130.7 7.7 %back.1.near = f32[256,2048]{1,0:T(8,128)S(1)} custom-call(s32[2]{0:T(128)S(1)} %pad_add_fusion.place, f32[8,128]{1,0:T(8,128)S(1)} %get-tuple-element.111.back, bf16[256,2048]{1,0:T(8,128)(2,1)S(1)} %get-tuple-element.112.grads, f8e4m3fn[256,2048]{1,0:T(32,128)(4,1)S(1)} %get-tuple-element.113.grads8, f8e4m3fn[256,2048]{1,0:T(32,128)(4,1)S(1)} %get-tuple-element.114.tails8, ...), custom_call_target="tpu_custom_call" | custom-call | flops 2281701376 | bytes 1048576 | tf_op jit(solution)/shard_map/back/pallas_call | solution.py:49
  138.6 5.3 %end_two.1 = (f32[192,128]{1,0:T(8,128)S(1)}, f32[192,128]{1,0:T(8,128)S(1)}) custom-call(s32[2]{0:T(128)S(1)} %pad_add_fusion.place, f32[256,256]{1,0:T(8,128)S(1)} %get-tuple-element.108.border, f32[256,256]{1,0:T(8,128)S(1)} %collective-permute-done.9.border_oth, bf16[256,1024]{1,0:T(8,128)(2,1)} %get-tuple-element.84.packs_hbm.packs, ...), custom_call_target="tpu_custom_call" | custom-call | flops 1140850688 | bytes 1048576 | tf_op jit(solution)/shard_map/end_two/pallas_call | solution.py:49
  144.5 0.9 collective-permute-done.12.last_came
  145.5 13.8 %all_to_all.30.came = f32[8,40,128]{2,1,0:T(8,128)S(1)} all-to-all(f32[8,40,128]{2,1,0:T(8,128)S(1)} %scatter.1), channel_id=1, replica_groups=mesh['dom'=8,'rep'=4] {'dom'}, dimensions={0} | all-to-all | bytes 327680 | tf_op jit(solution)/shard_map/all_to_all | solution.py:914
  159.2 10.3 %all_to_all.31.came = f32[8,40,128]{2,1,0:T(8,128)S(1)} all-to-all(f32[8,40,128]{2,1,0:T(8,128)S(1)} %gather.1), channel_id=1, replica_groups=mesh['dom'=8,'rep'=4] {'dom'}, dimensions={0} | all-to-all | bytes 327680 | tf_op jit(solution)/shard_map/all_to_all | solution.py:914
  169.7 0.9 update.1
  (69 shorter events, 3.2 us)
Async XLA Ops:
  5.0 9.2 %collective-permute-start.2 = (bf16[64,1024]{1,0:T(8,128)(2,1)S(1)}, bf16[64,1024]{1,0:T(8,128)(2,1)S(1)}, u32[]{:S(2)}, u32[]{:S(2)}) collective-permute-start(bf16[64,1024]{1,0:T(8,128)(2,1)S(1)} %get-tuple-element.79.pack), channel_id=1, source_target_pairs={{0,3},{1,2},{2,1},{3,0},{4,7},{5,6},{6,5},{7,4},{8,11},{9,10},{10,... | collective-permute-start | bytes 393224 | tf_op jit(solution)/shard_map/ppermute | solution.py:911
  7.4 6.9 %collective-permute-start.1 = (bf16[64,1024]{1,0:T(8,128)(2,1)S(1)}, bf16[64,1024]{1,0:T(8,128)(2,1)S(1)}, u32[]{:S(2)}, u32[]{:S(2)}) collective-permute-start(bf16[64,1024]{1,0:T(8,128)(2,1)S(1)} %get-tuple-element.79.pack), channel_id=1, source_target_pairs={{0,2},{1,3},{2,0},{3,1},{4,6},{5,7},{6,4},{7,5},{8,10},{9,11},{10,... | collective-permute-start | bytes 393224 | tf_op jit(solution)/shard_map/ppermute | solution.py:911
  8.0 6.3 %collective-permute-start = (bf16[64,1024]{1,0:T(8,128)(2,1)S(1)}, bf16[64,1024]{1,0:T(8,128)(2,1)S(1)}, u32[]{:S(2)}, u32[]{:S(2)}) collective-permute-start(bf16[64,1024]{1,0:T(8,128)(2,1)S(1)} %get-tuple-element.79.pack), channel_id=1, source_target_pairs={{0,1},{1,0},{2,3},{3,2},{4,5},{5,4},{6,7},{7,6},{8,9},{9,8},{10,11... | collective-permute-start | bytes 393224 | tf_op jit(solution)/shard_map/ppermute | solution.py:911
  8.1 12.9 %all-to-all-start = ((bf16[8,32,128]{2,1,0:T(8,128)(2,1)}), bf16[8,32,128]{2,1,0:T(8,128)(2,1)S(1)}, u32[]{:S(2)}, u32[]{:S(2)}) async-start(bf16[8,32,128]{2,1,0:T(8,128)(2,1)} %get-tuple-element.78), calls=%async_computation | async-start | bytes 131072 | tf_op jit(solution)/shard_map/all_to_all | solution.py:914
  50.7 5.0 %collective-permute-start.3 = (bf16[256,2048]{1,0:T(8,128)(2,1)}, bf16[256,2048]{1,0:T(8,128)(2,1)S(1)}, u32[]{:S(2)}, u32[]{:S(2)}) collective-permute-start(bf16[256,2048]{1,0:T(8,128)(2,1)} %get-tuple-element.90.z_own), channel_id=1, source_target_pairs={{0,1},{1,0},{2,3},{3,2},{4,5},{5,4},{6,7},{7,6},{8,9},{9,8},{10,11... | collective-permute-start | bytes 3145736 | tf_op jit(solution)/shard_map/ppermute | solution.py:911
  50.8 17.2 %all-to-all-start.1 = ((bf16[8,32,768]{2,1,0:T(8,128)(2,1)}), bf16[8,32,768]{2,1,0:T(8,128)(2,1)S(1)}, u32[]{:S(2)}, u32[]{:S(2)}) async-start(bf16[8,32,768]{2,1,0:T(8,128)(2,1)} %get-tuple-element.89), calls=%async_computation.1 | async-start | bytes 786432 | tf_op jit(solution)/shard_map/all_to_all | solution.py:914
  68.0 1.7 %collective-permute-start.4 = (bf16[8,32,768]{2,1,0:T(8,128)(2,1)S(1)}, bf16[8,32,768]{2,1,0:T(8,128)(2,1)S(1)}, u32[]{:S(2)}, u32[]{:S(2)}) collective-permute-start(bf16[8,32,768]{2,1,0:T(8,128)(2,1)S(1)} %all-to-all-done.1.came.came_hbm), channel_id=1, source_target_pairs={{0,1},{1,0},{2,3},{3,2},{4,5},{5,4},{6,7},{7,6},{8,9},{9,8},{10,11... | collective-permute-start | bytes 1179656 | tf_op jit(solution)/shard_map/ppermute | solution.py:911
  76.3 6.2 %collective-permute-start.5 = (bf16[48,2048]{1,0:T(8,128)(2,1)}, bf16[48,2048]{1,0:T(8,128)(2,1)S(1)}, u32[]{:S(2)}, u32[]{:S(2)}) collective-permute-start(bf16[48,2048]{1,0:T(8,128)(2,1)} %get-tuple-element.95.z_own), channel_id=1, source_target_pairs={{0,1},{1,0},{2,3},{3,2},{4,5},{5,4},{6,7},{7,6},{8,9},{9,8},{10,11... | collective-permute-start | bytes 589832 | tf_op jit(solution)/shard_map/ppermute | solution.py:911
  76.5 17.6 %all-to-all-start.2 = ((bf16[8,32,640]{2,1,0:T(8,128)(2,1)}), bf16[8,32,640]{2,1,0:T(8,128)(2,1)S(1)}, u32[]{:S(2)}, u32[]{:S(2)}) async-start(bf16[8,32,640]{2,1,0:T(8,128)(2,1)} %get-tuple-element.94), calls=%async_computation.2 | async-start | bytes 655360 | tf_op jit(solution)/shard_map/all_to_all | solution.py:914
  94.1 1.7 collective-permute-start.6
  104.2 13.8 %collective-permute-start.7 = (f32[48,2048]{1,0:T(8,128)}, f32[48,2048]{1,0:T(8,128)S(1)}, u32[]{:S(2)}, u32[]{:S(2)}) collective-permute-start(f32[48,2048]{1,0:T(8,128)} %get-tuple-element.99), channel_id=1, source_target_pairs={{0,1},{1,0},{2,3},{3,2},{4,5},{5,4},{6,7},{7,6},{8,9},{9,8},{10,11... | collective-permute-start | bytes 1179656 | tf_op jit(solution)/shard_map/ppermute | solution.py:911
  104.4 13.6 %all-to-all-start.3 = ((f32[8,32,128]{2,1,0:T(8,128)}), f32[8,32,128]{2,1,0:T(8,128)S(1)}, u32[]{:S(2)}, u32[]{:S(2)}) async-start(f32[8,32,128]{2,1,0:T(8,128)} %get-tuple-element.98), calls=%async_computation.3 | async-start | bytes 262144 | tf_op jit(solution)/shard_map/all_to_all | solution.py:914
  118.0 1.4 collective-permute-start.8
  130.2 8.3 %collective-permute-start.10 = (f32[256,2048]{1,0:T(8,128)S(1)}, f32[256,2048]{1,0:T(8,128)S(1)}, u32[]{:S(2)}, u32[]{:S(2)}) collective-permute-start(f32[256,2048]{1,0:T(8,128)S(1)} %get-tuple-element.115), channel_id=1, source_target_pairs={{0,1},{1,0},{2,3},{3,2},{4,5},{5,4},{6,7},{7,6},{8,9},{9,8},{10,11... | collective-permute-start | bytes 6291464 | tf_op jit(solution)/shard_map/ppermute | solution.py:911
  130.4 8.1 %collective-permute-start.9 = (f32[256,256]{1,0:T(8,128)S(1)}, f32[256,256]{1,0:T(8,128)S(1)}, u32[]{:S(2)}, u32[]{:S(2)}) collective-permute-start(f32[256,256]{1,0:T(8,128)S(1)} %get-tuple-element.108.border), channel_id=1, source_target_pairs={{0,1},{1,0},{2,3},{3,2},{4,5},{5,4},{6,7},{7,6},{8,9},{9,8},{10,11... | collective-permute-start | bytes 786440 | tf_op jit(solution)/shard_map/ppermute | solution.py:911
  138.4 31.1 %copy-start.3 = (f32[256,64]{0,1:T(8,128)S(1)}, f32[256,64]{0,1:T(8,128)}, u32[]{:S(2)}) copy-start(f32[256,64]{0,1:T(8,128)} %param.34) | copy-start | bytes 196612
  138.5 31.1 %copy-start.5 = (f32[100,64]{0,1:T(8,128)S(1)}, f32[100,64]{0,1:T(8,128)}, u32[]{:S(2)}) copy-start(f32[100,64]{0,1:T(8,128)} %param.33) | copy-start | bytes 76804
  138.5 31.1 %copy-start.6 = (f32[256,64]{0,1:T(8,128)S(1)}, f32[256,64]{0,1:T(8,128)}, u32[]{:S(2)}) copy-start(f32[256,64]{0,1:T(8,128)} %param.39) | copy-start | bytes 196612
  138.5 31.1 %copy-start.7 = (f32[256,64]{0,1:T(8,128)S(1)}, f32[256,64]{0,1:T(8,128)}, u32[]{:S(2)}) copy-start(f32[256,64]{0,1:T(8,128)} %param.44) | copy-start | bytes 196612
  138.5 31.1 %copy-start.9 = (f32[256,47]{0,1:T(8,128)S(1)}, f32[256,47]{0,1:T(8,128)}, u32[]{:S(2)}) copy-start(f32[256,47]{0,1:T(8,128)} %param.40) | copy-start | bytes 144388
  138.5 31.1 %copy-start.10 = (f32[256,47]{0,1:T(8,128)S(1)}, f32[256,47]{0,1:T(8,128)}, u32[]{:S(2)}) copy-start(f32[256,47]{0,1:T(8,128)} %param.45) | copy-start | bytes 144388
  138.5 31.1 %copy-start.11 = (f32[100,64]{0,1:T(8,128)S(1)}, f32[100,64]{0,1:T(8,128)}, u32[]{:S(2)}) copy-start(f32[100,64]{0,1:T(8,128)} %param.38) | copy-start | bytes 76804
  143.9 1.5 collective-permute-start.11
  144.1 1.3 collective-permute-start.12
  (14 other events, 280.5 us)

commit v6 on v5

--- a/solution.py
+++ b/solution.py
@@ -197,7 +197,9 @@
     def pick(i, total):
         return total + dot_nt(pick_rows(send[...], i * ROWS, ROWS), feat_t[:, span(i * ROWS, ROWS)])
 
-    total = lax.fori_loop(0, nodes // ROWS, pick, jnp.zeros((halo, width), F32))
+    total = jnp.zeros((halo, width), F32)
+    for i in range(nodes // ROWS):
+        total = pick(i, total)
     count = jnp.sum(mask[...].astype(F32))
     many = jnp.floor(count * (1.0 / 64.0))
     lane = lax.broadcasted_iota(I32, (halo, 128), 1)
@@ -240,10 +242,11 @@
 def table_kernel(place, pack, pack_one, pack_two, pack_three, feat_hbm, packs, most_out, table_hbm, feat_t, table, in_sems, out_sems):
     width, nodes = feat_t.shape
     units = packs.shape[0]
-    extra = jnp.zeros((table.shape[0] - units - width, ROWS), BF16)
-    steps = nodes // ROWS
-    blocks = Stream(in_sems, (feat_hbm, cols_at(ROWS), feat_t, cols_at(ROWS)))
-    stores = Stream(out_sems, (table, cols_at(ROWS), table_hbm, cols_at(ROWS)))
+    steps = 4
+    size = nodes // steps
+    extra = jnp.zeros((table.shape[0] - units - width, size), BF16)
+    blocks = Stream(in_sems, (feat_hbm, cols_at(size), feat_t, cols_at(size)))
+    stores = Stream(out_sems, (table, cols_at(size), table_hbm, cols_at(size)))
     loop(steps, blocks.start)
     for k, ref in enumerate((pack, pack_one, pack_two, pack_three)):
         packs[span(jnp.bitwise_xor(place[0] + 2 * place[1], k) * 64, 64), :] = ref[...]
@@ -251,7 +254,7 @@
 
     def step(i, most):
         blocks.wait(i)
-        here = span(i * ROWS, ROWS)
+        here = span(i * size, size)
         z = dot_nn(weight, feat_t[:, here])
         table[0:units, here] = z.astype(BF16)
         table[units:, here] = jnp.concatenate([feat_t[:, here], extra], axis=0)
@@ -499,7 +502,8 @@
     width = hidden_t.shape[0]
     kinds = z_own.shape[0]
     step = pl.program_id(0)
-    half = ROWS * pl.num_programs(0)
+    size = total.shape[1]
+    half = size * pl.num_programs(0)
 
     @pl.when(step == 0)
     def _():
@@ -520,7 +524,7 @@
     slope_t[...] = slope
     z = dot_nn(padded_rows(last_t, kinds), value).astype(BF16)
     z_own[...] = z
-    chosen = dot_nt(pick_rows(send[...], place[0] * half + step * ROWS, ROWS), z)
+    chosen = dot_nt(pick_rows(send[...], place[0] * half + step * size, size), z)
     chosen = jnp.concatenate([chosen, jnp.zeros((halo, 128 - kinds), F32)], axis=1)
     sent = z_send[:, :, 0:128]
     z_send[:, :, 0:128] = (sent.astype(F32) + chosen.reshape(sent.shape)).astype(BF16)
@@ -953,8 +957,8 @@
         [
             vm((in_width, nodes), BF16),
             vm((units + extra, nodes), BF16),
-            sems(1, nodes // ROWS),
-            sems(1, nodes // ROWS),
+            sems(1, 4),
+            sems(1, 4),
         ],
         flops=2 * units * nodes * in_width,
     )
@@ -1011,22 +1015,24 @@
     came, total = late(total, came)
     came_one = came
     came_oth = swap(came)
-    border_block = lambda array: (array, pl.BlockSpec((ROWS, halo), lambda i: (i, nodes // halo)))
+    wide = half // 2
+    wide_block = node_block(wide, units)
+    border_block = lambda array: (array, pl.BlockSpec((wide, halo), lambda i: (i, nodes // halo)))
     hidden_two, slope_two, z_own, z_send = run(
         layer_two_end_kernel,
         "layer_two_end",
-        [where, whole(flags_t), whole(packs), (send, VMEM), border_block(high), border_block(rest), (total, block)]
+        [where, whole(flags_t), whole(packs), (send, VMEM), border_block(high), border_block(rest), (total, wide_block)]
         + placed(VMEM, came, came_oth)
         + [whole(later), whole(last_t)],
         [
-            ((units, half), BF16, block),
-            ((units, half), F32, block),
-            ((kinds, half), BF16, node_block(ROWS, kinds)),
+            ((units, half), BF16, wide_block),
+            ((units, half), F32, wide_block),
+            ((kinds, half), BF16, node_block(wide, kinds)),
             ((parts, bound, 128 + units + 256), BF16, whole_spec((parts, bound, 128 + units + 256))),
         ],
         [vm((units, halo), BF16), vm((units, halo), F8), scalar],
         flops=work // 4,
-        grid=(steps,),
+        grid=(half // wide,),
     )
     z_oth = swap(z_own)
     came = exchange(z_send)
@@ -1074,10 +1080,10 @@
         back_three_kernel,
         "back_three",
         [where, *edge, whole(grads), whole(grads8), (back, VMEM)],
-        [((kinds, half), F32, node_block(FINE, kinds))],
-        ring_scratch((half, FINE)),
+        [((kinds, half), F32, node_block(ROWS, kinds))],
+        ring_scratch((half, ROWS)),
         flops=work // 2,
-        grid=(fine,),
+        grid=(steps,),
     )[0]
     ret, far, near = late(near, ret, far)
     ret_oth = swap(ret)

time: 172 us -> 168 us (0.977)
  Pallas kernels: 110 us -> 107 us
    pallas_call x14, Pallas kernels: 110 us -> 107 us  [run(): pl.pallas_call(kernel, grid=grid, in_specs=[spec for _, spec in args], ou...]
  transfers between devices with their start and end apart: 17 -> 17, of which waited for: 7 -> 8; matrix products, arithmetic and copies ran while one was open for 0% -> 0% of each run, Pallas kernels for 26% -> 26%
where the time goes in v6:
time: 168 us
  Pallas kernels  107 us (64%)
  starting transfers between devices  27.3 us (16%)
  blocking collectives  24 us (14%)
  waiting for transfers between devices  8.11 us (5%)
    pallas_call x14, Pallas kernels, run(): pl.pallas_call(kernel, grid=grid, in_specs=[spec for _, spec in args], ou...  107 us
    all_to_all x2, blocking collectives, exchange(): return lax.all_to_all(x, 'dom', split_axis=0, concat_axis=0, tiled=True)  24 us
    all_to_all x4, starting transfers between devices, exchange(): return lax.all_to_all(x, 'dom', split_axis=0, concat_axis=0, tiled=True)  22.3 us
    ppermute x13, waiting for transfers between devices, swap(): return lax.ppermute(x, 'rep', [(i, i ^ k) for i in range(reps)])  5.49 us
    ppermute x13, starting transfers between devices, swap(): return lax.ppermute(x, 'rep', [(i, i ^ k) for i in range(reps)])  4.98 us
  transfers between devices with their start and end apart: 17, of which 8 were waited for; matrix products, arithmetic and copies ran while one was open for 0% of the time, Pallas kernels for 26%

profile of v6, /device:TPU:0, one launch (start us, length us, event | category | flops | bytes accessed | tf_op | source)
XLA Modules:
  0.0 167.7 jit_solution(249489087671940799)
XLA Ops:
  0.7 2.8 %pack.1 = (bf16[8,32,128]{2,1,0:T(8,128)(2,1)}, bf16[64,1024]{1,0:T(8,128)(2,1)S(1)}, s32[256,1]{1,0:T(8,128)S(1)}) custom-call(bf16[100,4096]{1,0:T(8,128)(2,1)} %bitcast.60, s32[8,32]{1,0:T(8,128)} %bitcast.63, s32[1,3]{1,0:T(1,128)} %bitcast.64, s32[32,128]{1,0:T(8,128)} %bitcast.48, f32[64,100]{1,0:T(8,128)} %bitcast.44, f32[64,256]{1,0:T(8,128)} %bitcast.42, ...), custom_call_target="tpu_custom_call" | custom-call | flops 268435456 | bytes 1048576 | tf_op jit(solution)/shard_map/pack/pallas_call | solution.py:49
  3.5 2.4 %collective-permute-start.2 = (bf16[64,1024]{1,0:T(8,128)(2,1)S(1)}, bf16[64,1024]{1,0:T(8,128)(2,1)S(1)}, u32[]{:S(2)}, u32[]{:S(2)}) collective-permute-start(bf16[64,1024]{1,0:T(8,128)(2,1)S(1)} %get-tuple-element.79.pack), channel_id=1, source_target_pairs={{0,3},{1,2},{2,1},{3,0},{4,7},{5,6},{6,5},{7,4},{8,11},{9,10},{10,... | collective-permute-start | bytes 393224 | tf_op jit(solution)/shard_map/ppermute | solution.py:915
  6.6 6.0 %all-to-all-start = ((bf16[8,32,128]{2,1,0:T(8,128)(2,1)}), bf16[8,32,128]{2,1,0:T(8,128)(2,1)S(1)}, u32[]{:S(2)}, u32[]{:S(2)}) async-start(bf16[8,32,128]{2,1,0:T(8,128)(2,1)} %get-tuple-element.78), calls=%async_computation | async-start | bytes 131072 | tf_op jit(solution)/shard_map/all_to_all | solution.py:918
  12.7 4.4 %table.1 = (bf16[256,1024]{1,0:T(8,128)(2,1)}, f32[256,128]{1,0:T(8,128)S(1)}, bf16[368,4096]{1,0:T(8,128)(2,1)}) custom-call(s32[2]{0:T(128)S(1)} %pad_add_fusion.place, bf16[64,1024]{1,0:T(8,128)(2,1)S(1)} %get-tuple-element.79.pack, bf16[64,1024]{1,0:T(8,128)(2,1)S(1)} %collective-permute-done.pack_one, ...), custom_call_target="tpu_custom_call" | custom-call | flops 209715200 | bytes 1048576 | tf_op jit(solution)/shard_map/table/pallas_call | solution.py:49
  17.2 2.3 %all-to-all-done.rows = bf16[8,32,128]{2,1,0:T(8,128)(2,1)S(1)} async-done(((bf16[8,32,128]{2,1,0:T(8,128)(2,1)}), bf16[8,32,128]{2,1,0:T(8,128)(2,1)S(1)}, u32[]{:S(2)}, u32[]{:S(2)}) %all-to-all-start) | async-done | bytes 65568 | tf_op jit(solution)/shard_map/all_to_all | solution.py:918
  19.5 29.6 %layer_one.1 = (bf16[8,32,768]{2,1,0:T(8,128)(2,1)}, bf16[8,32,512]{2,1,0:T(8,128)(2,1)}, f32[8,256]{1,0:T(8,128)}, bf16[2048,4352]{1,0:T(8,128)(2,1)}, f8e4m3fn...) custom-call(s32[2]{0:T(128)S(1)} %pad_add_fusion.place, ...), custom_call_target="tpu_custom_call" | custom-call | flops 9126805504 | bytes 1048576 | tf_op jit(solution)/shard_map/layer_one/pallas_call | solution.py:49
  49.2 4.3 %all-to-all-start.1 = ((bf16[8,32,768]{2,1,0:T(8,128)(2,1)}), bf16[8,32,768]{2,1,0:T(8,128)(2,1)S(1)}, u32[]{:S(2)}, u32[]{:S(2)}) async-start(bf16[8,32,768]{2,1,0:T(8,128)(2,1)} %get-tuple-element.89), calls=%async_computation.1 | async-start | bytes 786432 | tf_op jit(solution)/shard_map/all_to_all | solution.py:918
  53.6 12.2 %layer_two_own.1.total = f32[256,2048]{1,0:T(8,128)} custom-call(s32[2]{0:T(128)S(1)} %pad_add_fusion.place, bf16[2048,4352]{1,0:T(8,128)(2,1)} %get-tuple-element.87.high, f8e4m3fn[2048,4352]{1,0:T(32,128)(4,1)} %get-tuple-element.88.rest, bf16[256,2048]{1,0:T(8,128)(2,1)} %get-tuple-element.90.z_own, bf16[256,2048]{1,0:T(8,128)(2,1)S(1)} %collective-permute-done.3.z_oth), custom_call_target="tpu_custom_call" | custom-call | flops 4563402752 | bytes 1048576 | tf_op jit(solution)/shard_map/layer_two_own/pallas_call | solution.py:49
  66.0 1.6 collective-permute-done.4.came_oth
  67.6 5.9 %layer_two_end.1 = (bf16[256,2048]{1,0:T(8,128)(2,1)}, f32[256,2048]{1,0:T(8,128)}, bf16[48,2048]{1,0:T(8,128)(2,1)}, bf16[8,32,640]{2,1,0:T(8,128)(2,1)}) custom-call(s32[2]{0:T(128)S(1)} %pad_add_fusion.place, f32[8,256]{1,0:T(8,128)} %get-tuple-element.86.flags_t, bf16[256,1024]{1,0:T(8,128)(2,1)} %get-tuple-element.84.packs_hbm.packs, ...), custom_call_target="tpu_custom_call" | custom-call | flops 1140850688 | bytes 1048576 | tf_op jit(solution)/shard_map/layer_two_end/pallas_call | solution.py:49
  73.7 5.9 %all-to-all-start.2 = ((bf16[8,32,640]{2,1,0:T(8,128)(2,1)}), bf16[8,32,640]{2,1,0:T(8,128)(2,1)S(1)}, u32[]{:S(2)}, u32[]{:S(2)}) async-start(bf16[8,32,640]{2,1,0:T(8,128)(2,1)} %get-tuple-element.94), calls=%async_computation.2 | async-start | bytes 655360 | tf_op jit(solution)/shard_map/all_to_all | solution.py:918
  79.7 11.6 %layer_three_own.1.total_hbm = f32[48,2048]{1,0:T(8,128)} custom-call(s32[2]{0:T(128)S(1)} %pad_add_fusion.place, bf16[2048,4352]{1,0:T(8,128)(2,1)} %get-tuple-element.87.high, f8e4m3fn[2048,4352]{1,0:T(32,128)(4,1)} %get-tuple-element.88.rest, bf16[48,2048]{1,0:T(8,128)(2,1)} %get-tuple-element.95.z_own, bf16[48,2048]{1,0:T(8,128)(2,1)S(1)} %collective-permute-done.5.z_oth), custom_call_target="tpu_custom_call" | custom-call | flops 4563402752 | bytes 1048576 | tf_op jit(solution)/shard_map/layer_three_own/pallas_call | solution.py:49
  91.4 1.5 collective-permute-done.6.came_oth
  93.0 8.4 %loss.1 = (f32[64,128]{1,0:T(8,128)S(1)}, f32[8,128]{1,0:T(8,128)S(1)}, f32[8,32,128]{2,1,0:T(8,128)}, bf16[96,2048]{1,0:T(8,128)(2,1)}, f8e4m3fn[48,2048]{1,0:T(8,128)(4,1)}, /*index=5*/f32[48,2048]{1,0:T(8,128)}) custom-call(s32[2]{0:T(128)S(1)} %pad_add_fusion.place, f32[8,256]{1,0:T(8,128)S(1)} %copy-done.4, ...), custom_call_target="tpu_custom_call" | custom-call | flops 4563402752 | bytes 1048576 | tf_op jit(solution)/shard_map/loss/pallas_call | solution.py:49
  101.6 6.0 %all-to-all-start.3 = ((f32[8,32,128]{2,1,0:T(8,128)}), f32[8,32,128]{2,1,0:T(8,128)S(1)}, u32[]{:S(2)}, u32[]{:S(2)}) async-start(f32[8,32,128]{2,1,0:T(8,128)} %get-tuple-element.98), calls=%async_computation.3 | async-start | bytes 262144 | tf_op jit(solution)/shard_map/all_to_all | solution.py:918
  107.6 7.3 %back_three.1.near_hbm = f32[48,2048]{1,0:T(8,128)} custom-call(s32[2]{0:T(128)S(1)} %pad_add_fusion.place, bf16[2048,4352]{1,0:T(8,128)(2,1)} %get-tuple-element.87.high, f8e4m3fn[2048,4352]{1,0:T(32,128)(4,1)} %get-tuple-element.88.rest, bf16[96,2048]{1,0:T(8,128)(2,1)} %get-tuple-element.100.grads, f8e4m3fn[48,2048]{1,0:T(8,128)(4,1)} %get-tuple-element.101.grads8, ...), custom_call_target="tpu_custom_call" | custom-call | flops 2281701376 | bytes 1048576 | tf_op jit(solution)/shard_map/back_three/pallas_call | solution.py:49
  115.1 1.3 collective-permute-done.8.ret_oth
  116.5 10.7 %end_three.1 = (f32[256,128]{1,0:T(8,128)S(1)}, f32[8,128]{1,0:T(8,128)S(1)}, f32[256,256]{1,0:T(8,128)S(1)}, f32[64,256]{1,0:T(8,128)S(1)}, bf16[256,2048]{1,0:...) custom-call(s32[2]{0:T(128)S(1)} %pad_add_fusion.place, ...), custom_call_target="tpu_custom_call" | custom-call | flops 4563402752 | bytes 1048576 | tf_op jit(solution)/shard_map/end_three/pallas_call | solution.py:49
  127.8 7.7 %back.1.near = f32[256,2048]{1,0:T(8,128)S(1)} custom-call(s32[2]{0:T(128)S(1)} %pad_add_fusion.place, f32[8,128]{1,0:T(8,128)S(1)} %get-tuple-element.111.back, bf16[256,2048]{1,0:T(8,128)(2,1)S(1)} %get-tuple-element.112.grads, f8e4m3fn[256,2048]{1,0:T(32,128)(4,1)S(1)} %get-tuple-element.113.grads8, f8e4m3fn[256,2048]{1,0:T(32,128)(4,1)S(1)} %get-tuple-element.114.tails8, ...), custom_call_target="tpu_custom_call" | custom-call | flops 2281701376 | bytes 1048576 | tf_op jit(solution)/shard_map/back/pallas_call | solution.py:49
  135.7 5.3 %end_two.1 = (f32[192,128]{1,0:T(8,128)S(1)}, f32[192,128]{1,0:T(8,128)S(1)}) custom-call(s32[2]{0:T(128)S(1)} %pad_add_fusion.place, f32[256,256]{1,0:T(8,128)S(1)} %get-tuple-element.108.border, f32[256,256]{1,0:T(8,128)S(1)} %collective-permute-done.9.border_oth, bf16[256,1024]{1,0:T(8,128)(2,1)} %get-tuple-element.84.packs_hbm.packs, ...), custom_call_target="tpu_custom_call" | custom-call | flops 1140850688 | bytes 1048576 | tf_op jit(solution)/shard_map/end_two/pallas_call | solution.py:49
  141.6 0.9 collective-permute-done.12.last_came
  142.5 13.7 %all_to_all.30.came = f32[8,40,128]{2,1,0:T(8,128)S(1)} all-to-all(f32[8,40,128]{2,1,0:T(8,128)S(1)} %scatter.1), channel_id=1, replica_groups=mesh['dom'=8,'rep'=4] {'dom'}, dimensions={0} | all-to-all | bytes 327680 | tf_op jit(solution)/shard_map/all_to_all | solution.py:918
  156.2 10.3 %all_to_all.31.came = f32[8,40,128]{2,1,0:T(8,128)S(1)} all-to-all(f32[8,40,128]{2,1,0:T(8,128)S(1)} %gather.1), channel_id=1, replica_groups=mesh['dom'=8,'rep'=4] {'dom'}, dimensions={0} | all-to-all | bytes 327680 | tf_op jit(solution)/shard_map/all_to_all | solution.py:918
  166.6 0.9 update.1
  (69 shorter events, 3.2 us)
Async XLA Ops:
  3.5 9.2 %collective-permute-start.2 = (bf16[64,1024]{1,0:T(8,128)(2,1)S(1)}, bf16[64,1024]{1,0:T(8,128)(2,1)S(1)}, u32[]{:S(2)}, u32[]{:S(2)}) collective-permute-start(bf16[64,1024]{1,0:T(8,128)(2,1)S(1)} %get-tuple-element.79.pack), channel_id=1, source_target_pairs={{0,3},{1,2},{2,1},{3,0},{4,7},{5,6},{6,5},{7,4},{8,11},{9,10},{10,... | collective-permute-start | bytes 393224 | tf_op jit(solution)/shard_map/ppermute | solution.py:915
  5.9 6.9 %collective-permute-start.1 = (bf16[64,1024]{1,0:T(8,128)(2,1)S(1)}, bf16[64,1024]{1,0:T(8,128)(2,1)S(1)}, u32[]{:S(2)}, u32[]{:S(2)}) collective-permute-start(bf16[64,1024]{1,0:T(8,128)(2,1)S(1)} %get-tuple-element.79.pack), channel_id=1, source_target_pairs={{0,2},{1,3},{2,0},{3,1},{4,6},{5,7},{6,4},{7,5},{8,10},{9,11},{10,... | collective-permute-start | bytes 393224 | tf_op jit(solution)/shard_map/ppermute | solution.py:915
  6.5 6.3 %collective-permute-start = (bf16[64,1024]{1,0:T(8,128)(2,1)S(1)}, bf16[64,1024]{1,0:T(8,128)(2,1)S(1)}, u32[]{:S(2)}, u32[]{:S(2)}) collective-permute-start(bf16[64,1024]{1,0:T(8,128)(2,1)S(1)} %get-tuple-element.79.pack), channel_id=1, source_target_pairs={{0,1},{1,0},{2,3},{3,2},{4,5},{5,4},{6,7},{7,6},{8,9},{9,8},{10,11... | collective-permute-start | bytes 393224 | tf_op jit(solution)/shard_map/ppermute | solution.py:915
  6.6 12.9 %all-to-all-start = ((bf16[8,32,128]{2,1,0:T(8,128)(2,1)}), bf16[8,32,128]{2,1,0:T(8,128)(2,1)S(1)}, u32[]{:S(2)}, u32[]{:S(2)}) async-start(bf16[8,32,128]{2,1,0:T(8,128)(2,1)} %get-tuple-element.78), calls=%async_computation | async-start | bytes 131072 | tf_op jit(solution)/shard_map/all_to_all | solution.py:918
  49.1 4.4 %collective-permute-start.3 = (bf16[256,2048]{1,0:T(8,128)(2,1)}, bf16[256,2048]{1,0:T(8,128)(2,1)S(1)}, u32[]{:S(2)}, u32[]{:S(2)}) collective-permute-start(bf16[256,2048]{1,0:T(8,128)(2,1)} %get-tuple-element.90.z_own), channel_id=1, source_target_pairs={{0,1},{1,0},{2,3},{3,2},{4,5},{5,4},{6,7},{7,6},{8,9},{9,8},{10,11... | collective-permute-start | bytes 3145736 | tf_op jit(solution)/shard_map/ppermute | solution.py:915
  49.2 16.6 %all-to-all-start.1 = ((bf16[8,32,768]{2,1,0:T(8,128)(2,1)}), bf16[8,32,768]{2,1,0:T(8,128)(2,1)S(1)}, u32[]{:S(2)}, u32[]{:S(2)}) async-start(bf16[8,32,768]{2,1,0:T(8,128)(2,1)} %get-tuple-element.89), calls=%async_computation.1 | async-start | bytes 786432 | tf_op jit(solution)/shard_map/all_to_all | solution.py:918
  65.9 1.7 %collective-permute-start.4 = (bf16[8,32,768]{2,1,0:T(8,128)(2,1)S(1)}, bf16[8,32,768]{2,1,0:T(8,128)(2,1)S(1)}, u32[]{:S(2)}, u32[]{:S(2)}) collective-permute-start(bf16[8,32,768]{2,1,0:T(8,128)(2,1)S(1)} %all-to-all-done.1.came.came_hbm), channel_id=1, source_target_pairs={{0,1},{1,0},{2,3},{3,2},{4,5},{5,4},{6,7},{7,6},{8,9},{9,8},{10,11... | collective-permute-start | bytes 1179656 | tf_op jit(solution)/shard_map/ppermute | solution.py:915
  73.5 6.2 %collective-permute-start.5 = (bf16[48,2048]{1,0:T(8,128)(2,1)}, bf16[48,2048]{1,0:T(8,128)(2,1)S(1)}, u32[]{:S(2)}, u32[]{:S(2)}) collective-permute-start(bf16[48,2048]{1,0:T(8,128)(2,1)} %get-tuple-element.95.z_own), channel_id=1, source_target_pairs={{0,1},{1,0},{2,3},{3,2},{4,5},{5,4},{6,7},{7,6},{8,9},{9,8},{10,11... | collective-permute-start | bytes 589832 | tf_op jit(solution)/shard_map/ppermute | solution.py:915
  73.7 17.6 %all-to-all-start.2 = ((bf16[8,32,640]{2,1,0:T(8,128)(2,1)}), bf16[8,32,640]{2,1,0:T(8,128)(2,1)S(1)}, u32[]{:S(2)}, u32[]{:S(2)}) async-start(bf16[8,32,640]{2,1,0:T(8,128)(2,1)} %get-tuple-element.94), calls=%async_computation.2 | async-start | bytes 655360 | tf_op jit(solution)/shard_map/all_to_all | solution.py:918
  91.3 1.7 %collective-permute-start.6 = (bf16[8,32,640]{2,1,0:T(8,128)(2,1)S(1)}, bf16[8,32,640]{2,1,0:T(8,128)(2,1)S(1)}, u32[]{:S(2)}, u32[]{:S(2)}) collective-permute-start(bf16[8,32,640]{2,1,0:T(8,128)(2,1)S(1)} %all-to-all-done.2.came.late_hbm), channel_id=1, source_target_pairs={{0,1},{1,0},{2,3},{3,2},{4,5},{5,4},{6,7},{7,6},{8,9},{9,8},{10,11... | collective-permute-start | bytes 983048 | tf_op jit(solution)/shard_map/ppermute | solution.py:915
  101.4 13.7 %collective-permute-start.7 = (f32[48,2048]{1,0:T(8,128)}, f32[48,2048]{1,0:T(8,128)S(1)}, u32[]{:S(2)}, u32[]{:S(2)}) collective-permute-start(f32[48,2048]{1,0:T(8,128)} %get-tuple-element.99), channel_id=1, source_target_pairs={{0,1},{1,0},{2,3},{3,2},{4,5},{5,4},{6,7},{7,6},{8,9},{9,8},{10,11... | collective-permute-start | bytes 1179656 | tf_op jit(solution)/shard_map/ppermute | solution.py:915
  101.6 13.5 %all-to-all-start.3 = ((f32[8,32,128]{2,1,0:T(8,128)}), f32[8,32,128]{2,1,0:T(8,128)S(1)}, u32[]{:S(2)}, u32[]{:S(2)}) async-start(f32[8,32,128]{2,1,0:T(8,128)} %get-tuple-element.98), calls=%async_computation.3 | async-start | bytes 262144 | tf_op jit(solution)/shard_map/all_to_all | solution.py:918
  115.1 1.3 collective-permute-start.8
  127.2 8.3 %collective-permute-start.10 = (f32[256,2048]{1,0:T(8,128)S(1)}, f32[256,2048]{1,0:T(8,128)S(1)}, u32[]{:S(2)}, u32[]{:S(2)}) collective-permute-start(f32[256,2048]{1,0:T(8,128)S(1)} %get-tuple-element.115), channel_id=1, source_target_pairs={{0,1},{1,0},{2,3},{3,2},{4,5},{5,4},{6,7},{7,6},{8,9},{9,8},{10,11... | collective-permute-start | bytes 6291464 | tf_op jit(solution)/shard_map/ppermute | solution.py:915
  127.4 8.1 %collective-permute-start.9 = (f32[256,256]{1,0:T(8,128)S(1)}, f32[256,256]{1,0:T(8,128)S(1)}, u32[]{:S(2)}, u32[]{:S(2)}) collective-permute-start(f32[256,256]{1,0:T(8,128)S(1)} %get-tuple-element.108.border), channel_id=1, source_target_pairs={{0,1},{1,0},{2,3},{3,2},{4,5},{5,4},{6,7},{7,6},{8,9},{9,8},{10,11... | collective-permute-start | bytes 786440 | tf_op jit(solution)/shard_map/ppermute | solution.py:915
  135.5 31.0 %copy-start.3 = (f32[256,64]{0,1:T(8,128)S(1)}, f32[256,64]{0,1:T(8,128)}, u32[]{:S(2)}) copy-start(f32[256,64]{0,1:T(8,128)} %param.34) | copy-start | bytes 196612
  135.5 31.0 %copy-start.5 = (f32[100,64]{0,1:T(8,128)S(1)}, f32[100,64]{0,1:T(8,128)}, u32[]{:S(2)}) copy-start(f32[100,64]{0,1:T(8,128)} %param.33) | copy-start | bytes 76804
  135.5 31.0 %copy-start.6 = (f32[256,64]{0,1:T(8,128)S(1)}, f32[256,64]{0,1:T(8,128)}, u32[]{:S(2)}) copy-start(f32[256,64]{0,1:T(8,128)} %param.39) | copy-start | bytes 196612
  135.5 31.0 %copy-start.7 = (f32[256,64]{0,1:T(8,128)S(1)}, f32[256,64]{0,1:T(8,128)}, u32[]{:S(2)}) copy-start(f32[256,64]{0,1:T(8,128)} %param.44) | copy-start | bytes 196612
  135.6 31.0 %copy-start.9 = (f32[256,47]{0,1:T(8,128)S(1)}, f32[256,47]{0,1:T(8,128)}, u32[]{:S(2)}) copy-start(f32[256,47]{0,1:T(8,128)} %param.40) | copy-start | bytes 144388
  135.6 31.0 %copy-start.10 = (f32[256,47]{0,1:T(8,128)S(1)}, f32[256,47]{0,1:T(8,128)}, u32[]{:S(2)}) copy-start(f32[256,47]{0,1:T(8,128)} %param.45) | copy-start | bytes 144388
  135.6 31.0 %copy-start.11 = (f32[100,64]{0,1:T(8,128)S(1)}, f32[100,64]{0,1:T(8,128)}, u32[]{:S(2)}) copy-start(f32[100,64]{0,1:T(8,128)} %param.38) | copy-start | bytes 76804
  141.0 1.5 collective-permute-start.11
  141.2 1.3 collective-permute-start.12
  (14 other events, 279.0 us)

commit v7 on v6

--- a/solution.py
+++ b/solution.py
@@ -24,7 +24,6 @@
 LIMIT = 52 << 20
 LOW_LIMIT = 34 << 20
 RESIDENT_BYTES = 30 << 20
-FEAT_SCALE = 32.0
 
 SMEM = pl.BlockSpec(memory_space=pltpu.SMEM)
 VMEM = pl.BlockSpec(memory_space=pltpu.VMEM)
@@ -372,23 +371,21 @@
     kept = kept & (flags[0:1, :] == 1.0)
     table[units:, nodes : nodes + halo] = jnp.where(kept, turned[0:extra, :], 0.0).astype(BF16)
     scale, back = scale_of(jnp.maximum(jnp.max(most[...]), jnp.max(jnp.abs(border))))
-    row = lax.broadcasted_iota(I32, (table.shape[0], 1), 0)
-    scale = jnp.where(row < units, scale, FEAT_SCALE)
-    back = jnp.where(row < units, back, 1.0 / FEAT_SCALE) * (1.0 / REST_GAIN)
+    back = back * (1.0 / REST_GAIN)
     bias = bias_column(packs, 0)
-    unused = jnp.zeros((table8.shape[0] - table.shape[0], 256), F32)
 
     def small(i):
         here = span(i * 256, 256)
-        value = table[:, here].astype(F32) * scale
-        table8[:, here] = jnp.concatenate([value, unused], axis=0).astype(F8)
-
-    loop((nodes + halo) // 256, small)
+        table8[:, here] = (table[0:units, here].astype(F32) * scale).astype(F8)
+
+    for i in range((nodes + halo) // 256):
+        small(i)
 
     def sums(i):
         here = slot_of(i)
-        low = dot_nt(table8[...], rest[here, :])[0 : table.shape[0]]
-        return dot_nt(table[...], high[here, :]) + low * back
+        low = dot_nt(table8[...], rest[here, :]) * back
+        top = dot_nt(table[...], high[here, :])
+        return jnp.concatenate([top[0:units] + low, top[units:]], axis=0)
 
     def keep(i, total):
         here = span(i * FINE, FINE)
@@ -465,10 +462,10 @@
     def _():
         def larger(i, most):
             here = span(i * ROWS, ROWS)
-            both = jnp.maximum(jnp.abs(z_own[:, here].astype(F32)), jnp.abs(z_oth[:, here].astype(F32)))
+            both = jnp.maximum(lane_most(z_own[:, here].astype(F32)), lane_most(z_oth[:, here].astype(F32)))
             return jnp.maximum(most, both)
 
-        most = lax.fori_loop(0, half // ROWS, larger, jnp.zeros((z_own.shape[0], ROWS), F32))
+        most = lax.fori_loop(0, half // ROWS, larger, jnp.zeros((z_own.shape[0], 128), F32))
         scale, inverse = scale_of(most)
         back[0] = inverse * (1.0 / REST_GAIN)
         for ref, first in ((z_own, place[0] * half), (z_oth, (1 - place[0]) * half)):
@@ -982,7 +979,7 @@
         [
             vm((units, pack_width), BF16),
             vm((both, table), BF16),
-            vm((-(-both // 32) * 32, table), F8),
+            vm((units, table), F8),
             vm((held * FINE, table), BF16),
             vm((held * FINE, table), F8),
             vm((units, half), BF16),

time: 168 us -> 167 us (level)
  Pallas kernels: 107 us -> 105 us
where the time goes in v7:
time: 167 us; the launch traced here: 166 us
  Pallas kernels  105 us (63%)
  starting transfers between devices  27.3 us (16%)
  blocking collectives  24 us (14%)
  waiting for transfers between devices  8.11 us (5%)
    pallas_call x14, Pallas kernels, run(): pl.pallas_call(kernel, grid=grid, in_specs=[spec for _, spec in args], ou...  105 us
    all_to_all x2, blocking collectives, exchange(): return lax.all_to_all(x, 'dom', split_axis=0, concat_axis=0, tiled=True)  24 us
    all_to_all x4, starting transfers between devices, exchange(): return lax.all_to_all(x, 'dom', split_axis=0, concat_axis=0, tiled=True)  22.3 us
    ppermute x13, waiting for transfers between devices, swap(): return lax.ppermute(x, 'rep', [(i, i ^ k) for i in range(reps)])  5.49 us
    ppermute x13, starting transfers between devices, swap(): return lax.ppermute(x, 'rep', [(i, i ^ k) for i in range(reps)])  4.98 us
  transfers between devices with their start and end apart: 17, of which 8 were waited for; matrix products, arithmetic and copies ran while one was open for 0% of the time, Pallas kernels for 26%

profile of v7, /device:TPU:0, one launch (start us, length us, event | category | flops | bytes accessed | tf_op | source)
XLA Modules:
  0.0 166.1 jit_solution(3432626254044288637)
XLA Ops:
  0.7 2.8 %pack.1 = (bf16[8,32,128]{2,1,0:T(8,128)(2,1)}, bf16[64,1024]{1,0:T(8,128)(2,1)S(1)}, s32[256,1]{1,0:T(8,128)S(1)}) custom-call(bf16[100,4096]{1,0:T(8,128)(2,1)} %bitcast.60, s32[8,32]{1,0:T(8,128)} %bitcast.63, s32[1,3]{1,0:T(1,128)} %bitcast.64, s32[32,128]{1,0:T(8,128)} %bitcast.48, f32[64,100]{1,0:T(8,128)} %bitcast.44, f32[64,256]{1,0:T(8,128)} %bitcast.42, ...), custom_call_target="tpu_custom_call" | custom-call | flops 268435456 | bytes 1048576 | tf_op jit(solution)/shard_map/pack/pallas_call | solution.py:48
  3.5 2.4 %collective-permute-start.2 = (bf16[64,1024]{1,0:T(8,128)(2,1)S(1)}, bf16[64,1024]{1,0:T(8,128)(2,1)S(1)}, u32[]{:S(2)}, u32[]{:S(2)}) collective-permute-start(bf16[64,1024]{1,0:T(8,128)(2,1)S(1)} %get-tuple-element.79.pack), channel_id=1, source_target_pairs={{0,3},{1,2},{2,1},{3,0},{4,7},{5,6},{6,5},{7,4},{8,11},{9,10},{10,... | collective-permute-start | bytes 393224 | tf_op jit(solution)/shard_map/ppermute | solution.py:912
  6.6 6.0 %all-to-all-start = ((bf16[8,32,128]{2,1,0:T(8,128)(2,1)}), bf16[8,32,128]{2,1,0:T(8,128)(2,1)S(1)}, u32[]{:S(2)}, u32[]{:S(2)}) async-start(bf16[8,32,128]{2,1,0:T(8,128)(2,1)} %get-tuple-element.78), calls=%async_computation | async-start | bytes 131072 | tf_op jit(solution)/shard_map/all_to_all | solution.py:915
  12.7 4.4 %table.1 = (bf16[256,1024]{1,0:T(8,128)(2,1)}, f32[256,128]{1,0:T(8,128)S(1)}, bf16[368,4096]{1,0:T(8,128)(2,1)}) custom-call(s32[2]{0:T(128)S(1)} %pad_add_fusion.place, bf16[64,1024]{1,0:T(8,128)(2,1)S(1)} %get-tuple-element.79.pack, bf16[64,1024]{1,0:T(8,128)(2,1)S(1)} %collective-permute-done.pack_one, ...), custom_call_target="tpu_custom_call" | custom-call | flops 209715200 | bytes 1048576 | tf_op jit(solution)/shard_map/table/pallas_call | solution.py:48
  17.2 2.3 %all-to-all-done.rows = bf16[8,32,128]{2,1,0:T(8,128)(2,1)S(1)} async-done(((bf16[8,32,128]{2,1,0:T(8,128)(2,1)}), bf16[8,32,128]{2,1,0:T(8,128)(2,1)S(1)}, u32[]{:S(2)}, u32[]{:S(2)}) %all-to-all-start) | async-done | bytes 65568 | tf_op jit(solution)/shard_map/all_to_all | solution.py:915
  19.5 28.0 %layer_one.1 = (bf16[8,32,768]{2,1,0:T(8,128)(2,1)}, bf16[8,32,512]{2,1,0:T(8,128)(2,1)}, f32[8,256]{1,0:T(8,128)}, bf16[2048,4352]{1,0:T(8,128)(2,1)}, f8e4m3fn...) custom-call(s32[2]{0:T(128)S(1)} %pad_add_fusion.place, ...), custom_call_target="tpu_custom_call" | custom-call | flops 9126805504 | bytes 1048576 | tf_op jit(solution)/shard_map/layer_one/pallas_call | solution.py:48
  47.6 4.3 %all-to-all-start.1 = ((bf16[8,32,768]{2,1,0:T(8,128)(2,1)}), bf16[8,32,768]{2,1,0:T(8,128)(2,1)S(1)}, u32[]{:S(2)}, u32[]{:S(2)}) async-start(bf16[8,32,768]{2,1,0:T(8,128)(2,1)} %get-tuple-element.89), calls=%async_computation.1 | async-start | bytes 786432 | tf_op jit(solution)/shard_map/all_to_all | solution.py:915
  51.9 12.2 %layer_two_own.1.total = f32[256,2048]{1,0:T(8,128)} custom-call(s32[2]{0:T(128)S(1)} %pad_add_fusion.place, bf16[2048,4352]{1,0:T(8,128)(2,1)} %get-tuple-element.87.high, f8e4m3fn[2048,4352]{1,0:T(32,128)(4,1)} %get-tuple-element.88.rest, bf16[256,2048]{1,0:T(8,128)(2,1)} %get-tuple-element.90.z_own, bf16[256,2048]{1,0:T(8,128)(2,1)S(1)} %collective-permute-done.3.z_oth), custom_call_target="tpu_custom_call" | custom-call | flops 4563402752 | bytes 1048576 | tf_op jit(solution)/shard_map/layer_two_own/pallas_call | solution.py:48
  64.4 1.6 collective-permute-done.4.came_oth
  66.0 5.9 %layer_two_end.1 = (bf16[256,2048]{1,0:T(8,128)(2,1)}, f32[256,2048]{1,0:T(8,128)}, bf16[48,2048]{1,0:T(8,128)(2,1)}, bf16[8,32,640]{2,1,0:T(8,128)(2,1)}) custom-call(s32[2]{0:T(128)S(1)} %pad_add_fusion.place, f32[8,256]{1,0:T(8,128)} %get-tuple-element.86.flags_t, bf16[256,1024]{1,0:T(8,128)(2,1)} %get-tuple-element.84.packs_hbm.packs, ...), custom_call_target="tpu_custom_call" | custom-call | flops 1140850688 | bytes 1048576 | tf_op jit(solution)/shard_map/layer_two_end/pallas_call | solution.py:48
  72.1 5.9 %all-to-all-start.2 = ((bf16[8,32,640]{2,1,0:T(8,128)(2,1)}), bf16[8,32,640]{2,1,0:T(8,128)(2,1)S(1)}, u32[]{:S(2)}, u32[]{:S(2)}) async-start(bf16[8,32,640]{2,1,0:T(8,128)(2,1)} %get-tuple-element.94), calls=%async_computation.2 | async-start | bytes 655360 | tf_op jit(solution)/shard_map/all_to_all | solution.py:915
  78.1 11.6 %layer_three_own.1.total_hbm = f32[48,2048]{1,0:T(8,128)} custom-call(s32[2]{0:T(128)S(1)} %pad_add_fusion.place, bf16[2048,4352]{1,0:T(8,128)(2,1)} %get-tuple-element.87.high, f8e4m3fn[2048,4352]{1,0:T(32,128)(4,1)} %get-tuple-element.88.rest, bf16[48,2048]{1,0:T(8,128)(2,1)} %get-tuple-element.95.z_own, bf16[48,2048]{1,0:T(8,128)(2,1)S(1)} %collective-permute-done.5.z_oth), custom_call_target="tpu_custom_call" | custom-call | flops 4563402752 | bytes 1048576 | tf_op jit(solution)/shard_map/layer_three_own/pallas_call | solution.py:48
  89.8 1.5 collective-permute-done.6.came_oth
  91.4 8.4 %loss.1 = (f32[64,128]{1,0:T(8,128)S(1)}, f32[8,128]{1,0:T(8,128)S(1)}, f32[8,32,128]{2,1,0:T(8,128)}, bf16[96,2048]{1,0:T(8,128)(2,1)}, f8e4m3fn[48,2048]{1,0:T(8,128)(4,1)}, /*index=5*/f32[48,2048]{1,0:T(8,128)}) custom-call(s32[2]{0:T(128)S(1)} %pad_add_fusion.place, f32[8,256]{1,0:T(8,128)S(1)} %copy-done.4, ...), custom_call_target="tpu_custom_call" | custom-call | flops 4563402752 | bytes 1048576 | tf_op jit(solution)/shard_map/loss/pallas_call | solution.py:48
  100.0 6.0 %all-to-all-start.3 = ((f32[8,32,128]{2,1,0:T(8,128)}), f32[8,32,128]{2,1,0:T(8,128)S(1)}, u32[]{:S(2)}, u32[]{:S(2)}) async-start(f32[8,32,128]{2,1,0:T(8,128)} %get-tuple-element.98), calls=%async_computation.3 | async-start | bytes 262144 | tf_op jit(solution)/shard_map/all_to_all | solution.py:915
  106.0 7.3 %back_three.1.near_hbm = f32[48,2048]{1,0:T(8,128)} custom-call(s32[2]{0:T(128)S(1)} %pad_add_fusion.place, bf16[2048,4352]{1,0:T(8,128)(2,1)} %get-tuple-element.87.high, f8e4m3fn[2048,4352]{1,0:T(32,128)(4,1)} %get-tuple-element.88.rest, bf16[96,2048]{1,0:T(8,128)(2,1)} %get-tuple-element.100.grads, f8e4m3fn[48,2048]{1,0:T(8,128)(4,1)} %get-tuple-element.101.grads8, ...), custom_call_target="tpu_custom_call" | custom-call | flops 2281701376 | bytes 1048576 | tf_op jit(solution)/shard_map/back_three/pallas_call | solution.py:48
  113.5 1.3 collective-permute-done.8.ret_oth
  114.9 10.7 %end_three.1 = (f32[256,128]{1,0:T(8,128)S(1)}, f32[8,128]{1,0:T(8,128)S(1)}, f32[256,256]{1,0:T(8,128)S(1)}, f32[64,256]{1,0:T(8,128)S(1)}, bf16[256,2048]{1,0:...) custom-call(s32[2]{0:T(128)S(1)} %pad_add_fusion.place, ...), custom_call_target="tpu_custom_call" | custom-call | flops 4563402752 | bytes 1048576 | tf_op jit(solution)/shard_map/end_three/pallas_call | solution.py:48
  126.2 7.7 %back.1.near = f32[256,2048]{1,0:T(8,128)S(1)} custom-call(s32[2]{0:T(128)S(1)} %pad_add_fusion.place, f32[8,128]{1,0:T(8,128)S(1)} %get-tuple-element.111.back, bf16[256,2048]{1,0:T(8,128)(2,1)S(1)} %get-tuple-element.112.grads, f8e4m3fn[256,2048]{1,0:T(32,128)(4,1)S(1)} %get-tuple-element.113.grads8, f8e4m3fn[256,2048]{1,0:T(32,128)(4,1)S(1)} %get-tuple-element.114.tails8, ...), custom_call_target="tpu_custom_call" | custom-call | flops 2281701376 | bytes 1048576 | tf_op jit(solution)/shard_map/back/pallas_call | solution.py:48
  134.0 5.3 %end_two.1 = (f32[192,128]{1,0:T(8,128)S(1)}, f32[192,128]{1,0:T(8,128)S(1)}) custom-call(s32[2]{0:T(128)S(1)} %pad_add_fusion.place, f32[256,256]{1,0:T(8,128)S(1)} %get-tuple-element.108.border, f32[256,256]{1,0:T(8,128)S(1)} %collective-permute-done.9.border_oth, bf16[256,1024]{1,0:T(8,128)(2,1)} %get-tuple-element.84.packs_hbm.packs, ...), custom_call_target="tpu_custom_call" | custom-call | flops 1140850688 | bytes 1048576 | tf_op jit(solution)/shard_map/end_two/pallas_call | solution.py:48
  140.0 0.9 collective-permute-done.12.last_came
  140.9 13.7 %all_to_all.30.came = f32[8,40,128]{2,1,0:T(8,128)S(1)} all-to-all(f32[8,40,128]{2,1,0:T(8,128)S(1)} %scatter.1), channel_id=1, replica_groups=mesh['dom'=8,'rep'=4] {'dom'}, dimensions={0} | all-to-all | bytes 327680 | tf_op jit(solution)/shard_map/all_to_all | solution.py:915
  154.6 10.3 %all_to_all.31.came = f32[8,40,128]{2,1,0:T(8,128)S(1)} all-to-all(f32[8,40,128]{2,1,0:T(8,128)S(1)} %gather.1), channel_id=1, replica_groups=mesh['dom'=8,'rep'=4] {'dom'}, dimensions={0} | all-to-all | bytes 327680 | tf_op jit(solution)/shard_map/all_to_all | solution.py:915
  165.0 0.9 update.1
  (69 shorter events, 3.2 us)
Async XLA Ops:
  3.5 9.2 %collective-permute-start.2 = (bf16[64,1024]{1,0:T(8,128)(2,1)S(1)}, bf16[64,1024]{1,0:T(8,128)(2,1)S(1)}, u32[]{:S(2)}, u32[]{:S(2)}) collective-permute-start(bf16[64,1024]{1,0:T(8,128)(2,1)S(1)} %get-tuple-element.79.pack), channel_id=1, source_target_pairs={{0,3},{1,2},{2,1},{3,0},{4,7},{5,6},{6,5},{7,4},{8,11},{9,10},{10,... | collective-permute-start | bytes 393224 | tf_op jit(solution)/shard_map/ppermute | solution.py:912
  5.9 6.9 %collective-permute-start.1 = (bf16[64,1024]{1,0:T(8,128)(2,1)S(1)}, bf16[64,1024]{1,0:T(8,128)(2,1)S(1)}, u32[]{:S(2)}, u32[]{:S(2)}) collective-permute-start(bf16[64,1024]{1,0:T(8,128)(2,1)S(1)} %get-tuple-element.79.pack), channel_id=1, source_target_pairs={{0,2},{1,3},{2,0},{3,1},{4,6},{5,7},{6,4},{7,5},{8,10},{9,11},{10,... | collective-permute-start | bytes 393224 | tf_op jit(solution)/shard_map/ppermute | solution.py:912
  6.5 6.3 %collective-permute-start = (bf16[64,1024]{1,0:T(8,128)(2,1)S(1)}, bf16[64,1024]{1,0:T(8,128)(2,1)S(1)}, u32[]{:S(2)}, u32[]{:S(2)}) collective-permute-start(bf16[64,1024]{1,0:T(8,128)(2,1)S(1)} %get-tuple-element.79.pack), channel_id=1, source_target_pairs={{0,1},{1,0},{2,3},{3,2},{4,5},{5,4},{6,7},{7,6},{8,9},{9,8},{10,11... | collective-permute-start | bytes 393224 | tf_op jit(solution)/shard_map/ppermute | solution.py:912
  6.6 12.9 %all-to-all-start = ((bf16[8,32,128]{2,1,0:T(8,128)(2,1)}), bf16[8,32,128]{2,1,0:T(8,128)(2,1)S(1)}, u32[]{:S(2)}, u32[]{:S(2)}) async-start(bf16[8,32,128]{2,1,0:T(8,128)(2,1)} %get-tuple-element.78), calls=%async_computation | async-start | bytes 131072 | tf_op jit(solution)/shard_map/all_to_all | solution.py:915
  47.5 4.4 %collective-permute-start.3 = (bf16[256,2048]{1,0:T(8,128)(2,1)}, bf16[256,2048]{1,0:T(8,128)(2,1)S(1)}, u32[]{:S(2)}, u32[]{:S(2)}) collective-permute-start(bf16[256,2048]{1,0:T(8,128)(2,1)} %get-tuple-element.90.z_own), channel_id=1, source_target_pairs={{0,1},{1,0},{2,3},{3,2},{4,5},{5,4},{6,7},{7,6},{8,9},{9,8},{10,11... | collective-permute-start | bytes 3145736 | tf_op jit(solution)/shard_map/ppermute | solution.py:912
  47.6 16.6 %all-to-all-start.1 = ((bf16[8,32,768]{2,1,0:T(8,128)(2,1)}), bf16[8,32,768]{2,1,0:T(8,128)(2,1)S(1)}, u32[]{:S(2)}, u32[]{:S(2)}) async-start(bf16[8,32,768]{2,1,0:T(8,128)(2,1)} %get-tuple-element.89), calls=%async_computation.1 | async-start | bytes 786432 | tf_op jit(solution)/shard_map/all_to_all | solution.py:915
  64.2 1.7 %collective-permute-start.4 = (bf16[8,32,768]{2,1,0:T(8,128)(2,1)S(1)}, bf16[8,32,768]{2,1,0:T(8,128)(2,1)S(1)}, u32[]{:S(2)}, u32[]{:S(2)}) collective-permute-start(bf16[8,32,768]{2,1,0:T(8,128)(2,1)S(1)} %all-to-all-done.1.came.came_hbm), channel_id=1, source_target_pairs={{0,1},{1,0},{2,3},{3,2},{4,5},{5,4},{6,7},{7,6},{8,9},{9,8},{10,11... | collective-permute-start | bytes 1179656 | tf_op jit(solution)/shard_map/ppermute | solution.py:912
  71.9 6.2 %collective-permute-start.5 = (bf16[48,2048]{1,0:T(8,128)(2,1)}, bf16[48,2048]{1,0:T(8,128)(2,1)S(1)}, u32[]{:S(2)}, u32[]{:S(2)}) collective-permute-start(bf16[48,2048]{1,0:T(8,128)(2,1)} %get-tuple-element.95.z_own), channel_id=1, source_target_pairs={{0,1},{1,0},{2,3},{3,2},{4,5},{5,4},{6,7},{7,6},{8,9},{9,8},{10,11... | collective-permute-start | bytes 589832 | tf_op jit(solution)/shard_map/ppermute | solution.py:912
  72.1 17.6 %all-to-all-start.2 = ((bf16[8,32,640]{2,1,0:T(8,128)(2,1)}), bf16[8,32,640]{2,1,0:T(8,128)(2,1)S(1)}, u32[]{:S(2)}, u32[]{:S(2)}) async-start(bf16[8,32,640]{2,1,0:T(8,128)(2,1)} %get-tuple-element.94), calls=%async_computation.2 | async-start | bytes 655360 | tf_op jit(solution)/shard_map/all_to_all | solution.py:915
  89.6 1.7 %collective-permute-start.6 = (bf16[8,32,640]{2,1,0:T(8,128)(2,1)S(1)}, bf16[8,32,640]{2,1,0:T(8,128)(2,1)S(1)}, u32[]{:S(2)}, u32[]{:S(2)}) collective-permute-start(bf16[8,32,640]{2,1,0:T(8,128)(2,1)S(1)} %all-to-all-done.2.came.late_hbm), channel_id=1, source_target_pairs={{0,1},{1,0},{2,3},{3,2},{4,5},{5,4},{6,7},{7,6},{8,9},{9,8},{10,11... | collective-permute-start | bytes 983048 | tf_op jit(solution)/shard_map/ppermute | solution.py:912
  99.8 13.7 %collective-permute-start.7 = (f32[48,2048]{1,0:T(8,128)}, f32[48,2048]{1,0:T(8,128)S(1)}, u32[]{:S(2)}, u32[]{:S(2)}) collective-permute-start(f32[48,2048]{1,0:T(8,128)} %get-tuple-element.99), channel_id=1, source_target_pairs={{0,1},{1,0},{2,3},{3,2},{4,5},{5,4},{6,7},{7,6},{8,9},{9,8},{10,11... | collective-permute-start | bytes 1179656 | tf_op jit(solution)/shard_map/ppermute | solution.py:912
  100.0 13.5 %all-to-all-start.3 = ((f32[8,32,128]{2,1,0:T(8,128)}), f32[8,32,128]{2,1,0:T(8,128)S(1)}, u32[]{:S(2)}, u32[]{:S(2)}) async-start(f32[8,32,128]{2,1,0:T(8,128)} %get-tuple-element.98), calls=%async_computation.3 | async-start | bytes 262144 | tf_op jit(solution)/shard_map/all_to_all | solution.py:915
  113.5 1.3 collective-permute-start.8
  125.6 8.3 %collective-permute-start.10 = (f32[256,2048]{1,0:T(8,128)S(1)}, f32[256,2048]{1,0:T(8,128)S(1)}, u32[]{:S(2)}, u32[]{:S(2)}) collective-permute-start(f32[256,2048]{1,0:T(8,128)S(1)} %get-tuple-element.115), channel_id=1, source_target_pairs={{0,1},{1,0},{2,3},{3,2},{4,5},{5,4},{6,7},{7,6},{8,9},{9,8},{10,11... | collective-permute-start | bytes 6291464 | tf_op jit(solution)/shard_map/ppermute | solution.py:912
  125.8 8.1 %collective-permute-start.9 = (f32[256,256]{1,0:T(8,128)S(1)}, f32[256,256]{1,0:T(8,128)S(1)}, u32[]{:S(2)}, u32[]{:S(2)}) collective-permute-start(f32[256,256]{1,0:T(8,128)S(1)} %get-tuple-element.108.border), channel_id=1, source_target_pairs={{0,1},{1,0},{2,3},{3,2},{4,5},{5,4},{6,7},{7,6},{8,9},{9,8},{10,11... | collective-permute-start | bytes 786440 | tf_op jit(solution)/shard_map/ppermute | solution.py:912
  133.9 31.0 %copy-start.3 = (f32[256,64]{0,1:T(8,128)S(1)}, f32[256,64]{0,1:T(8,128)}, u32[]{:S(2)}) copy-start(f32[256,64]{0,1:T(8,128)} %param.34) | copy-start | bytes 196612
  133.9 31.0 %copy-start.5 = (f32[100,64]{0,1:T(8,128)S(1)}, f32[100,64]{0,1:T(8,128)}, u32[]{:S(2)}) copy-start(f32[100,64]{0,1:T(8,128)} %param.33) | copy-start | bytes 76804
  133.9 31.0 %copy-start.6 = (f32[256,64]{0,1:T(8,128)S(1)}, f32[256,64]{0,1:T(8,128)}, u32[]{:S(2)}) copy-start(f32[256,64]{0,1:T(8,128)} %param.39) | copy-start | bytes 196612
  133.9 31.0 %copy-start.7 = (f32[256,64]{0,1:T(8,128)S(1)}, f32[256,64]{0,1:T(8,128)}, u32[]{:S(2)}) copy-start(f32[256,64]{0,1:T(8,128)} %param.44) | copy-start | bytes 196612
  133.9 31.0 %copy-start.9 = (f32[256,47]{0,1:T(8,128)S(1)}, f32[256,47]{0,1:T(8,128)}, u32[]{:S(2)}) copy-start(f32[256,47]{0,1:T(8,128)} %param.40) | copy-start | bytes 144388
  133.9 31.0 %copy-start.10 = (f32[256,47]{0,1:T(8,128)S(1)}, f32[256,47]{0,1:T(8,128)}, u32[]{:S(2)}) copy-start(f32[256,47]{0,1:T(8,128)} %param.45) | copy-start | bytes 144388
  134.0 31.0 %copy-start.11 = (f32[100,64]{0,1:T(8,128)S(1)}, f32[100,64]{0,1:T(8,128)}, u32[]{:S(2)}) copy-start(f32[100,64]{0,1:T(8,128)} %param.38) | copy-start | bytes 76804
  139.4 1.5 collective-permute-start.11
  139.6 1.3 collective-permute-start.12
  (14 other events, 279.0 us)
